TPU v7x, 32 devices: a whole 2x2x4 slice. The times are simulated.
32 devices in a mesh: shard: 2 (over core), seq: 4 (over y, x), replica: 4 (over z).
Axes of the slice: x: 2, y: 2, z: 4, core: 2. Of those that a mesh axis runs over, the one named last changes fastest.
Arguments:
- tokens: bfloat16 [16, 256, 2048], P(('shard', 'replica'), 'seq'), may hold values from -6 to 6
- cotangent: bfloat16 [16, 256, 2048], P(('shard', 'replica'), 'seq'), may hold values from -6 to 6
- lengths: int32 [16], P(('shard', 'replica')), may hold values from 64 to 256, as said below
- norm_gains: bfloat16 [2, 2048], P(None, 'shard'), may hold values from 0.5 to 1.5
- w_in: bfloat16 [2048, 12288], P('shard'), may hold values from -0.125 to 0.125
- w_ab: bfloat16 [2048, 32], P('shard'), may hold values from -0.125 to 0.125
- conv_weight: bfloat16 [4, 8192], P(None, 'shard'), may hold values from -3 to 3
- gate_params: float32 [2, 16], replicated, as said below
- onorm_gain: float32 [256], replicated, may hold values from 0.5 to 1.5
- w_o: bfloat16 [4096, 2048], P('shard'), may hold values from -0.09375 to 0.09375
- w_gu: bfloat16 [2048, 11264], P('shard'), may hold values from -0.125 to 0.125
- w_down: bfloat16 [5632, 2048], P('shard'), may hold values from -0.078125 to 0.078125
Outputs:
- output: bfloat16 [16, 256, 2048], P(('shard', 'replica'), 'seq')
- input_grad: bfloat16 [16, 256, 2048], P(('shard', 'replica'), 'seq')
- norm_gains_grad: float32 [2, 2048], P(None, ('shard', 'seq'))
- w_in_grad: float32 [2048, 12288], P(('shard', 'seq'))
- w_ab_grad: float32 [2048, 32], P(('shard', 'seq'))
- conv_grad: float32 [4, 8192], P(None, ('shard', 'seq'))
- gate_params_grad: float32 [2, 16], replicated
- onorm_grad: float32 [256], replicated
- w_o_grad: float32 [4096, 2048], P(('shard', 'seq'))
- w_gu_grad: float32 [2048, 11264], P(('shard', 'seq'))
- w_down_grad: float32 [5632, 2048], P(('shard', 'seq'))
Inputs may be any that keep to these rules, and one draw needn't show every extreme that they name: `lengths`: each aligned run of 2 slots holds one slot of exactly 256 valid tokens; positions from a slot's length on are padding. `gate_params`: row 0 holds the logarithms of the heads' decay speeds, row 1 the biases added before the softplus.
All inputs are finite; a program needn't handle non-finite values.
Results may differ from a plain program's by a relative error of at most 0.017.
Values may be sent and summed in bfloat16 or wider, within the bound.
No kernel may reach another device: no remote copies, remote signals or barrier semaphores. Data moves between devices by JAX's collectives and lax.ppermute only.
A program may use at most 576 MiB of HBM per device.

v0:
```python
import jax
import jax.numpy as jnp
from jax import lax
from jax.sharding import PartitionSpec as P

D = 2048
HEADS = 16
DK = 128
DV = 256
FF = 5632
KERNEL = 4
BLOCK = 64
KD = 2048
VD = 4096
CONVW = 8192
PROJW = 12288


HIGHEST = lax.Precision.HIGHEST
EPS = 1e-06


def shifted(value, axis, steps):
    count = lax.axis_size(axis)
    leading, last = (max(0, -steps), min(count, count - steps))
    return lax.ppermute(value, axis, [(source, source + steps) for source in range(leading, last)])


def rms_scaled(values, gain):
    return values * lax.rsqrt(jnp.mean(values * values, -1, keepdims=True) + EPS) * gain


def block_step(state_now, block_item):
    queries, key_rows, values, decays, write_rate = block_item
    block_width = decays.shape[-1]
    cumul = jnp.cumsum(decays, -1)
    row_ids = lax.broadcasted_iota(jnp.int32, (block_width, block_width), 0)
    col_ids = lax.broadcasted_iota(jnp.int32, (block_width, block_width), 1)
    inclusive = row_ids >= col_ids
    strict = row_ids > col_ids
    spread = cumul[:, :, None] - cumul[:, None, :]
    decay_weight = jnp.where(inclusive, jnp.exp(jnp.where(inclusive, spread, 0.0)), 0.0)
    inner_keys = jnp.einsum("hcd,hsd->hcs", key_rows, key_rows, precision=HIGHEST)
    system = jnp.eye(block_width, dtype=jnp.float32) + jnp.where(
        strict, write_rate[:, :, None] * inner_keys * decay_weight, 0.0
    )
    start_decay = jnp.exp(cumul)[:, :, None]
    recalled = jnp.einsum("hcd,hdw->hcw", key_rows, state_now, precision=HIGHEST)
    target = write_rate[:, :, None] * (values - start_decay * recalled)
    update = lax.linalg.triangular_solve(
        system, target, left_side=True, lower=True, unit_diagonal=True
    )
    scores = jnp.einsum("hcd,hsd->hcs", queries, key_rows, precision=HIGHEST) * decay_weight
    outputs = start_decay * jnp.einsum("hcd,hdw->hcw", queries, state_now, precision=HIGHEST)
    outputs = outputs + jnp.einsum("hcs,hsw->hcw", scores, update, precision=HIGHEST)
    total_decay = cumul[:, -1]
    tail_decay = jnp.exp(total_decay[:, None] - cumul)[:, :, None]
    new_state = jnp.exp(total_decay)[:, None, None] * state_now
    new_state = new_state + jnp.einsum(
        "hcd,hcw->hdw", key_rows * tail_decay, update, precision=HIGHEST
    )
    return (new_state, outputs)


def to_blocks(stacked):
    head_count, length = (stacked.shape[0], stacked.shape[1])
    shaped = stacked.reshape((head_count, length // BLOCK, BLOCK) + stacked.shape[2:])
    return jnp.moveaxis(shaped, 1, 0)


def segment(state_now, queries, key_rows, values, decays, write_rate):
    blocks = tuple(
        (to_blocks(stacked) for stacked in (queries, key_rows, values, decays, write_rate))
    )
    final_state, outputs = lax.scan(block_step, state_now, blocks)
    outputs = jnp.moveaxis(outputs, 0, 1)
    return (outputs.reshape(outputs.shape[0], -1, outputs.shape[-1]), final_state)


def prepare(extended, conv_f32, rate_in, gate_params, valid_mask):
    length = rate_in.shape[0]
    mixed = sum((conv_f32[offset] * extended[offset : offset + length] for offset in range(KERNEL)))
    active = jax.nn.silu(mixed)
    queries = active[:, :KD].reshape(length, HEADS, DK)
    key_rows = active[:, KD : 2 * KD].reshape(length, HEADS, DK)
    values = active[:, 2 * KD :].reshape(length, HEADS, DV)
    queries = (
        queries * lax.rsqrt(jnp.sum(queries * queries, -1, keepdims=True) + EPS) * DK ** (-0.5)
    )
    key_rows = key_rows * lax.rsqrt(jnp.sum(key_rows * key_rows, -1, keepdims=True) + EPS)
    decays = (
        -jnp.exp(gate_params[0])
        * jax.nn.softplus(rate_in[:, :HEADS] + gate_params[1])
        * valid_mask[:, None]
    )
    write_rate = jax.nn.sigmoid(rate_in[:, HEADS:]) * valid_mask[:, None]
    return (
        jnp.swapaxes(queries, 0, 1),
        jnp.swapaxes(key_rows, 0, 1),
        jnp.swapaxes(values, 0, 1),
        decays.T,
        write_rate.T,
    )


def finish(head_out, gate_pre, out_gain):
    rows_first = jnp.swapaxes(head_out, 0, 1)
    scaled = rms_scaled(rows_first, out_gain)
    return scaled.reshape(gate_pre.shape) * jax.nn.silu(gate_pre)


def chain_forward(transfer, carried_state):
    state_now = jnp.zeros_like(carried_state)
    for turn_index in range(lax.axis_size("seq") - 1):
        advanced = (
            jnp.einsum("hij,hjk->hik", transfer, state_now, precision=HIGHEST) + carried_state
        )
        state_now = shifted(advanced.astype(jnp.bfloat16), "seq", 1).astype(advanced.dtype)
    return state_now


def chain_backward(transposed, local_grad):
    state_grad = jnp.zeros_like(local_grad)
    for turn_index in range(lax.axis_size("seq") - 1):
        advanced = (
            jnp.einsum("hij,hjk->hik", transposed, state_grad, precision=HIGHEST) + local_grad
        )
        state_grad = shifted(advanced.astype(jnp.bfloat16), "seq", -1).astype(advanced.dtype)
    return state_grad


def gather_mixer(norm_gains, w_in, w_ab, conv_weight, w_o):
    return (
        lax.all_gather(norm_gains, "shard", axis=1, tiled=True),
        lax.all_gather(w_in, "shard", axis=0, tiled=True),
        lax.all_gather(w_ab, "shard", axis=0, tiled=True),
        lax.all_gather(conv_weight, "shard", axis=1, tiled=True),
        lax.all_gather(w_o, "shard", axis=0, tiled=True),
    )


def gather_mlp(w_gu, w_down):
    return (
        lax.all_gather(w_gu, "shard", axis=0, tiled=True),
        lax.all_gather(w_down, "shard", axis=0, tiled=True),
    )


def body(
    tokens,
    cotangent,
    lengths,
    norm_gains,
    w_in,
    w_ab,
    conv_weight,
    gate_params,
    onorm_gain,
    w_o,
    w_gu,
    w_down,
):
    micro_count = tokens.shape[0]
    row_count = tokens.shape[1]
    flat_rows = micro_count * row_count
    margin = KERNEL - 1
    stacked_heads = micro_count * HEADS
    position = lax.axis_index("seq") * row_count + jnp.arange(row_count, dtype=jnp.int32)
    eye_key = jnp.broadcast_to(jnp.eye(DK, dtype=jnp.float32), (stacked_heads, DK, DK))
    zero_state = jnp.zeros((stacked_heads, DK, DV), jnp.float32)
    owners = lax.axis_size("shard") * lax.axis_size("seq")
    owner_index = lax.axis_index("shard") * lax.axis_size("seq") + lax.axis_index("seq")
    gain_rows, in_full, ab_full, conv_full, out_full = gather_mixer(
        norm_gains, w_in, w_ab, conv_weight, w_o
    )
    gain_rows = gain_rows.astype(jnp.float32)
    flat_in = tokens.reshape(flat_rows, D).astype(jnp.float32)
    normed = rms_scaled(flat_in, gain_rows[0]).astype(jnp.bfloat16)
    projected = jnp.dot(normed, in_full, preferred_element_type=jnp.float32)
    conv_in = projected[:, :CONVW].astype(jnp.bfloat16).reshape(micro_count, row_count, CONVW)
    gate_pre = projected[:, CONVW:].reshape(micro_count, row_count, VD)
    rate_in = jnp.dot(normed, ab_full, preferred_element_type=jnp.float32).reshape(
        micro_count, row_count, 2 * HEADS
    )
    carried = shifted(conv_in[:, row_count - margin :], "seq", 1)
    extended = jnp.concatenate([carried, conv_in], 1).astype(jnp.float32)
    valid_mask = (position[None, :] < lengths[:, None]).astype(jnp.float32)
    batched_prepare = jax.vmap(prepare, in_axes=(0, None, 0, None, 0))

    def prepared(ext_rows, kernel, rate_rows, params):
        return batched_prepare(ext_rows, kernel, rate_rows, params, valid_mask)

    mixer_inputs, prepare_back = jax.vjp(
        prepared, extended, conv_full.astype(jnp.float32), rate_in, gate_params
    )
    queries, key_rows, values, decays, write_rate = tuple(
        (item.reshape((stacked_heads,) + item.shape[2:]) for item in mixer_inputs)
    )
    transfer = segment(eye_key, queries, key_rows, jnp.zeros_like(queries), decays, write_rate)[1]
    carried_state = segment(zero_state, queries, key_rows, values, decays, write_rate)[1]
    state_in = chain_forward(transfer, carried_state)
    primal, segment_back = jax.vjp(segment, state_in, queries, key_rows, values, decays, write_rate)
    head_out = primal[0].reshape(micro_count, HEADS, row_count, DV)
    gated, finish_back = jax.vjp(
        jax.vmap(finish, in_axes=(0, 0, None)), head_out, gate_pre, onorm_gain
    )
    mixed_in = gated.reshape(flat_rows, VD).astype(jnp.bfloat16)
    middle = flat_in + jnp.dot(mixed_in, out_full, preferred_element_type=jnp.float32)
    renormed = rms_scaled(middle, gain_rows[1]).astype(jnp.bfloat16)
    gate_up_full, down_full = gather_mlp(w_gu, w_down)
    gate_up = jnp.dot(renormed, gate_up_full, preferred_element_type=jnp.float32)
    gate_part = gate_up[:, :FF]
    up_part = gate_up[:, FF:]
    hidden = (jax.nn.silu(gate_part) * up_part).astype(jnp.bfloat16)
    result = middle + jnp.dot(hidden, down_full, preferred_element_type=jnp.float32)
    results = result.astype(jnp.bfloat16).reshape(micro_count, row_count, D)
    normed_own, renormed_own, mixed_own, hidden_own = (
        lax.all_to_all(normed, ("shard", "seq"), split_axis=1, concat_axis=0, tiled=True),
        lax.all_to_all(renormed, ("shard", "seq"), split_axis=1, concat_axis=0, tiled=True),
        lax.all_to_all(mixed_in, ("shard", "seq"), split_axis=1, concat_axis=0, tiled=True),
        lax.all_to_all(hidden, ("shard", "seq"), split_axis=1, concat_axis=0, tiled=True),
    )
    upstream = cotangent.reshape(flat_rows, D)
    gate_up_full, down_full = gather_mlp(w_gu, w_down)
    hidden_grad = jnp.dot(upstream, down_full.T, preferred_element_type=jnp.float32)
    sigmoid_gate = jax.nn.sigmoid(gate_part)
    silu_slope = sigmoid_gate * (1.0 + gate_part * (1.0 - sigmoid_gate))
    gate_up_grad = jnp.concatenate(
        [hidden_grad * up_part * silu_slope, hidden_grad * gate_part * sigmoid_gate], 1
    ).astype(jnp.bfloat16)
    renormed_grad = jnp.dot(gate_up_grad, gate_up_full.T, preferred_element_type=jnp.float32)
    unused_norm, norm2_back = jax.vjp(rms_scaled, middle, gain_rows[1])
    middle_grad, gain2_grad = norm2_back(renormed_grad)
    middle_grad = middle_grad + upstream.astype(jnp.float32)
    mixed_grad = middle_grad.astype(jnp.bfloat16)
    gu_piece = lax.all_gather(gate_up_grad, ("shard", "seq"), axis=0, tiled=True)
    mid_piece = lax.all_gather(mixed_grad, ("shard", "seq"), axis=0, tiled=True)
    cot_piece = lax.all_gather(upstream, ("shard", "seq"), axis=0, tiled=True)
    gu_total = jnp.dot(renormed_own.T, gu_piece, preferred_element_type=jnp.float32)
    down_total = jnp.dot(hidden_own.T, cot_piece, preferred_element_type=jnp.float32)
    out_total = jnp.dot(mixed_own.T, mid_piece, preferred_element_type=jnp.float32)
    grad_gu = gu_total
    grad_down = down_total
    grad_out = out_total
    gated_grad = jnp.dot(mixed_grad, out_full.T, preferred_element_type=jnp.float32).reshape(
        micro_count, row_count, VD
    )
    head_grad, gate_pre_grad, onorm_grad = finish_back(gated_grad)
    head_grad = head_grad.reshape(stacked_heads, row_count, DV)
    local_grad = segment_back((head_grad, jnp.zeros_like(state_in)))[0]
    state_out_grad = chain_backward(jnp.swapaxes(transfer, 1, 2), local_grad)
    pieces = segment_back((head_grad, state_out_grad))[1:]
    pieces = tuple((item.reshape((micro_count, HEADS) + item.shape[1:]) for item in pieces))
    ext_grad, conv_grad, rate_grad, params_grad = prepare_back(pieces)
    carried_back = shifted(ext_grad[:, :margin].astype(jnp.bfloat16), "seq", -1).astype(jnp.float32)
    own_grad = ext_grad[:, margin:]
    own_grad = jnp.concatenate(
        [own_grad[:, : row_count - margin], own_grad[:, row_count - margin :] + carried_back], 1
    )
    proj_grad = (
        jnp.concatenate([own_grad, gate_pre_grad], 2).reshape(flat_rows, PROJW).astype(jnp.bfloat16)
    )
    rate_grad = rate_grad.reshape(flat_rows, 2 * HEADS)
    grad_ab = jnp.dot(normed.astype(jnp.float32).T, rate_grad, precision=HIGHEST)
    normed_grad = jnp.dot(proj_grad, in_full.T, preferred_element_type=jnp.float32)
    normed_grad = normed_grad + jnp.dot(rate_grad, ab_full.astype(jnp.float32).T, precision=HIGHEST)
    unused_first, norm1_back = jax.vjp(rms_scaled, flat_in, gain_rows[0])
    inputs_grad, gain1_grad = norm1_back(normed_grad)
    input_grads = (
        (inputs_grad + middle_grad).astype(jnp.bfloat16).reshape(micro_count, row_count, D)
    )
    grad_in = jnp.dot(
        normed_own.T,
        lax.all_gather(proj_grad, ("shard", "seq"), axis=0, tiled=True),
        preferred_element_type=jnp.float32,
    )
    summed = (grad_gu, grad_down, grad_out, grad_in)
    small_sums = (params_grad, onorm_grad, jnp.stack([gain1_grad, gain2_grad]), conv_grad, grad_ab)
    owned = (
        lax.psum(summed[0].astype(jnp.bfloat16), "replica").astype(jnp.float32),
        lax.psum(summed[1].astype(jnp.bfloat16), "replica").astype(jnp.float32),
        lax.psum(summed[2].astype(jnp.bfloat16), "replica").astype(jnp.float32),
        lax.psum(summed[3].astype(jnp.bfloat16), "replica").astype(jnp.float32),
    )
    small_total = lax.psum(
        (small_sums[0], small_sums[1], small_sums[2], small_sums[3], small_sums[4]),
        ("shard", "seq", "replica"),
    )
    grad_gu, grad_down, grad_out, grad_in = owned
    params_total, onorm_total, gains_total, conv_total, ab_total = small_total
    own_width = D // owners
    conv_width = CONVW // owners
    gains_own = lax.dynamic_slice_in_dim(gains_total, owner_index * own_width, own_width, 1)
    ab_own = lax.dynamic_slice_in_dim(ab_total, owner_index * own_width, own_width, 0)
    conv_own = lax.dynamic_slice_in_dim(conv_total, owner_index * conv_width, conv_width, 1)
    return (
        results,
        input_grads,
        gains_own,
        grad_in,
        ab_own,
        conv_own,
        params_total,
        onorm_total,
        grad_out,
        grad_gu,
        grad_down,
    )


def solution(mesh):
    in_specs = (
        P(("shard", "replica"), "seq", None),
        P(("shard", "replica"), "seq", None),
        P(("shard", "replica")),
        P(None, "shard"),
        P("shard", None),
        P("shard", None),
        P(None, "shard"),
        P(),
        P(),
        P("shard", None),
        P("shard", None),
        P("shard", None),
    )
    out_specs = (
        P(("shard", "replica"), "seq", None),
        P(("shard", "replica"), "seq", None),
        P(None, ("shard", "seq")),
        P(("shard", "seq"), None),
        P(("shard", "seq"), None),
        P(None, ("shard", "seq")),
        P(),
        P(),
        P(("shard", "seq"), None),
        P(("shard", "seq"), None),
        P(("shard", "seq"), None),
    )
    return jax.shard_map(body, mesh=mesh, in_specs=in_specs, out_specs=out_specs, check_vma=False)
```

profile of v0, /device:TPU:0, one launch (start us, length us, event | category | flops | bytes accessed | tf_op | source)
XLA Modules:
  0.0 1786.1 jit_solution(5197975560398596853)
XLA Ops:
  18.6 66.9 %all-gather.9.cloned.1.call-done = bf16[2048,12288]{1,0:T(8,128)(2,1)} async-done(((bf16[1024,12288]{1,0:T(8,128)(2,1)}), bf16[2048,12288]{1,0:T(8,128)(2,1)}) %all-gather.9.cloned.1.call-update) | async-done | bytes 50331664 | tf_op jit(solution)/shard_map/all_gather | solution.py:135
  85.5 23.6 %fusion.133 = f32[128,12288]{1,0:T(8,128)S(1)} fusion(bf16[128,2048]{1,0:T(8,128)(2,1)S(1)} %fusion.74, bf16[2048,12288]{1,0:T(8,128)(2,1)} %all-gather.9.cloned.1.call-done), kind=kOutput, calls=%fused_computation.260 | convolution fusion | flops 6442450944 | bytes 57147392 | tf_op jit(solution)/shard_map/dot_general | solution.py:179
  134.5 4.7 copy.506
  139.2 7.9 add_bitcast_fusion
  147.1 69.4 %custom-call.15 = f32[32,1,64,64]{0,2,3,1:T(8,128)} custom-call(f32[32,1,64,64]{0,3,2,1:T(8,128)} %get-tuple-element.647), custom_call_target="InvertDiagBlocksLowerTriangular" | custom-call | tf_op jit(solution)/shard_map/while/body/eval_jaxpr/triangular_solve | solution.py:50
  232.5 4.4 fusion.89
  239.2 4.5 collective-permute-start.1
  243.7 44.5 %collective-permute-done.1 = bf16[32,128,256]{2,1,0:T(8,128)(2,1)S(1)} collective-permute-done((bf16[32,128,256]{2,1,0:T(8,128)(2,1)S(1)}, bf16[32,128,256]{2,1,0:T(8,128)(2,1)S(1)}, u32[]{:S(2)}, u32[]{:S(2)}) %collective-permute-start.1) | collective-permute-done | bytes 2097184 | tf_op jit(solution)/shard_map/ppermute | solution.py:26
  290.7 4.5 collective-permute-start.2
  295.3 44.0 %collective-permute-done.2 = bf16[32,128,256]{2,1,0:T(8,128)(2,1)S(1)} collective-permute-done((bf16[32,128,256]{2,1,0:T(8,128)(2,1)S(1)}, bf16[32,128,256]{2,1,0:T(8,128)(2,1)S(1)}, u32[]{:S(2)}, u32[]{:S(2)}) %collective-permute-start.2) | collective-permute-done | bytes 2097184 | tf_op jit(solution)/shard_map/ppermute | solution.py:26
  343.1 6.6 collective-permute-start.3
  356.2 52.6 %collective-permute-done.3 = bf16[32,128,256]{2,1,0:T(8,128)(2,1)} collective-permute-done((bf16[32,128,256]{2,1,0:T(8,128)(2,1)}, bf16[32,128,256]{2,1,0:T(8,128)(2,1)}, u32[]{:S(2)}, u32[]{:S(2)}) %collective-permute-start.3) | collective-permute-done | bytes 2097184 | tf_op jit(solution)/shard_map/ppermute | solution.py:26
  408.8 4.8 bitcast_subtract_fusion
  434.8 8.7 multiply_reduce_fusion.12
  445.5 20.1 %fusion.139 = f32[128,11264]{1,0:T(8,128)} fusion(bf16[128,2048]{1,0:T(8,128)(2,1)} %multiply_convert_fusion.4, bf16[2048,11264]{1,0:T(8,128)(2,1)} %all-gather.13.cloned.1.call-done), kind=kOutput, calls=%fused_computation.266 | convolution fusion | flops 5905580032 | bytes 52428800 | tf_op jit(solution)/shard_map/dot_general | solution.py:211
  465.6 15.4 multiply_convert_fusion.1
  481.0 23.0 %multiply_reduce_fusion.9 = (f32[2048]{0:T(1024)}, f32[128]{0:T(128)S(1)}, f32[128,2048]{1,0:T(8,128)}) fusion(f32[128,2048]{1,0:T(8,128)} %copy-done.8, f32[128]{0:T(128)S(1)} %fusion.113, f32[2048]{0:T(1024)S(1)} %bitcast.437, bf16[2048,11264]{1,0:T(8,128)(2,1)} %all-gather.13.cloned.1.call-done, bf16[128,5632]{1,0:T(8,128)(2,1)} %get-tuple-element.627, ...), kind=kOutput, calls=%fused_computation.155 | convolution fusion | flops 5912918016 | bytes 51135488 | tf_op jit(solution)/shard_map/dot_general | solution.py:231
  516.6 13.3 fusion.140
  530.0 5.0 fusion.129
  540.8 6.3 fusion.15
  553.0 4.2 fusion.39
  557.2 5.5 add_add_fusion
  567.7 70.2 %collective-permute-done.4 = bf16[32,128,256]{2,1,0:T(8,128)(2,1)S(1)} collective-permute-done((bf16[32,128,256]{2,1,0:T(8,128)(2,1)S(1)}, bf16[32,128,256]{2,1,0:T(8,128)(2,1)S(1)}, u32[]{:S(2)}, u32[]{:S(2)}) %collective-permute-start.4) | collective-permute-done | bytes 2097184 | tf_op jit(solution)/shard_map/ppermute | solution.py:26
  641.8 92.0 %collective-permute-done.5 = bf16[32,128,256]{2,1,0:T(8,128)(2,1)S(1)} collective-permute-done((bf16[32,128,256]{2,1,0:T(8,128)(2,1)S(1)}, bf16[32,128,256]{2,1,0:T(8,128)(2,1)S(1)}, u32[]{:S(2)}, u32[]{:S(2)}) %collective-permute-start.5) | collective-permute-done | bytes 2097184 | tf_op jit(solution)/shard_map/ppermute | solution.py:26
  743.1 52.5 %collective-permute-done.6 = bf16[32,128,256]{2,1,0:T(8,128)(2,1)} collective-permute-done((bf16[32,128,256]{2,1,0:T(8,128)(2,1)}, bf16[32,128,256]{2,1,0:T(8,128)(2,1)}, u32[]{:S(2)}, u32[]{:S(2)}) %collective-permute-start.6) | collective-permute-done | bytes 2097184 | tf_op jit(solution)/shard_map/ppermute | solution.py:26
  807.4 9.5 multiply_reduce_fusion.7
  830.2 4.7 multiply_reduce_fusion.10
  838.2 4.8 fusion.56
  860.4 10.8 multiply_reduce_fusion.3
  871.2 5.4 broadcast_multiply_fusion
  876.7 4.3 fusion.128
  882.9 5.6 collective-permute-done.7
  894.4 4.4 all-to-all-start.3
  906.2 22.4 %all-to-all-done.3 = bf16[128,8,704]{0,2,1:T(8,128)(2,1)} async-done(((bf16[128,8,704]{0,2,1:T(8,128)(2,1)}), bf16[128,8,704]{0,2,1:T(8,128)(2,1)}, u32[]{:S(2)}, u32[]{:S(2)}) %all-to-all-start.3) | async-done | bytes 1441824 | tf_op jit(solution)/shard_map/all_to_all | solution.py:221
  928.6 4.3 all-to-all-start.1
  932.9 7.4 convolution_convert_fusion.2
  948.9 10.4 all-to-all-done.1
  962.9 6.3 convolution_convert_fusion.3
  976.5 16.4 convolution_convert_fusion.1
  993.0 55.7 %all-gather.17.cloned.1.call-done = bf16[1024,12288]{1,0:T(8,128)(2,1)} async-done(((bf16[128,12288]{1,0:T(8,128)(2,1)}), bf16[1024,12288]{1,0:T(8,128)(2,1)}) %all-gather.17.cloned.1.call-update) | async-done | bytes 25165840 | tf_op jit(solution)/shard_map/all_gather | solution.py:274
  1048.6 17.1 convolution_convert_fusion
  1067.0 12.1 fusion.3
  1079.2 23.5 %fusion.122 = f32[128,2048]{1,0:T(8,128)} fusion(bf16[2048,12288]{1,0:T(8,128)(2,1)} %all-gather.9.cloned.1.call-done, bf16[128,4096]{1,0:T(8,128)(2,1)} %get-tuple-element.629, bf16[128,8192]{1,0:T(8,128)(2,1)S(1)} %bitcast.384), kind=kOutput, calls=%fused_computation.252 | convolution fusion | flops 6448742400 | bytes 54525952 | tf_op jit(solution)/shard_map/dot_general | solution.py:265
  1106.2 39.7 %all-reduce.16 = (f32[2,2048]{1,0:T(2,128)S(1)}, f32[2,16]{1,0:T(2,128)}, f32[256]{0:T(256)}) all-reduce(f32[2,2048]{1,0:T(2,128)S(1)} %pad_maximum_fusion.3, f32[2,16]{1,0:T(2,128)S(1)} %pad_add_fusion.3, f32[256]{0:T(256)S(1)} %copy-done.103), channel_id=1, replica_groups=mesh['shard'=2,'seq'=4,'replica'=4] {'shard','seq','replica'}, use_global_device_ids=true, to_apply=%region_23.26 | all-reduce | flops 4384 | bytes 35072 | tf_op jit(solution)/shard_map/psum | solution.py:285
  1149.3 31.7 %all-reduce.22.cloned.1.call-done = (f32[2048,32]{0,1:T(8,128)}, f32[4,8192]{1,0:T(4,128)}) async-done(((f32[2048,32]{0,1:T(8,128)}, f32[4,8192]{1,0:T(4,128)}), (f32[2048,32]{0,1:T(8,128)}, f32[4,8192]{1,0:T(4,128)})) %all-reduce.22.cloned.1.call-update) | async-done | bytes 393232 | tf_op jit(solution)/shard_map/psum | solution.py:285
  1183.6 574.6 %all-reduce.24.cloned.1.call-done = (bf16[256,12288]{1,0:T(8,128)(2,1)}, bf16[512,2048]{1,0:T(8,128)(2,1)}, bf16[256,11264]{1,0:T(8,128)(2,1)}, bf16[704,2048]{1,0:T(8,128)(2,1)}) async-done(((bf16[256,12288]{1,0:T(8,128)(2,1)}, bf16[512,2048]{1,0:T(8,128)(2,1)}, bf16[256,11264]{1,0:T(8,128)(2,1)}, bf16[704,2048]{1,0:T(8,128)(2,1)}), (bf16[256,12288]{1,0:T(8,128)(2,1)}, bf16[512,2048]{1,0:T(8,128)(2,1)}, ...) | async-done | bytes 17039376 | tf_op jit(solution)/shard_map/psum | solution.py:283
  1758.2 9.2 convert_element_type.175
  1767.4 5.8 convert_element_type.179
  (427 shorter events, 229.4 us)
Async XLA Ops:
  7.2 78.3 %all-gather.9.cloned.1.call-start = ((), (), s32[]{:S(2)}) async-start(), calls=%async_computation.4 | async-start | bytes 75497472 | tf_op jit(solution)/shard_map/all_gather | solution.py:135
  7.9 426.9 %all-gather.11.cloned.1.call-start = ((), (), s32[]{:S(2)}) async-start(), calls=%async_computation.5 | async-start | bytes 25165824 | tf_op jit(solution)/shard_map/all_gather | solution.py:138
  8.7 436.8 %all-gather.13.cloned.1.call-start = ((), (), s32[]{:S(2)}) async-start(), calls=%async_computation.6 | async-start | bytes 69206016 | tf_op jit(solution)/shard_map/all_gather | solution.py:144
  9.5 456.1 %all-gather.15.cloned.1.call-start = ((), (), s32[]{:S(2)}) async-start(), calls=%async_computation.7 | async-start | bytes 34603008 | tf_op jit(solution)/shard_map/all_gather | solution.py:145
  10.0 922.9 %all-gather.23.cloned.1.call-start = ((), (), s32[]{:S(2)}) async-start(), calls=%async_computation.11 | async-start | bytes 4718592 | tf_op jit(solution)/shard_map/all_gather | solution.py:238
  12.9 96.2 %copy-start.96 = (f32[128]{0:T(128)}, f32[128]{0:T(128)S(1)}, u32[]{:S(2)}) copy-start(f32[128]{0:T(128)S(1)} %rsqrt.56) | copy-start | bytes 1540
  14.9 94.1 %copy-start.79 = (f32[1,2048]{1,0:T(1,128)}, f32[1,2048]{1,0:T(1,128)S(1)}, u32[]{:S(2)}) copy-start(f32[1,2048]{1,0:T(1,128)S(1)} %get-tuple-element.659) | copy-start | bytes 24580
  14.9 489.1 %copy-start.73 = (f32[1,2048]{1,0:T(1,128)}, f32[1,2048]{1,0:T(1,128)S(1)}, u32[]{:S(2)}) copy-start(f32[1,2048]{1,0:T(1,128)S(1)} %get-tuple-element.658) | copy-start | bytes 24580
  18.6 98.4 %copy-start.65 = (f32[1,8192]{1,0:T(1,128)}, f32[1,8192]{1,0:T(1,128)S(1)}, u32[]{:S(2)}) copy-start(f32[1,8192]{1,0:T(1,128)S(1)} %get-tuple-element.642) | copy-start | bytes 98308
  18.6 98.4 %copy-start.67 = (f32[1,8192]{1,0:T(1,128)}, f32[1,8192]{1,0:T(1,128)S(1)}, u32[]{:S(2)}) copy-start(f32[1,8192]{1,0:T(1,128)S(1)} %get-tuple-element.643) | copy-start | bytes 98308
  18.6 98.4 %copy-start.69 = (f32[1,8192]{1,0:T(1,128)}, f32[1,8192]{1,0:T(1,128)S(1)}, u32[]{:S(2)}) copy-start(f32[1,8192]{1,0:T(1,128)S(1)} %get-tuple-element.644) | copy-start | bytes 98308
  18.6 98.4 %copy-start.71 = (f32[1,8192]{1,0:T(1,128)}, f32[1,8192]{1,0:T(1,128)S(1)}, u32[]{:S(2)}) copy-start(f32[1,8192]{1,0:T(1,128)S(1)} %get-tuple-element.645) | copy-start | bytes 98308
  109.1 11.7 copy-start.22
  109.4 6.9 collective-permute-start
  239.2 49.1 %collective-permute-start.1 = (bf16[32,128,256]{2,1,0:T(8,128)(2,1)S(1)}, bf16[32,128,256]{2,1,0:T(8,128)(2,1)S(1)}, u32[]{:S(2)}, u32[]{:S(2)}) collective-permute-start(bf16[32,128,256]{2,1,0:T(8,128)(2,1)S(1)} %add_convert_fusion.5), channel_id=1, source_target_pairs={{0,4},{4,8},{8,12},{1,5},{5,9},{9,13},{2,6},{6,10},{10,14},{3,7},{... | collective-permute-start | bytes 6291464 | tf_op jit(solution)/shard_map/ppermute | solution.py:26
  290.7 48.6 %collective-permute-start.2 = (bf16[32,128,256]{2,1,0:T(8,128)(2,1)S(1)}, bf16[32,128,256]{2,1,0:T(8,128)(2,1)S(1)}, u32[]{:S(2)}, u32[]{:S(2)}) collective-permute-start(bf16[32,128,256]{2,1,0:T(8,128)(2,1)S(1)} %add_convert_fusion.4), channel_id=1, source_target_pairs={{0,4},{4,8},{8,12},{1,5},{5,9},{9,13},{2,6},{6,10},{10,14},{3,7},{... | collective-permute-start | bytes 6291464 | tf_op jit(solution)/shard_map/ppermute | solution.py:26
  343.1 65.8 %collective-permute-start.3 = (bf16[32,128,256]{2,1,0:T(8,128)(2,1)}, bf16[32,128,256]{2,1,0:T(8,128)(2,1)}, u32[]{:S(2)}, u32[]{:S(2)}) collective-permute-start(bf16[32,128,256]{2,1,0:T(8,128)(2,1)} %add_convert_fusion.3), channel_id=1, source_target_pairs={{0,4},{4,8},{8,12},{1,5},{5,9},{9,13},{2,6},{6,10},{10,14},{3,7},{... | collective-permute-start | bytes 6291464 | tf_op jit(solution)/shard_map/ppermute | solution.py:26
  349.7 613.1 %all-gather.19.cloned.1.call-start = ((), (), s32[]{:S(2)}) async-start(), calls=%async_computation.9 | async-start | bytes 4718592 | tf_op jit(solution)/shard_map/all_gather | solution.py:237
  356.2 58.7 %copy-start.16 = (f32[32,64,64]{2,1,0:T(8,128)S(1)}, f32[32,64,64]{2,1,0:T(8,128)}, u32[]{:S(2)}) copy-start(f32[32,64,64]{2,1,0:T(8,128)} %copy-done.14) | copy-start | bytes 1572868
  443.6 60.4 %copy-start.94 = (f32[128]{0:T(128)}, f32[128]{0:T(128)S(1)}, u32[]{:S(2)}) copy-start(f32[128]{0:T(128)S(1)} %fusion.113) | copy-start | bytes 1540
  506.9 469.7 %all-gather.21.cloned.1.call-start = ((), (), s32[]{:S(2)}) async-start(), calls=%async_computation.10 | async-start | bytes 25952256 | tf_op jit(solution)/shard_map/all_gather | solution.py:236
  510.5 538.1 %all-gather.17.cloned.1.call-start = ((), (), s32[]{:S(2)}) async-start(), calls=%async_computation.8 | async-start | bytes 28311552 | tf_op jit(solution)/shard_map/all_gather | solution.py:274
  548.3 190.7 %copy-start.4 = (f32[2,16,64,256]{3,2,1,0:T(8,128)}, f32[2,16,64,256]{3,2,1,0:T(8,128)S(1)}, u32[]{:S(2)}) copy-start(f32[2,16,64,256]{3,2,1,0:T(8,128)S(1)} %copy.522) | copy-start | bytes 6291460
  566.4 71.5 %collective-permute-start.4 = (bf16[32,128,256]{2,1,0:T(8,128)(2,1)S(1)}, bf16[32,128,256]{2,1,0:T(8,128)(2,1)S(1)}, u32[]{:S(2)}, u32[]{:S(2)}) collective-permute-start(bf16[32,128,256]{2,1,0:T(8,128)(2,1)S(1)} %add_convert_fusion.2), channel_id=1, source_target_pairs={{4,0},{8,4},{12,8},{5,1},{9,5},{13,9},{6,2},{10,6},{14,10},{7,3},{... | collective-permute-start | bytes 6291464 | tf_op jit(solution)/shard_map/ppermute | solution.py:26
  640.3 98.7 %copy-start.2 = (f32[32,64,256]{2,1,0:T(8,128)S(1)}, f32[32,64,256]{2,1,0:T(8,128)}, u32[]{:S(2)}) copy-start(f32[32,64,256]{2,1,0:T(8,128)} %copy-done.1) | copy-start | bytes 6291460
  640.3 93.4 %collective-permute-start.5 = (bf16[32,128,256]{2,1,0:T(8,128)(2,1)S(1)}, bf16[32,128,256]{2,1,0:T(8,128)(2,1)S(1)}, u32[]{:S(2)}, u32[]{:S(2)}) collective-permute-start(bf16[32,128,256]{2,1,0:T(8,128)(2,1)S(1)} %add_convert_fusion.1), channel_id=1, source_target_pairs={{4,0},{8,4},{12,8},{5,1},{9,5},{13,9},{6,2},{10,6},{14,10},{7,3},{... | collective-permute-start | bytes 6291464 | tf_op jit(solution)/shard_map/ppermute | solution.py:26
  737.5 58.2 %collective-permute-start.6 = (bf16[32,128,256]{2,1,0:T(8,128)(2,1)}, bf16[32,128,256]{2,1,0:T(8,128)(2,1)}, u32[]{:S(2)}, u32[]{:S(2)}) collective-permute-start(bf16[32,128,256]{2,1,0:T(8,128)(2,1)} %add_convert_fusion), channel_id=1, source_target_pairs={{4,0},{8,4},{12,8},{5,1},{9,5},{13,9},{6,2},{10,6},{14,10},{7,3},{... | collective-permute-start | bytes 6291464 | tf_op jit(solution)/shard_map/ppermute | solution.py:26
  743.1 56.0 %copy-start.3 = (f32[32,64,256]{2,1,0:T(8,128)S(1)}, f32[32,64,256]{2,1,0:T(8,128)}, u32[]{:S(2)}) copy-start(f32[32,64,256]{2,1,0:T(8,128)} %copy-done.1) | copy-start | bytes 6291460
  860.4 10.8 copy-start.66
  860.4 10.8 copy-start.68
  860.4 10.8 copy-start.70
  881.0 7.5 collective-permute-start.7
  894.4 34.1 %all-to-all-start.3 = ((bf16[128,8,704]{0,2,1:T(8,128)(2,1)}), bf16[128,8,704]{0,2,1:T(8,128)(2,1)}, u32[]{:S(2)}, u32[]{:S(2)}) async-start(bf16[128,8,704]{0,2,1:T(8,128)(2,1)} %bitcast.411), calls=%async_computation.3 | async-start | bytes 2883584 | tf_op jit(solution)/shard_map/all_to_all | solution.py:221
  928.6 30.8 %all-to-all-start.1 = ((bf16[128,8,512]{2,0,1:T(8,128)(2,1)}), bf16[128,8,512]{2,0,1:T(8,128)(2,1)}, u32[]{:S(2)}, u32[]{:S(2)}) async-start(bf16[128,8,512]{2,0,1:T(8,128)(2,1)} %bitcast.415), calls=%async_computation.1 | async-start | bytes 2097152 | tf_op jit(solution)/shard_map/all_to_all | solution.py:220
  932.9 248.1 %all-reduce.22.cloned.1.call-start = ((), (), s32[]{:S(2)}) async-start(), calls=%async_computation.12 | async-start | bytes 786432 | tf_op jit(solution)/shard_map/psum | solution.py:285
  959.3 13.6 all-to-all-start.2
  973.0 20.0 %all-to-all-start = ((bf16[128,8,256]{2,0,1:T(8,128)(2,1)}), bf16[128,8,256]{2,0,1:T(8,128)(2,1)S(1)}, u32[]{:S(2)}, u32[]{:S(2)}) async-start(bf16[128,8,256]{2,0,1:T(8,128)(2,1)} %copy.555), calls=%async_computation | async-start | bytes 1048576 | tf_op jit(solution)/shard_map/all_to_all | solution.py:218
  976.5 781.7 %all-reduce.24.cloned.1.call-start = ((), (), s32[]{:S(2)}) async-start(), calls=%async_computation.13 | async-start | bytes 34078720 | tf_op jit(solution)/shard_map/psum | solution.py:283
  1067.0 12.2 copy-start.110
  1079.2 23.5 %copy-start.62 = (bf16[2048,32]{0,1:T(8,128)(2,1)S(1)}, bf16[2048,32]{0,1:T(8,128)(2,1)}, u32[]{:S(2)}) copy-start(bf16[2048,32]{0,1:T(8,128)(2,1)} %copy-done.61) | copy-start | bytes 393220
  1079.2 23.5 %copy-start.98 = (f32[128]{0:T(128)S(1)}, f32[128]{0:T(128)}, u32[]{:S(2)}) copy-start(f32[128]{0:T(128)} %copy-done.96) | copy-start | bytes 1540
  1102.8 43.8 %copy-start.113 = (f32[128]{0:T(128)S(1)}, f32[128]{0:T(128)}, u32[]{:S(2)}) copy-start(f32[128]{0:T(128)} %copy-done.112) | copy-start | bytes 1540
  1102.8 43.8 %copy-start.39 = (bf16[2,64,2048]{2,1,0:T(8,128)(2,1)S(1)}, bf16[2,64,2048]{2,1,0:T(8,128)(2,1)}, u32[]{:S(2)}) copy-start(bf16[2,64,2048]{2,1,0:T(8,128)(2,1)} %param.16) | copy-start | bytes 1572868
  1102.8 43.8 %copy-start.42 = (f32[128,2048]{1,0:T(8,128)S(1)}, f32[128,2048]{1,0:T(8,128)}, u32[]{:S(2)}) copy-start(f32[128,2048]{1,0:T(8,128)} %get-tuple-element.668) | copy-start | bytes 3145732
  1102.8 43.8 %copy-start.55 = (bf16[2,64,2048]{2,1,0:T(8,128)(2,1)S(1)}, bf16[2,64,2048]{2,1,0:T(8,128)(2,1)}, u32[]{:S(2)}) copy-start(bf16[2,64,2048]{2,1,0:T(8,128)(2,1)} %param.17) | copy-start | bytes 1572868
  1102.8 43.8 %copy-start.74 = (f32[1,2048]{1,0:T(1,128)S(1)}, f32[1,2048]{1,0:T(1,128)}, u32[]{:S(2)}) copy-start(f32[1,2048]{1,0:T(1,128)} %copy-done.73) | copy-start | bytes 24580
  1102.8 43.8 %copy-start.95 = (f32[128]{0:T(128)S(1)}, f32[128]{0:T(128)}, u32[]{:S(2)}) copy-start(f32[128]{0:T(128)} %copy-done.94) | copy-start | bytes 1540
  1102.8 43.8 %copy-start.106 = (f32[128]{0:T(128)S(1)}, f32[128]{0:T(128)}, u32[]{:S(2)}) copy-start(f32[128]{0:T(128)} %copy-done.105) | copy-start | bytes 1540
  (88 other events, 291.4 us)
Sparse Core Ops, SparseCore 0:
  9.6 75.8 all-gather.8
  87.0 31.2 all-gather.10
  119.8 69.9 all-gather.12
  191.2 39.0 all-gather.14
  349.8 53.9 all-gather.22
  507.0 40.4 all-gather.18
  549.3 212.3 all-gather.20
  891.8 156.7 all-gather.16
  1054.0 126.9 all-reduce.21
  1185.1 573.0 all-reduce.23
where the time goes:
time: 1790 us
  waiting for transfers between devices  1130 us (63%)
  matrix products  293 us (16%)
  other arithmetic  184 us (10%)
  local copies, waits for them, and re-layouts  73.7 us (4%)
  blocking collectives  45.4 us (3%)
  starting transfers between devices  41.9 us (2%)
    psum x1, waiting for transfers between devices, body(): lax.psum(summed[3].astype(jnp.bfloat16), 'replica').astype(jnp.float32)  575 us
    ppermute x8, waiting for transfers between devices, shifted(): lax.ppermute(value, axis, [(source, source + steps) for source in range(l...  364 us
    another operation x5, other arithmetic, block_step(): lax.linalg.triangular_solve(system, target, left_side=True, lower=True, u...  77.3 us
    all_gather x1, waiting for transfers between devices, gather_mixer(): lax.all_gather(w_in, 'shard', axis=0, tiled=True)  66.9 us
    all_gather x1, waiting for transfers between devices, body(): lax.all_gather(proj_grad, ('shard', 'seq'), axis=0, tiled=True)  55.7 us
    psum x1, blocking collectives, body(): lax.psum((small_sums[0], small_sums[1], small_sums[2], small_sums[3], sma...  39.7 us
  transfers between devices with their start and end apart: 22, of which 15 were waited for; matrix products, arithmetic and copies ran while one was open for 29% of the time, Pallas kernels for 0%

commit v1 on v0

v1 whole, which is shorter than its diff:
```python
import functools

import jax
import jax.numpy as jnp
from jax import lax
from jax.experimental import pallas as pl
from jax.experimental.pallas import tpu as pltpu
from jax.sharding import PartitionSpec as P

D = 2048
HEADS = 16
DK = 128
DV = 256
FF = 5632
KERNEL = 4
KD = 2048
VD = 4096
CONVW = 8192
PROJW = 12288
EPS = 1e-06
HIGHEST = lax.Precision.HIGHEST
LOWEST_DECAY = -104.0
F32 = jnp.float32
BF16 = jnp.bfloat16
EVERY = ("shard", "seq", "replica")
GROUP = ("shard", "seq")


def mm(left, right, dims=((1,), (0,))):
    return lax.dot_general(
        left.astype(BF16), right.astype(BF16), (dims, ((), ())), preferred_element_type=F32
    )


def split(value):
    high = value.astype(BF16)
    return high, (value - high.astype(F32)).astype(BF16)


def mm3(left, right, dims=((1,), (0,))):
    left_high, left_low = split(left)
    right_high, right_low = split(right)
    return (
        mm(left_high, right_high, dims)
        + mm(left_high, right_low, dims)
        + mm(left_low, right_high, dims)
    )


ROWS_ROWS = ((1,), (1,))
COLS_COLS = ((0,), (0,))


def delayed(value, steps, rows):
    if steps == 0:
        return value
    return jnp.where(rows >= steps, pltpu.roll(value, steps, 0), 0.0)


def advanced(value, steps, rows):
    if steps == 0:
        return value
    length = value.shape[0]
    return jnp.where(rows < length - steps, pltpu.roll(value, length - steps, 0), 0.0)


def in_order(ref, place):
    pieces = ref.shape[0]
    return jnp.concatenate([ref[jnp.bitwise_xor(place, j), 0] for j in range(pieces)], 0)


def put_back(ref, place, value):
    pieces = ref.shape[0]
    width = value.shape[0] // pieces
    for j in range(pieces):
        ref[jnp.bitwise_xor(place, j), 0] = value[j * width : (j + 1) * width].astype(ref.dtype)


def convolved(source, taps, rows):
    mixed = taps[KERNEL - 1 : KERNEL] * source
    for offset in range(KERNEL - 1):
        mixed = mixed + taps[offset : offset + 1] * delayed(source, KERNEL - 1 - offset, rows)
    return mixed


def unit(value):
    scale = lax.rsqrt(jnp.sum(value * value, -1, keepdims=True) + EPS)
    return value * scale, scale


def decay_matrices(rates):
    length = rates.shape[1]
    row_ids = lax.broadcasted_iota(jnp.int32, (length, length), 0)
    col_ids = lax.broadcasted_iota(jnp.int32, (length, length), 1)
    decay_row = rates[0:1]
    rate_row = rates[1:2]
    diagonal = row_ids == col_ids
    running = jnp.sum(jnp.where(row_ids >= col_ids, decay_row, 0.0), 1, keepdims=True)
    running_row = jnp.sum(jnp.where(diagonal, running, 0.0), 0, keepdims=True)
    rate = jnp.sum(jnp.where(diagonal, rate_row, 0.0), 1, keepdims=True)
    spread = jnp.minimum(running - running_row, 0.0)
    weight = jnp.where(row_ids >= col_ids, jnp.exp(spread), 0.0)
    return row_ids, col_ids, rate, weight


def lower_inverse(system, row_ids, col_ids):
    length = system.shape[0]
    eye = (row_ids == col_ids).astype(F32)
    same = jnp.bitwise_xor(row_ids, col_ids)
    inverse = eye - jnp.where(same < 2, system, 0.0)
    size = 2
    while size < length:
        between = jnp.where((same >= size) & (same < 2 * size), system, 0.0)
        inverse = inverse - mm3(inverse, mm3(between, inverse))
        size *= 2
    return inverse


def head_inputs(place, q_ref, k_ref, v_ref, taps_q, taps_k, taps_v, rates_ref):
    raw = tuple(in_order(ref, place).astype(BF16).astype(F32) for ref in (q_ref, k_ref, v_ref))
    rows = lax.broadcasted_iota(jnp.int32, (raw[0].shape[0], 1), 0)
    mixed = tuple(
        convolved(source, taps[...].astype(F32), rows)
        for source, taps in zip(raw, (taps_q, taps_k, taps_v))
    )
    slopes = tuple(jax.nn.sigmoid(item) for item in mixed)
    query_unit, query_scale = unit(mixed[0] * slopes[0])
    key_rows, key_scale = unit(mixed[1] * slopes[1])
    values = mixed[2] * slopes[2]
    queries = query_unit * DK ** (-0.5)
    return raw, rows, mixed, slopes, queries, key_rows, values, query_unit, query_scale, key_scale


def forward_kernel(
    place_ref, q_ref, k_ref, v_ref, g_ref, taps_q, taps_k, taps_v, rates_ref, gain_ref,
    gated_ref, inverse_ref, update_ref,
):
    place = place_ref[0]
    items = head_inputs(place, q_ref, k_ref, v_ref, taps_q, taps_k, taps_v, rates_ref)
    queries, key_rows, values = items[4:7]
    row_ids, col_ids, rate, weight = decay_matrices(rates_ref[0, 0])
    system = jnp.where(
        row_ids > col_ids, rate * mm3(key_rows, key_rows, ROWS_ROWS) * weight, 0.0
    )
    inverse = lower_inverse(system, row_ids, col_ids)
    update = mm3(inverse, rate * values)
    scores = mm(queries, key_rows, ROWS_ROWS) * weight
    outputs = mm(scores, update)
    scaled = (
        outputs
        * lax.rsqrt(jnp.mean(outputs * outputs, -1, keepdims=True) + EPS)
        * gain_ref[...]
    )
    gate = in_order(g_ref, place)
    put_back(gated_ref, place, scaled * (gate * jax.nn.sigmoid(gate)))
    inverse_ref[0, 0] = inverse
    update_ref[0, 0] = update


def unit_back(grad, direction, scale):
    return scale * (grad - direction * jnp.sum(grad * direction, -1, keepdims=True))


def backward_kernel(
    place_ref, q_ref, k_ref, v_ref, g_ref, taps_q, taps_k, taps_v, rates_ref, gain_ref,
    inverse_ref, update_ref, grad_ref,
    dq_ref, dk_ref, dv_ref, dg_ref, small_ref,
):
    place = place_ref[0]
    raw, rows, mixed, slopes, queries, key_rows, values, query_unit, query_scale, key_scale = (
        head_inputs(place, q_ref, k_ref, v_ref, taps_q, taps_k, taps_v, rates_ref)
    )
    row_ids, col_ids, rate, weight = decay_matrices(rates_ref[0, 0])
    inner = mm3(key_rows, key_rows, ROWS_ROWS)
    strict = row_ids > col_ids
    keyed = jnp.where(strict, inner * weight, 0.0)
    scores = mm(queries, key_rows, ROWS_ROWS) * weight
    inverse = inverse_ref[0, 0]
    update = update_ref[0, 0]
    outputs = mm(scores, update)
    gate = in_order(g_ref, place)
    upstream = in_order(grad_ref, place).astype(F32)
    gate_slope = jax.nn.sigmoid(gate)
    out_scale = lax.rsqrt(jnp.mean(outputs * outputs, -1, keepdims=True) + EPS)
    out_unit = outputs * out_scale
    gain = gain_ref[...]
    scaled_grad = upstream * (gate * gate_slope)
    put_back(
        dg_ref, place, upstream * out_unit * gain * (gate_slope * (1.0 + gate * (1.0 - gate_slope)))
    )
    gain_grad = jnp.sum(scaled_grad * out_unit, 0, keepdims=True)
    unit_grad = scaled_grad * gain
    out_grad = out_scale * (
        unit_grad - out_unit * jnp.mean(unit_grad * out_unit, -1, keepdims=True)
    )
    scores_grad = jnp.where(row_ids >= col_ids, mm(out_grad, update, ROWS_ROWS), 0.0)
    update_grad = mm(scores, out_grad, COLS_COLS)
    target_grad = mm3(inverse, update_grad, COLS_COLS)
    system_grad = jnp.where(strict, -mm(target_grad, update, ROWS_ROWS), 0.0)
    value_grad = rate * target_grad
    keyed_grad = system_grad * keyed
    rate_grad = jnp.sum(target_grad * values, 1, keepdims=True) + jnp.sum(
        keyed_grad, 1, keepdims=True
    )
    spread_grad = keyed_grad * rate + scores_grad * scores
    inner_grad = system_grad * weight * rate
    raw_scores_grad = scores_grad * weight
    query_grad = mm(raw_scores_grad, key_rows) * DK ** (-0.5)
    key_grad = (
        mm(raw_scores_grad, queries, COLS_COLS)
        + mm(inner_grad, key_rows)
        + mm(inner_grad, key_rows, COLS_COLS)
    )
    diagonal = row_ids == col_ids
    column_sum = jnp.sum(spread_grad, 0, keepdims=True)
    running_grad = jnp.sum(spread_grad, 1, keepdims=True) - jnp.sum(
        jnp.where(diagonal, column_sum, 0.0), 1, keepdims=True
    )
    decay_grad = jnp.sum(jnp.where(row_ids >= col_ids, running_grad, 0.0), 0, keepdims=True)
    rate_grad_row = jnp.sum(jnp.where(diagonal, rate_grad, 0.0), 0, keepdims=True)
    active_grads = (
        unit_back(query_grad, query_unit, query_scale),
        unit_back(key_grad, key_rows, key_scale),
        value_grad,
    )
    starts = (0, DK, 2 * DK)
    small_ref[...] = jnp.zeros_like(small_ref)
    for at, grad_out, source, before, slope, taps, out_ref in zip(
        starts, active_grads, raw, mixed, slopes, (taps_q, taps_k, taps_v), (dq_ref, dk_ref, dv_ref)
    ):
        mixed_grad = grad_out * (slope * (1.0 + before * (1.0 - slope)))
        kernel = taps[...].astype(F32)
        width = source.shape[1]
        total = kernel[KERNEL - 1 : KERNEL] * mixed_grad
        for offset in range(KERNEL):
            steps = KERNEL - 1 - offset
            if steps:
                total = total + kernel[offset : offset + 1] * advanced(mixed_grad, steps, rows)
            small_ref[0, 0, offset : offset + 1, at : at + width] = jnp.sum(
                mixed_grad * delayed(source, steps, rows), 0, keepdims=True
            )
        put_back(out_ref, place, total)
    small_ref[0, 0, 4:5, 0:DV] = gain_grad
    length = decay_grad.shape[1]
    small_ref[0, 0, 5:6, 0:length] = decay_grad
    small_ref[0, 0, 6:7, 0:length] = rate_grad_row


def mixer_specs(pieces, row, heads, length):
    def piece(width, shift):
        return pl.BlockSpec((pieces, 1, row, width), lambda b, h, place: (0, b, 0, h + shift))

    def taps(width, shift):
        return pl.BlockSpec((KERNEL, width), lambda b, h, place: (0, h + shift))

    proj = [piece(DK, 0), piece(DK, heads), piece(DV, heads), piece(DV, 2 * heads)]
    kernel = [taps(DK, 0), taps(DK, heads), taps(DV, heads)]
    rates = pl.BlockSpec((1, 1, 8, length), lambda b, h, place: (b, h, 0, 0))
    gain = pl.BlockSpec((1, DV), lambda b, h, place: (0, 0))
    square = pl.BlockSpec((1, 1, length, length), lambda b, h, place: (b, h, 0, 0))
    return piece, proj, kernel, rates, gain, square


VMEM_LIMIT = 40 * 1024 * 1024


def mixer_forward(place, projected, taps, rates, gain):
    pieces, micro, row, _ = projected.shape
    heads, length = rates.shape[1], rates.shape[3]
    piece, proj, kernel, rate_spec, gain_spec, square = mixer_specs(pieces, row, heads, length)
    return pl.pallas_call(
        forward_kernel,
        grid_spec=pltpu.PrefetchScalarGridSpec(
            num_scalar_prefetch=1,
            grid=(micro, heads),
            in_specs=proj + kernel + [rate_spec, gain_spec],
            out_specs=[piece(DV, 0), square, square],
        ),
        out_shape=[
            jax.ShapeDtypeStruct((pieces, micro, row, heads * DV), BF16),
            jax.ShapeDtypeStruct((micro, heads, length, length), F32),
            jax.ShapeDtypeStruct((micro, heads, length, DV), F32),
        ],
        compiler_params=pltpu.CompilerParams(vmem_limit_bytes=VMEM_LIMIT),
    )(place, projected, projected, projected, projected, taps, taps, taps, rates, gain)


def mixer_backward(place, projected, taps, rates, gain, inverse, update, grad):
    pieces, micro, row, _ = projected.shape
    heads, length = rates.shape[1], rates.shape[3]
    piece, proj, kernel, rate_spec, gain_spec, square = mixer_specs(pieces, row, heads, length)
    small = pl.BlockSpec((1, 1, 8, 2 * DK + DV), lambda b, h, place: (b, h, 0, 0))

    def out(width):
        return jax.ShapeDtypeStruct((pieces, micro, row, heads * width), BF16)

    return pl.pallas_call(
        backward_kernel,
        grid_spec=pltpu.PrefetchScalarGridSpec(
            num_scalar_prefetch=1,
            grid=(micro, heads),
            in_specs=proj + kernel + [rate_spec, gain_spec, square, square, piece(DV, 0)],
            out_specs=[piece(DK, 0), piece(DK, 0), piece(DV, 0), piece(DV, 0), small],
        ),
        out_shape=[
            out(DK),
            out(DK),
            out(DV),
            out(DV),
            jax.ShapeDtypeStruct((micro, heads, 8, 2 * DK + DV), F32),
        ],
        compiler_params=pltpu.CompilerParams(vmem_limit_bytes=VMEM_LIMIT),
    )(
        place, projected, projected, projected, projected, taps, taps, taps, rates, gain,
        inverse, update, grad,
    )


def swapped(value, axis, step):
    count = lax.axis_size(axis)
    return lax.ppermute(value, axis, [(source, source ^ step) for source in range(count)])


def around(value, axis):
    return [value] + [swapped(value, axis, step) for step in range(1, lax.axis_size(axis))]


def settled(parts, index):
    stacked = jnp.stack(parts)
    return [
        lax.dynamic_index_in_dim(stacked, jnp.bitwise_xor(index, at), 0, keepdims=False)
        for at in range(len(parts))
    ]


def part_of(value, index, count, axis):
    width = value.shape[axis] // count
    return lax.dynamic_slice_in_dim(value, index * width, width, axis)


def dot(left, right):
    return jnp.dot(left, right, preferred_element_type=F32)


def dot_rows(left, right):
    return lax.dot_general(left, right, (((1,), (1,)), ((), ())), preferred_element_type=F32)


def dot_cols(left, right):
    return lax.dot_general(left, right, (((0,), (0,)), ((), ())), preferred_element_type=F32)


def rms_parts(values):
    return lax.rsqrt(jnp.mean(values * values, -1, keepdims=True) + EPS)


def rms_back(values, scale, gain, grad):
    weighted = grad * gain
    unit_rows = values * scale
    inner = jnp.mean(weighted * unit_rows, -1, keepdims=True)
    return scale * (weighted - unit_rows * inner), jnp.sum(grad * unit_rows, 0)


def body(
    tokens,
    cotangent,
    lengths,
    norm_gains,
    w_in,
    w_ab,
    conv_weight,
    gate_params,
    onorm_gain,
    w_o,
    w_gu,
    w_down,
):
    shards, seqs, replicas = (lax.axis_size(name) for name in EVERY)
    shard, seq = lax.axis_index("shard"), lax.axis_index("seq")
    owners = shards * seqs
    owner = shard * seqs + seq
    micro, row = tokens.shape[0], tokens.shape[1]
    flat = micro * row
    length = row * seqs
    heads = HEADS // seqs
    depth = D // shards
    key_width, value_width = heads * DK, heads * DV
    place = jnp.reshape(seq, (1,)).astype(jnp.int32)

    def blocks(value, count, axis=1):
        return [part_of(value, jnp.bitwise_xor(shard, step), count, axis) for step in range(count)]

    small = jnp.concatenate([norm_gains.reshape(-1), conv_weight.reshape(-1), w_ab.reshape(-1)])
    small = lax.all_gather(small, "shard")
    cuts = (norm_gains.size, norm_gains.size + conv_weight.size)
    gains = jnp.swapaxes(small[:, : cuts[0]].reshape(shards, 2, depth), 0, 1).reshape(2, D)
    gains = gains.astype(F32)
    taps_full = jnp.swapaxes(small[:, cuts[0] : cuts[1]].reshape(shards, KERNEL, -1), 0, 1)
    taps_full = taps_full.reshape(KERNEL, CONVW)
    ab_full = small[:, cuts[1] :].reshape(D, 2 * HEADS)

    def head_columns(value):
        return [
            part_of(value[..., :KD], seq, seqs, value.ndim - 1),
            part_of(value[..., KD : 2 * KD], seq, seqs, value.ndim - 1),
            part_of(value[..., 2 * KD : CONVW], seq, seqs, value.ndim - 1),
        ]

    in_own = jnp.concatenate(head_columns(w_in) + [part_of(w_in[:, CONVW:], seq, seqs, 1)], 1)
    in_parts = around(in_own, "shard")
    taps = jnp.concatenate(head_columns(taps_full), 1).astype(F32)
    out_parts = around(w_o, "shard")
    ff_shard = FF // shards

    def gate_up_columns(index):
        return jnp.concatenate(
            [part_of(w_gu[:, :FF], index, shards, 1), part_of(w_gu[:, FF:], index, shards, 1)], 1
        )

    gu_parts = [gate_up_columns(shard)] + [
        swapped(gate_up_columns(jnp.bitwise_xor(shard, step)), "shard", step)
        for step in range(1, shards)
    ]

    pieces = jnp.stack(around(tokens, "seq"))
    flat_all = pieces.reshape(seqs * flat, D).astype(F32)
    normed = (flat_all * rms_parts(flat_all) * gains[0]).astype(BF16)
    projected = sum(dot(left, right) for left, right in zip(blocks(normed, shards), in_parts))
    projected = projected.reshape(seqs, micro, row, -1)
    rate_in = dot(normed, ab_full).reshape(seqs, micro, row, 2, HEADS)
    rate_in = part_of(rate_in, seq, seqs, 4)
    rate_in = jnp.stack(settled(list(rate_in), seq))
    rate_in = jnp.transpose(rate_in, (3, 1, 4, 0, 2)).reshape(2, micro, heads, length)
    position = jnp.arange(length, dtype=jnp.int32)
    valid = (position[None, :] < lengths[:, None]).astype(F32)[:, None, :]
    own_params = part_of(gate_params, seq, seqs, 1)[:, None, :, None]
    rate_shifted = rate_in[0] + own_params[1]
    decays = -jnp.exp(own_params[0]) * jax.nn.softplus(rate_shifted) * valid
    written = jax.nn.sigmoid(rate_in[1])
    rates = jnp.stack([jnp.maximum(decays, LOWEST_DECAY), written * valid], 2)
    rates = jnp.pad(rates, ((0, 0), (0, 0), (0, 6), (0, 0)))
    gain_row = onorm_gain.reshape(1, DV)
    gated, inverse, update = mixer_forward(place, projected, taps, rates, gain_row)

    mixed_parts = [gated[0]] + [swapped(gated[step], "seq", step) for step in range(1, seqs)]
    mixed_in = jnp.concatenate(settled(mixed_parts, seq), -1).reshape(flat, VD)
    flat_in = tokens.reshape(flat, D).astype(F32)
    middle = flat_in + sum(
        dot(left, right) for left, right in zip(blocks(mixed_in, shards), out_parts)
    )
    middle_scale = rms_parts(middle)
    renormed = (middle * middle_scale * gains[1]).astype(BF16)

    upstream = cotangent.reshape(flat, D)
    pair_up = jnp.concatenate(around(upstream, "shard"), 0)
    hidden_grad = dot_rows(pair_up, w_down)
    pair_renormed = jnp.concatenate(around(renormed, "shard"), 0)
    gate_up = sum(dot(left, right) for left, right in zip(blocks(pair_renormed, shards), gu_parts))

    def feed_forward(gate_up_rows, grad_rows):
        width = gate_up_rows.shape[1] // 2
        gate, up = gate_up_rows[:, :width], gate_up_rows[:, width:]
        slope = jax.nn.sigmoid(gate)
        hidden_rows = (gate * slope * up).astype(BF16)
        gate_grad = grad_rows * up * (slope * (1.0 + gate * (1.0 - slope)))
        return hidden_rows, gate_grad.astype(BF16), (grad_rows * gate * slope).astype(BF16)

    hidden, gate_grad, up_grad = feed_forward(gate_up, hidden_grad)
    gate_up_grad = jnp.concatenate([gate_grad, up_grad], 1)

    def scattered(parts):
        return parts[0] + sum(
            swapped(parts[step], "shard", step) for step in range(1, len(parts))
        )

    column_parts = [dot_rows(gate_up_grad, part).reshape(shards, flat, depth) for part in gu_parts]
    rows_for = [
        jnp.concatenate([column_parts[step ^ at][step] for at in range(shards)], 1)
        for step in range(shards)
    ]
    renormed_grad = scattered(rows_for)
    renormed_grad = jnp.concatenate(
        settled([renormed_grad[:, at * depth : (at + 1) * depth] for at in range(shards)], shard), 1
    )
    middle_grad, gain2_grad = rms_back(middle, middle_scale, gains[1], renormed_grad)
    middle_grad = middle_grad + upstream.astype(F32)
    mixed_grad = middle_grad.astype(BF16)
    down_rows = dot(hidden, w_down).reshape(shards, flat, D)
    result = middle + scattered(list(down_rows))
    results = result.astype(BF16).reshape(micro, row, D)

    gated_grad = [dot_rows(mixed_grad, part).astype(BF16) for part in out_parts]
    gated_grad = jnp.concatenate(settled(gated_grad, shard), 1)
    grad_parts = [
        swapped(part_of(gated_grad, jnp.bitwise_xor(seq, step), seqs, 1), "seq", step)
        if step
        else part_of(gated_grad, seq, seqs, 1)
        for step in range(seqs)
    ]
    grad_parts = jnp.stack(grad_parts).reshape(seqs, micro, row, value_width)
    dq, dk, dv, dg, small_grad = mixer_backward(
        place, projected, taps, rates, gain_row, inverse, update, grad_parts
    )
    rows_all = seqs * flat
    types = [item.reshape(rows_all, -1) for item in (dq, dk, dv, dg)]
    proj_grad = jnp.concatenate(types, 1)
    decay_grad = small_grad[:, :, 5, :length]
    write_grad = small_grad[:, :, 6, :length]
    shifted_grad = decay_grad * -jnp.exp(own_params[0]) * jax.nn.sigmoid(rate_shifted) * valid
    params_grad = jnp.stack(
        [jnp.sum(decay_grad * decays, (0, 2)), jnp.sum(shifted_grad, (0, 2))]
    )
    rate_grad = jnp.stack([shifted_grad, write_grad * written * (1.0 - written) * valid])
    rate_grad = jnp.transpose(rate_grad.reshape(2, micro, heads, seqs, row), (3, 1, 4, 0, 2))
    rate_grad = jnp.stack(settled(list(rate_grad), seq))
    wide_rates = jnp.zeros((seqs, micro, row, 2, HEADS), F32)
    wide_rates = lax.dynamic_update_slice_in_dim(wide_rates, rate_grad, seq * heads, 4)
    wide_rates = wide_rates.reshape(rows_all, 2 * HEADS)
    grad_ab = lax.dot_general(
        normed.astype(F32), wide_rates, (((0,), (0,)), ((), ())), precision=HIGHEST
    )
    ab_blocks = blocks(ab_full.astype(F32), shards, 0)
    normed_grad = [
        dot_rows(proj_grad, part)
        + lax.dot_general(wide_rates, ab, (((1,), (1,)), ((), ())), precision=HIGHEST)
        for part, ab in zip(in_parts, ab_blocks)
    ]
    normed_grad = jnp.concatenate(settled(normed_grad, shard), 1).reshape(seqs, flat, D)
    normed_grad = normed_grad[0] + sum(
        swapped(normed_grad[step].astype(BF16), "seq", step).astype(F32)
        for step in range(1, seqs)
    )
    inputs_grad, gain1_grad = rms_back(flat_in, rms_parts(flat_in), gains[0], normed_grad)
    input_grads = (inputs_grad + middle_grad).astype(BF16).reshape(micro, row, D)

    def type_part(index):
        return jnp.concatenate([part_of(item, index, shards, 1) for item in types], 1)

    pair_proj = jnp.concatenate(
        [type_part(shard)]
        + [
            swapped(type_part(jnp.bitwise_xor(shard, step)), "shard", step)
            for step in range(1, shards)
        ],
        0,
    )
    pair_normed = jnp.concatenate(around(normed, "shard"), 0)
    grad_in = dot_cols(pair_normed, pair_proj).astype(BF16)
    width = grad_in.shape[1]
    slice_rows = D // (owners * replicas)
    grad_in = grad_in.reshape(owners, replicas, slice_rows, width)
    grad_in = jnp.swapaxes(grad_in, 0, 1).reshape(replicas, owners * slice_rows, width)
    grad_in = lax.psum_scatter(grad_in, "replica", scatter_dimension=0, tiled=False)
    grad_in = lax.all_to_all(
        grad_in.reshape(owners, slice_rows, width), GROUP, split_axis=0, concat_axis=0, tiled=False
    )
    grad_in = lax.all_gather(grad_in, "replica", axis=0)
    grad_in = grad_in.reshape(replicas, shards, seqs, slice_rows, width)
    grad_in = jnp.transpose(grad_in, (0, 3, 2, 1, 4)).reshape(D // owners, seqs, shards, width)
    key_part, value_part = key_width // shards, value_width // shards
    edges = (0, key_part, 2 * key_part, 2 * key_part + value_part, width)
    grad_in = jnp.concatenate(
        [
            grad_in[..., low:high].reshape(D // owners, -1)
            for low, high in zip(edges[:-1], edges[1:])
        ],
        1,
    ).astype(F32)

    mixed_own = lax.all_to_all(mixed_in, GROUP, split_axis=1, concat_axis=0, tiled=True)
    mid_piece = lax.all_gather(mixed_grad, GROUP, axis=0, tiled=True)
    grad_out = lax.psum(dot_cols(mixed_own, mid_piece).astype(BF16), "replica").astype(F32)

    all_up = lax.all_gather(upstream, EVERY, axis=0, tiled=True)
    all_renormed = lax.all_gather(renormed, EVERY, axis=0, tiled=True)
    own_down = part_of(w_down, seq, seqs, 0)
    own_gu = [
        jnp.concatenate(
            [part_of(part[:, :ff_shard], seq, seqs, 1), part_of(part[:, ff_shard:], seq, seqs, 1)],
            1,
        )
        for part in gu_parts
    ]
    own_hidden_grad = dot_rows(all_up, own_down)
    own_gate_up = sum(
        dot(left, right) for left, right in zip(blocks(all_renormed, shards), own_gu)
    )
    own_hidden, own_gate_grad, own_up_grad = feed_forward(own_gate_up, own_hidden_grad)
    grad_down = dot_cols(own_hidden, all_up)
    grad_gu = jnp.concatenate(
        [dot_cols(all_renormed, own_gate_grad), dot_cols(all_renormed, own_up_grad)], 1
    ).astype(BF16)
    grad_gu = lax.all_to_all(
        grad_gu.reshape(owners, D // owners, 2 * (FF // owners)),
        GROUP,
        split_axis=0,
        concat_axis=0,
        tiled=False,
    )
    grad_gu = jnp.transpose(
        grad_gu.reshape(owners, D // owners, 2, FF // owners), (1, 2, 0, 3)
    ).reshape(D // owners, 2 * FF).astype(F32)

    taps_grad = jnp.sum(small_grad[:, :, :KERNEL], 0)
    conv_grad = jnp.zeros((KERNEL, CONVW), F32)
    for low, high, start in ((0, DK, 0), (DK, 2 * DK, KD), (2 * DK, 2 * DK + DV, 2 * KD)):
        rows_in = jnp.swapaxes(taps_grad[..., low:high], 0, 1).reshape(KERNEL, -1)
        conv_grad = lax.dynamic_update_slice_in_dim(
            conv_grad, rows_in, start + seq * rows_in.shape[1], 1
        )
    onorm_grad = jnp.sum(small_grad[:, :, 4, :DV], (0, 1))
    wide_params = lax.dynamic_update_slice_in_dim(
        jnp.zeros((2, HEADS), F32), params_grad, seq * heads, 1
    )
    params_total, onorm_total, gains_total, conv_total, ab_total = lax.psum(
        (wide_params, onorm_grad, jnp.stack([gain1_grad, gain2_grad]), conv_grad, grad_ab), EVERY
    )
    gains_own = part_of(gains_total, owner, owners, 1)
    ab_own = part_of(ab_total, owner, owners, 0)
    conv_own = part_of(conv_total, owner, owners, 1)
    return (
        results,
        input_grads,
        gains_own,
        grad_in,
        ab_own,
        conv_own,
        params_total,
        onorm_total,
        grad_out,
        grad_gu,
        grad_down,
    )


def solution(mesh):
    in_specs = (
        P(("shard", "replica"), "seq", None),
        P(("shard", "replica"), "seq", None),
        P(("shard", "replica")),
        P(None, "shard"),
        P("shard", None),
        P("shard", None),
        P(None, "shard"),
        P(),
        P(),
        P("shard", None),
        P("shard", None),
        P("shard", None),
    )
    out_specs = (
        P(("shard", "replica"), "seq", None),
        P(("shard", "replica"), "seq", None),
        P(None, ("shard", "seq")),
        P(("shard", "seq"), None),
        P(("shard", "seq"), None),
        P(None, ("shard", "seq")),
        P(),
        P(),
        P(("shard", "seq"), None),
        P(("shard", "seq"), None),
        P(("shard", "seq"), None),
    )
    return jax.shard_map(body, mesh=mesh, in_specs=in_specs, out_specs=out_specs, check_vma=False)
```

time: 1790 us -> 1200 us (0.67)
  waiting for transfers between devices: 1130 us -> 527 us
  other arithmetic: 184 us -> 74.6 us
  local copies, waits for them, and re-layouts: 73.7 us -> 155 us
  Pallas kernels: 0 us -> 67.1 us
  matrix products: 293 us -> 249 us
  blocking collectives: 45.4 us -> 77.3 us
    psum x2, waiting for transfers between devices: 606 us -> 81.1 us  [the longest x1 44 us: body(): lax.psum((wide_params, onorm_grad, jnp.stack([gain1_grad, gain2_grad]), c...]
    ppermute x8 -> x21, waiting for transfers between devices: 364 us -> 48.2 us  [swapped(): lax.ppermute(value, axis, [(source, source ^ step) for source in range(co...]
    all_gather x8 -> x4, waiting for transfers between devices: 123 us -> 268 us  [the longest x1 113 us: body(): all_up = lax.all_gather(upstream, EVERY, axis=0, tiled=True)]
    another operation x9 -> x6, other arithmetic: 82.8 us -> 1.93 us  [the longest x1 1.24 us: settled(): stacked = jnp.stack(parts)]
    reduce_scatter x0 -> x1, waiting for transfers between devices: none -> 74.5 us  [body(): lax.psum_scatter(grad_in, 'replica', scatter_dimension=0, tiled=False)]
    pallas_call x0 -> x2, Pallas kernels: none -> 67.1 us  [the longest x1 46.6 us: mixer_forward(): pl.pallas_call(forward_kernel, grid_spec=pltpu.PrefetchScalarGridSpec(num...]
    slice x9 -> x21, local copies, waits for them, and re-layouts: 2.75 us -> 54 us  [the longest x6 16.3 us: body(): grad_in[..., low:high].reshape(D // owners, -1)]
    dynamic_slice x3 -> x18, local copies, waits for them, and re-layouts: 3.27 us -> 37.4 us  [the longest x16 37.3 us: part_of(): return lax.dynamic_slice_in_dim(value, index * width, width, axis)]
  transfers between devices with their start and end apart: 22 -> 30, of which waited for: 15 -> 17; matrix products, arithmetic and copies ran while one was open for 29% -> 27% of each run, Pallas kernels for 0% -> 6%
where the time goes in v1:
time: 1200 us
  waiting for transfers between devices  527 us (44%)
  matrix products  249 us (21%)
  local copies, waits for them, and re-layouts  155 us (13%)
  blocking collectives  77.3 us (6%)
  other arithmetic  74.6 us (6%)
  Pallas kernels  67.1 us (6%)
  starting transfers between devices  26.9 us (2%)
  between operations  17.5 us (1%)
    all_gather x1, waiting for transfers between devices, body(): all_up = lax.all_gather(upstream, EVERY, axis=0, tiled=True)  113 us
    all_gather x1, waiting for transfers between devices, body(): grad_in = lax.all_gather(grad_in, 'replica', axis=0)  95.9 us
    dot_general x10, matrix products, dot(): return jnp.dot(left, right, preferred_element_type=F32)  90.1 us
    dot_general x5, matrix products, dot_cols(): lax.dot_general(left, right, (((0,), (0,)), ((), ())), preferred_element_...  88 us
    reduce_scatter x1, waiting for transfers between devices, body(): lax.psum_scatter(grad_in, 'replica', scatter_dimension=0, tiled=False)  74.5 us
    dot_general x8, matrix products, dot_rows(): lax.dot_general(left, right, (((1,), (1,)), ((), ())), preferred_element_...  67.4 us
    all_gather x1, waiting for transfers between devices, body(): all_renormed = lax.all_gather(renormed, EVERY, axis=0, tiled=True)  59.9 us
    ppermute x21, waiting for transfers between devices, swapped(): lax.ppermute(value, axis, [(source, source ^ step) for source in range(co...  48.2 us
  transfers between devices with their start and end apart: 30, of which 17 were waited for; matrix products, arithmetic and copies ran while one was open for 27% of the time, Pallas kernels for 6%

profile of v1, /device:TPU:0, one launch (start us, length us, event | category | flops | bytes accessed | tf_op | source)
XLA Modules:
  0.0 1195.0 jit_solution(811189072838164382)
XLA Ops:
  12.5 16.0 %fusion.137 = (bf16[1024,5632]{1,0:T(8,128)(2,1)}, bf16[1024,5632]{1,0:T(8,128)(2,1)}) fusion(bf16[1024,11264]{1,0:T(8,128)(2,1)} %param.22), kind=kLoop, calls=%fused_computation.295 | loop fusion | bytes 46137344 | tf_op jit(solution)/shard_map/slice | solution.py:417
  28.6 15.6 %constant_dynamic-slice_fusion.17 = (bf16[1024,2816]{1,0:T(8,128)(2,1)}, bf16[1024,2816]{1,0:T(8,128)(2,1)S(1)}, bf16[1024,2816]{1,0:T(8,128)(2,1)}, bf16[1024,2816]{1,0:T(8,128)(2,1)}) fusion(bf16[1024,5632]{1,0:T(8,128)(2,1)} %get-tuple-element.93, s32[]{:T(128)S(6)} %select_n.171, s32[]{:T(128)S(6)} %select_n.172, bf16[1024,5632]{1,0:T(8,128)(2,1)} %get-tuple-element.92), kind=kLoop, calls=%fused_computation.208 | loop fusion | bytes 46137352 | tf_op jit(solution)/shard_map/dynamic_slice | solution.py:338
  44.2 11.9 pad_maximum_fusion.1
  56.1 6.0 fusion.136
  76.0 9.6 all-gather
  87.3 14.0 %collective-permute-done = bf16[2,64,2048]{2,1,0:T(8,128)(2,1)S(1)} collective-permute-done((bf16[2,64,2048]{2,1,0:T(8,128)(2,1)S(1)}, bf16[2,64,2048]{2,1,0:T(8,128)(2,1)S(1)}, u32[]{:S(2)}, u32[]{:S(2)}) %collective-permute-start) | collective-permute-done | bytes 524320 | tf_op jit(solution)/shard_map/ppermute | solution.py:321
  113.8 5.6 convolution_add_fusion.2
  119.5 46.6 %shard_map.203 = (bf16[4,2,64,1024]{3,2,1,0:T(8,128)(2,1)S(1)}, f32[2,4,256,256]{3,2,1,0:T(8,128)S(1)}, f32[2,4,256,256]{3,2,1,0:T(8,128)S(1)}) custom-call(s32[1]{0:T(128)} %bitcast.1.place_ref, f32[4,2,64,3072]{3,2,1,0:T(8,128)S(1)} %bitcast.219, f32[4,2,64,3072]{3,2,1,0:T(8,128)S(1)} %bitcast.220, f32[4,2,64,3072]{3,2,1,0:T(8,128)S(1)} %bitcast.221, ...), custom_call_target="tpu_custom_call" | custom-call | tf_op jit(solution)/shard_map/pallas_call | solution.py:271
  171.8 6.9 collective-permute-done.6
  190.8 5.0 multiply_reduce_fusion.6
  199.0 6.1 fusion.71
  205.1 10.1 convolution_add_fusion.1
  215.3 10.1 multiply_convert_fusion.4
  225.3 6.5 fusion.7
  231.9 6.0 fusion.51
  238.3 7.9 fusion.52
  250.9 6.5 fusion.43
  257.4 6.7 fusion.44
  269.4 6.8 collective-permute-done.15
  276.2 10.6 collective-permute-done.14
  288.6 20.5 %shard_map.204 = (bf16[4,2,64,512]{3,2,1,0:T(8,128)(2,1)S(1)}, bf16[4,2,64,512]{3,2,1,0:T(8,128)(2,1)S(1)}, bf16[4,2,64,1024]{3,2,1,0:T(8,128)(2,1)S(1)}, bf16[4...) custom-call(s32[1]{0:T(128)} %bitcast.1.place_ref, f32[4,2,64,3072]{3,2,1,0:T(8,128)} %bitcast.223, ...), custom_call_target="tpu_custom_call" | custom-call | tf_op jit(solution)/shard_map/pallas_call | solution.py:297
  313.0 13.2 %convolution_convert_fusion = bf16[2048,1536]{1,0:T(8,128)(2,1)S(1)} fusion(bf16[512,2048]{1,0:T(8,128)(2,1)S(1)} %collective-permute-done.19, bf16[512,2048]{1,0:T(8,128)(2,1)S(1)} %copy-done.38, bf16[512,1536]{1,0:T(8,128)(2,1)S(1)} %collective-permute-done.20, bf16[512,512]{1,0:T(8,128)(2,1)S(1)} %get-tuple-element.113, ...), kind=kOutput, calls=%fused_computation.16 | convolution fusion | flops 6469713920 | bytes 13631488 | tf_op jit(solution)/shard_map/dot_general | solution.py:350
  349.0 11.6 all-to-all-done.1
  360.6 6.2 convolution_convert_fusion.1
  367.5 74.5 %reduce-scatter.2.cloned.1.call-done = bf16[1,512,1536]{2,1,0:T(8,128)(2,1)} async-done(((bf16[4,512,1536]{2,1,0:T(8,128)(2,1)}), bf16[1,512,1536]{2,1,0:T(8,128)(2,1)}) %reduce-scatter.2.cloned.1.call-update) | async-done | bytes 1572880 | tf_op jit(solution)/shard_map/reduce_scatter | solution.py:553
  442.0 25.4 %all_to_all.26 = bf16[8,64,1536]{2,1,0:T(8,128)(2,1)} all-to-all(bf16[8,64,1536]{2,1,0:T(8,128)(2,1)} %bitcast.273), channel_id=1, replica_groups=mesh['shard'=2,'seq'=4,'replica'=4] {'shard','seq'}, dimensions={0} | all-to-all | bytes 3145728 | tf_op jit(solution)/shard_map/all_to_all | solution.py:554
  468.5 5.3 constant_dynamic-slice_fusion.2
  473.9 9.7 fusion.138
  487.0 6.3 fusion.65
  495.5 6.3 add_bitcast_fusion
  511.9 44.0 %all-reduce.8.cloned.1.call-done = (f32[2048,32]{0,1:T(8,128)}, f32[4,8192]{1,0:T(4,128)}) async-done(((f32[2048,32]{0,1:T(8,128)}, f32[4,8192]{1,0:T(4,128)}), (f32[2048,32]{0,1:T(8,128)}, f32[4,8192]{1,0:T(4,128)})) %all-reduce.8.cloned.1.call-update) | async-done | bytes 393232 | tf_op jit(solution)/shard_map/psum | solution.py:615
  561.6 42.4 %all-reduce.1 = (f32[2,2048]{1,0:T(2,128)S(1)}, f32[2,16]{1,0:T(2,128)}, f32[256]{0:T(256)}) all-reduce(f32[2,2048]{1,0:T(2,128)S(1)} %pad_maximum_fusion.22, f32[2,16]{1,0:T(2,128)S(1)} %dynamic_update_slice.19, f32[256]{0:T(256)S(1)} %copy-done.61), channel_id=1, replica_groups=mesh['shard'=2,'seq'=4,'replica'=4] {'shard','seq','replica'}, use_global_device_ids=true, to_apply=%region_7.8 | all-reduce | flops 4384 | bytes 35072 | tf_op jit(solution)/shard_map/psum | solution.py:615
  607.3 37.0 %all-reduce.6.cloned.1.call-done = bf16[512,2048]{1,0:T(8,128)(2,1)} async-done(((bf16[512,2048]{1,0:T(8,128)(2,1)}), bf16[512,2048]{1,0:T(8,128)(2,1)}) %all-reduce.6.cloned.1.call-update) | async-done | bytes 2097168 | tf_op jit(solution)/shard_map/psum | solution.py:572
  648.4 112.6 %all-gather.11.cloned.1.call-done = bf16[4096,2048]{1,0:T(8,128)(2,1)} async-done(((bf16[128,2048]{1,0:T(8,128)(2,1)}), bf16[4096,2048]{1,0:T(8,128)(2,1)}) %all-gather.11.cloned.1.call-update) | async-done | bytes 16777232 | tf_op jit(solution)/shard_map/all_gather | solution.py:574
  761.1 19.0 %fusion.40 = f32[704,4096]{1,0:T(8,128)} fusion(bf16[4096,2048]{1,0:T(8,128)(2,1)} %all-gather.11.cloned.1.call-done, bf16[2816,2048]{1,0:T(8,128)(2,1)} %param.23, s32[]{:T(128)S(6)} %select_n.188), kind=kOutput, calls=%fused_computation.63 | convolution fusion | flops 11811160064 | bytes 31195140 | tf_op jit(solution)/shard_map/dot_general | solution.py:346
  780.1 95.9 %all-gather.13.cloned.1.call-done = bf16[32,64,1536]{2,1,0:T(8,128)(2,1)} async-done(((bf16[8,64,1536]{2,1,0:T(8,128)(2,1)}), bf16[32,64,1536]{2,1,0:T(8,128)(2,1)}) %all-gather.13.cloned.1.call-update) | async-done | bytes 6291472 | tf_op jit(solution)/shard_map/all_gather | solution.py:557
  898.5 20.9 %maximum_convert_fusion = f32[256,12288]{0,1:T(8,128)} fusion(bf16[256,4096]{0,1:T(8,128)(2,1)S(1)} %bitcast.254, bf16[256,4096]{0,1:T(8,128)(2,1)} %bitcast.255, bf16[256,2048]{0,1:T(8,128)(2,1)S(1)} %bitcast.262, bf16[256,2048]{0,1:T(8,128)(2,1)} %bitcast.263), kind=kLoop, calls=%fused_computation.19 | loop fusion | flops 25165824 | bytes 18874368 | tf_op jit(solution)/shard_map/convert_element_type | solution.py:568
  919.4 12.8 %copy.96 = f32[256,12288]{1,0:T(8,128)} copy(f32[256,12288]{0,1:T(8,128)} %maximum_convert_fusion) | data formatting | bytes 25165824
  932.2 59.9 %all-gather.9.cloned.1.call-done = bf16[4096,2048]{1,0:T(8,128)(2,1)} async-done(((bf16[128,2048]{1,0:T(8,128)(2,1)}), bf16[4096,2048]{1,0:T(8,128)(2,1)}) %all-gather.9.cloned.1.call-update) | async-done | bytes 16777232 | tf_op jit(solution)/shard_map/all_gather | solution.py:575
  992.1 19.9 %fusion.5 = f32[4096,1408]{0,1:T(8,128)} fusion(bf16[4096,2048]{1,0:T(8,128)(2,1)} %all-gather.9.cloned.1.call-done, s32[]{:T(128)S(6)} %select_n.154, bf16[1024,704]{1,0:T(8,128)(2,1)S(1)} %copy-done.41, bf16[1024,704]{1,0:T(8,128)(2,1)S(1)} %copy-done.42), kind=kOutput, calls=%fused_computation.13 | convolution fusion | flops 11816927232 | bytes 34340868 | tf_op jit(solution)/shard_map/dot_general | solution.py:342
  1012.1 26.2 %convolution_add_fusion = f32[4096,1408]{0,1:T(8,128)} fusion(f32[4096,1408]{0,1:T(8,128)} %fusion.5, bf16[4096,2048]{1,0:T(8,128)(2,1)} %all-gather.9.cloned.1.call-done, s32[]{:T(128)S(6)} %select_n.157, bf16[1024,704]{1,0:T(8,128)(2,1)} %constant_dynamic-slice_fusion, bf16[1024,704]{1,0:T(8,128)(2,1)} %constant_dynamic-slice_fusion.1), kind=kOutput, calls=%fused_computation | convolution fusion | flops 11822694400 | bytes 57671684 | tf_op jit(solution)/shard_map/dot_general | solution.py:342
  1038.3 21.7 %fusion.22 = bf16[2048,704]{0,1:T(8,128)(2,1)S(1)} fusion(bf16[4096,2048]{1,0:T(8,128)(2,1)} %all-gather.9.cloned.1.call-done, f32[704,4096]{1,0:T(8,128)} %fusion.40, f32[4096,1408]{0,1:T(8,128)} %convolution_add_fusion), kind=kOutput, calls=%fused_computation.42 | convolution fusion | flops 11829903360 | bytes 42729472 | tf_op jit(solution)/shard_map/dot_general | solution.py:350
  1060.2 23.7 %fusion.19 = bf16[2048,704]{0,1:T(8,128)(2,1)S(1)} fusion(bf16[4096,2048]{1,0:T(8,128)(2,1)} %all-gather.9.cloned.1.call-done, f32[704,4096]{1,0:T(8,128)} %fusion.40, f32[4096,1408]{0,1:T(8,128)} %convolution_add_fusion), kind=kOutput, calls=%fused_computation.41 | convolution fusion | flops 11841437696 | bytes 54263808 | tf_op jit(solution)/shard_map/dot_general | solution.py:350
  1092.0 23.2 %fusion.10 = f32[704,2048]{1,0:T(8,128)} fusion(bf16[4096,2048]{1,0:T(8,128)(2,1)} %all-gather.11.cloned.1.call-done, f32[4096,1408]{0,1:T(8,128)} %convolution_add_fusion), kind=kOutput, calls=%fused_computation.22 | convolution fusion | flops 11828461568 | bytes 45613056 | tf_op jit(solution)/shard_map/dot_general | solution.py:350
  1115.2 42.2 %all-to-all-done.2 = bf16[8,256,1408]{1,2,0:T(8,128)(2,1)} async-done(((bf16[8,256,1408]{1,2,0:T(8,128)(2,1)}), bf16[8,256,1408]{1,2,0:T(8,128)(2,1)}, u32[]{:S(2)}, u32[]{:S(2)}) %all-to-all-start.2) | async-done | bytes 5767200 | tf_op jit(solution)/shard_map/all_to_all | solution.py:593
  1157.4 8.3 convert_bitcast_fusion
  1165.7 9.6 copy.95
  1175.3 11.9 copy.97
  (324 shorter events, 152.8 us)
Async XLA Ops:
  8.0 78.5 %copy-start = (f32[2,16]{1,0:T(2,128)S(1)}, f32[2,16]{1,0:T(2,128)}, u32[]{:S(2)}) copy-start(f32[2,16]{1,0:T(2,128)} %param.19) | copy-start | bytes 388
  8.0 352.6 %all-gather.7.cloned.1.call-start = ((), (), s32[]{:S(2)}) async-start(), calls=%async_computation.5 | async-start | bytes 4718592 | tf_op jit(solution)/shard_map/all_gather | solution.py:571
  8.1 79.0 %collective-permute-start.2 = (bf16[2,64,2048]{2,1,0:T(8,128)(2,1)}, bf16[2,64,2048]{2,1,0:T(8,128)(2,1)}, u32[]{:S(2)}, u32[]{:S(2)}) collective-permute-start(bf16[2,64,2048]{2,1,0:T(8,128)(2,1)} %param.12), channel_id=1, source_target_pairs={{0,12},{4,8},{8,4},{12,0},{1,13},{5,9},{9,5},{13,1},{2,14},{6,10},... | collective-permute-start | bytes 1572872 | tf_op jit(solution)/shard_map/ppermute | solution.py:321
  12.0 75.2 %collective-permute-start.1 = (bf16[2,64,2048]{2,1,0:T(8,128)(2,1)}, bf16[2,64,2048]{2,1,0:T(8,128)(2,1)}, u32[]{:S(2)}, u32[]{:S(2)}) collective-permute-start(bf16[2,64,2048]{2,1,0:T(8,128)(2,1)} %param.12), channel_id=1, source_target_pairs={{0,8},{4,12},{8,0},{12,4},{1,9},{5,13},{9,1},{13,5},{2,10},{6,14},... | collective-permute-start | bytes 1572872 | tf_op jit(solution)/shard_map/ppermute | solution.py:321
  28.5 27.5 %slice-start = ((s8[25165824]{0:T(1024)(128)(4,1)}), s8[4194304]{0:T(1024)(128)(4,1)S(1)}, s32[]{:S(2)}) async-start(s8[25165824]{0:T(1024)(128)(4,1)} %bitcast.249), calls=%async_computation.11 | async-start | bytes 8388608
  28.5 27.5 %slice-start.1 = ((s8[25165824]{0:T(1024)(128)(4,1)}), s8[4194304]{0:T(1024)(128)(4,1)S(1)}, s32[]{:S(2)}) async-start(s8[25165824]{0:T(1024)(128)(4,1)} %bitcast.249), calls=%async_computation.12 | async-start | bytes 8388608
  28.6 27.5 %slice-start.2 = ((s8[25165824]{0:T(1024)(128)(4,1)}), s8[4194304]{0:T(1024)(128)(4,1)S(1)}, s32[]{:S(2)}) async-start(s8[25165824]{0:T(1024)(128)(4,1)} %bitcast.249), calls=%async_computation.13 | async-start | bytes 8388608
  28.6 27.5 %slice-start.3 = ((s8[25165824]{0:T(1024)(128)(4,1)}), s8[4194304]{0:T(1024)(128)(4,1)S(1)}, s32[]{:S(2)}) async-start(s8[25165824]{0:T(1024)(128)(4,1)} %bitcast.249), calls=%async_computation.14 | async-start | bytes 8388608
  56.1 143.0 %collective-permute-start.9 = (bf16[1024,5632]{1,0:T(8,128)(2,1)}, bf16[1024,5632]{1,0:T(8,128)(2,1)}, u32[]{:S(2)}, u32[]{:S(2)}) collective-permute-start(bf16[1024,5632]{1,0:T(8,128)(2,1)} %pad_maximum_fusion.1), channel_id=1, source_target_pairs={{0,16},{16,0},{1,17},{17,1},{2,18},{18,2},{3,19},{19,3},{4,20},{20... | collective-permute-start | bytes 34603016 | tf_op jit(solution)/shard_map/ppermute | solution.py:321
  68.4 41.6 %copy-start.23 = (bf16[1024,1024]{1,0:T(8,128)(2,1)}, bf16[1024,1024]{1,0:T(8,128)(2,1)S(1)}, u32[]{:S(2)}) copy-start(bf16[1024,1024]{1,0:T(8,128)(2,1)S(1)} %get-tuple-element.165) | copy-start | bytes 6291460
  75.0 38.8 %collective-permute-start.3 = (bf16[1024,3072]{1,0:T(8,128)(2,1)}, bf16[1024,3072]{1,0:T(8,128)(2,1)}, u32[]{:S(2)}, u32[]{:S(2)}) collective-permute-start(bf16[1024,3072]{1,0:T(8,128)(2,1)} %pad_maximum_fusion.4), channel_id=1, source_target_pairs={{0,16},{16,0},{1,17},{17,1},{2,18},{18,2},{3,19},{19,3},{4,20},{20... | collective-permute-start | bytes 18874376 | tf_op jit(solution)/shard_map/ppermute | solution.py:321
  75.5 115.2 %collective-permute-start.7 = (bf16[2048,2048]{1,0:T(8,128)(2,1)}, bf16[2048,2048]{1,0:T(8,128)(2,1)}, u32[]{:S(2)}, u32[]{:S(2)}) collective-permute-start(bf16[2048,2048]{1,0:T(8,128)(2,1)} %param.21), channel_id=1, source_target_pairs={{0,16},{16,0},{1,17},{17,1},{2,18},{18,2},{3,19},{19,3},{4,20},{20... | collective-permute-start | bytes 25165832 | tf_op jit(solution)/shard_map/ppermute | solution.py:321
  86.6 23.0 %copy-start.58 = (f32[4]{0:T(128)}, f32[4]{0:T(128)S(1)}, u32[]{:S(2)}) copy-start(f32[4]{0:T(128)S(1)} %get-tuple-element.162) | copy-start | bytes 52
  86.7 22.9 %copy-start.56 = (f32[2,256]{1,0:T(2,128)}, f32[2,256]{1,0:T(2,128)S(1)}, u32[]{:S(2)}) copy-start(f32[2,256]{1,0:T(2,128)S(1)} %compare_convert_fusion.1) | copy-start | bytes 6148
  87.1 14.2 %collective-permute-start = (bf16[2,64,2048]{2,1,0:T(8,128)(2,1)S(1)}, bf16[2,64,2048]{2,1,0:T(8,128)(2,1)S(1)}, u32[]{:S(2)}, u32[]{:S(2)}) collective-permute-start(bf16[2,64,2048]{2,1,0:T(8,128)(2,1)S(1)} %copy-done.12), channel_id=1, source_target_pairs={{0,4},{4,0},{8,12},{12,8},{1,5},{5,1},{9,13},{13,9},{2,6},{6,2},{1... | collective-permute-start | bytes 1572872 | tf_op jit(solution)/shard_map/ppermute | solution.py:321
  87.2 22.4 %copy-start.47 = (f32[1,2,1024]{2,0,1:T(1,128)}, f32[1,2,1024]{2,0,1:T(1,128)S(1)}, u32[]{:S(2)}) copy-start(f32[1,2,1024]{2,0,1:T(1,128)S(1)} %get-tuple-element.156) | copy-start | bytes 24580
  119.4 46.6 %copy-start.2 = (f32[512,3072]{1,0:T(8,128)}, f32[512,3072]{1,0:T(8,128)S(1)}, u32[]{:S(2)}) copy-start(f32[512,3072]{1,0:T(8,128)S(1)} %convolution_add_fusion.2) | copy-start | bytes 18874372
  168.3 10.4 collective-permute-start.6
  169.8 13.0 %collective-permute-start.5 = (bf16[2,64,1024]{2,1,0:T(8,128)(2,1)}, bf16[2,64,1024]{2,1,0:T(8,128)(2,1)S(1)}, u32[]{:S(2)}, u32[]{:S(2)}) collective-permute-start(bf16[2,64,1024]{2,1,0:T(8,128)(2,1)} %get-tuple-element.136), channel_id=1, source_target_pairs={{0,8},{4,12},{8,0},{12,4},{1,9},{5,13},{9,1},{13,5},{2,10},{6,14},... | collective-permute-start | bytes 786440 | tf_op jit(solution)/shard_map/ppermute | solution.py:321
  170.1 12.9 %collective-permute-start.4 = (bf16[2,64,1024]{2,1,0:T(8,128)(2,1)}, bf16[2,64,1024]{2,1,0:T(8,128)(2,1)S(1)}, u32[]{:S(2)}, u32[]{:S(2)}) collective-permute-start(bf16[2,64,1024]{2,1,0:T(8,128)(2,1)} %get-tuple-element.137), channel_id=1, source_target_pairs={{0,4},{4,0},{8,12},{12,8},{1,5},{5,1},{9,13},{13,9},{2,6},{6,2},{1... | collective-permute-start | bytes 786440 | tf_op jit(solution)/shard_map/ppermute | solution.py:321
  196.9 2.1 collective-permute-start.8
  197.0 18.3 %collective-permute-start.11 = (bf16[128,2048]{1,0:T(8,128)(2,1)S(1)}, bf16[128,2048]{1,0:T(8,128)(2,1)}, u32[]{:S(2)}, u32[]{:S(2)}) collective-permute-start(bf16[128,2048]{1,0:T(8,128)(2,1)S(1)} %bitcast.271), channel_id=1, source_target_pairs={{0,16},{16,0},{1,17},{17,1},{2,18},{18,2},{3,19},{19,3},{4,20},{20... | collective-permute-start | bytes 1572872 | tf_op jit(solution)/shard_map/ppermute | solution.py:321
  238.1 8.6 collective-permute-start.12
  246.3 2.7 collective-permute-start.10
  250.8 191.2 %reduce-scatter.2.cloned.1.call-start = ((), (), s32[]{:S(2)}) async-start(), calls=%async_computation.4 | async-start | bytes 7864320 | tf_op jit(solution)/shard_map/reduce_scatter | solution.py:553
  265.9 10.3 collective-permute-start.15
  267.3 19.4 %collective-permute-start.14 = (bf16[128,1024]{1,0:T(8,128)(2,1)}, bf16[128,1024]{1,0:T(8,128)(2,1)S(1)}, u32[]{:S(2)}, u32[]{:S(2)}) collective-permute-start(bf16[128,1024]{1,0:T(8,128)(2,1)} %get-tuple-element.117), channel_id=1, source_target_pairs={{0,8},{4,12},{8,0},{12,4},{1,9},{5,13},{9,1},{13,5},{2,10},{6,14},... | collective-permute-start | bytes 786440 | tf_op jit(solution)/shard_map/ppermute | solution.py:321
  267.8 18.9 %collective-permute-start.13 = (bf16[128,1024]{1,0:T(8,128)(2,1)}, bf16[128,1024]{1,0:T(8,128)(2,1)S(1)}, u32[]{:S(2)}, u32[]{:S(2)}) collective-permute-start(bf16[128,1024]{1,0:T(8,128)(2,1)} %get-tuple-element.116), channel_id=1, source_target_pairs={{0,4},{4,0},{8,12},{12,8},{1,5},{5,1},{9,13},{13,9},{2,6},{6,2},{1... | collective-permute-start | bytes 786440 | tf_op jit(solution)/shard_map/ppermute | solution.py:321
  269.4 40.3 %collective-permute-start.19 = (bf16[512,2048]{1,0:T(8,128)(2,1)}, bf16[512,2048]{1,0:T(8,128)(2,1)S(1)}, u32[]{:S(2)}, u32[]{:S(2)}) collective-permute-start(bf16[512,2048]{1,0:T(8,128)(2,1)} %copy-done.37), channel_id=1, source_target_pairs={{0,16},{16,0},{1,17},{17,1},{2,18},{18,2},{3,19},{19,3},{4,20},{20... | collective-permute-start | bytes 6291464 | tf_op jit(solution)/shard_map/ppermute | solution.py:321
  309.6 3.5 collective-permute-start.20
  341.5 19.1 %all-to-all-start.1 = ((bf16[128,8,512]{2,0,1:T(8,128)(2,1)}), bf16[128,8,512]{2,0,1:T(8,128)(2,1)}, u32[]{:S(2)}, u32[]{:S(2)}) async-start(bf16[128,8,512]{2,0,1:T(8,128)(2,1)} %copy.92), calls=%async_computation.2 | async-start | bytes 2097152 | tf_op jit(solution)/shard_map/all_to_all | solution.py:570
  345.7 210.2 %all-reduce.8.cloned.1.call-start = ((), (), s32[]{:S(2)}) async-start(), calls=%async_computation.10 | async-start | bytes 786432 | tf_op jit(solution)/shard_map/psum | solution.py:615
  349.0 295.3 %all-reduce.6.cloned.1.call-start = ((), (), s32[]{:S(2)}) async-start(), calls=%async_computation.6 | async-start | bytes 4194304 | tf_op jit(solution)/shard_map/psum | solution.py:572
  366.8 101.4 %copy-start.14 = (bf16[2,64,2048]{2,1,0:T(8,128)(2,1)S(1)}, bf16[2,64,2048]{2,1,0:T(8,128)(2,1)}, u32[]{:S(2)}) copy-start(bf16[2,64,2048]{2,1,0:T(8,128)(2,1)} %param.12) | copy-start | bytes 1572868
  366.9 394.2 %all-gather.11.cloned.1.call-start = ((), (), s32[]{:S(2)}) async-start(), calls=%async_computation.8 | async-start | bytes 17301504 | tf_op jit(solution)/shard_map/all_gather | solution.py:574
  367.4 508.6 %all-gather.13.cloned.1.call-start = ((), (), s32[]{:S(2)}) async-start(), calls=%async_computation.9 | async-start | bytes 7864320 | tf_op jit(solution)/shard_map/all_gather | solution.py:557
  442.0 31.8 %copy-start.50 = (f32[1,2,4,4,64]{4,3,2,1,0:T(4,128)S(1)}, f32[1,2,4,4,64]{4,3,2,1,0:T(4,128)}, u32[]{:S(2)}) copy-start(f32[1,2,4,4,64]{4,3,2,1,0:T(4,128)} %copy-done.49) | copy-start | bytes 24580
  467.4 524.7 %all-gather.9.cloned.1.call-start = ((), (), s32[]{:S(2)}) async-start(), calls=%async_computation.7 | async-start | bytes 17301504 | tf_op jit(solution)/shard_map/all_gather | solution.py:575
  502.9 55.8 %copy-start.15 = (bf16[2,64,2048]{2,1,0:T(8,128)(2,1)S(1)}, bf16[2,64,2048]{2,1,0:T(8,128)(2,1)}, u32[]{:S(2)}) copy-start(bf16[2,64,2048]{2,1,0:T(8,128)(2,1)} %param.12) | copy-start | bytes 1572868
  502.9 55.8 %copy-start.48 = (f32[1,2,1024]{2,0,1:T(1,128)S(1)}, f32[1,2,1024]{2,0,1:T(1,128)}, u32[]{:S(2)}) copy-start(f32[1,2,1024]{2,0,1:T(1,128)} %copy-done.47) | copy-start | bytes 24580
  504.6 57.0 %copy-start.54 = (f32[2048]{0:T(1024)S(1)}, f32[2048]{0:T(1024)}, u32[]{:S(2)}) copy-start(f32[2048]{0:T(1024)} %get-tuple-element.71) | copy-start | bytes 24580
  504.6 57.0 %copy-start.61 = (f32[256]{0:T(256)S(1)}, f32[256]{0:T(256)}, u32[]{:S(2)}) copy-start(f32[256]{0:T(256)} %get-tuple-element.75) | copy-start | bytes 3076
  504.6 54.1 %collective-permute-start.18 = (bf16[128,2048]{1,0:T(8,128)(2,1)}, bf16[128,2048]{1,0:T(8,128)(2,1)}, u32[]{:S(2)}, u32[]{:S(2)}) collective-permute-start(bf16[128,2048]{1,0:T(8,128)(2,1)} %get-tuple-element.109), channel_id=1, source_target_pairs={{0,12},{4,8},{8,4},{12,0},{1,13},{5,9},{9,5},{13,1},{2,14},{6,10},... | collective-permute-start | bytes 1572872 | tf_op jit(solution)/shard_map/ppermute | solution.py:321
  505.3 53.3 %collective-permute-start.17 = (bf16[128,2048]{1,0:T(8,128)(2,1)}, bf16[128,2048]{1,0:T(8,128)(2,1)}, u32[]{:S(2)}, u32[]{:S(2)}) collective-permute-start(bf16[128,2048]{1,0:T(8,128)(2,1)} %get-tuple-element.110), channel_id=1, source_target_pairs={{0,8},{4,12},{8,0},{12,4},{1,9},{5,13},{9,1},{13,5},{2,10},{6,14},... | collective-permute-start | bytes 1572872 | tf_op jit(solution)/shard_map/ppermute | solution.py:321
  506.9 51.7 %collective-permute-start.16 = (bf16[128,2048]{1,0:T(8,128)(2,1)S(1)}, bf16[128,2048]{1,0:T(8,128)(2,1)}, u32[]{:S(2)}, u32[]{:S(2)}) collective-permute-start(bf16[128,2048]{1,0:T(8,128)(2,1)S(1)} %get-tuple-element.108), channel_id=1, source_target_pairs={{0,4},{4,0},{8,12},{12,8},{1,5},{5,1},{9,13},{13,9},{2,6},{6,2},{1... | collective-permute-start | bytes 1572872 | tf_op jit(solution)/shard_map/ppermute | solution.py:321
  919.4 72.7 %copy-start.41 = (bf16[1024,704]{1,0:T(8,128)(2,1)S(1)}, bf16[1024,704]{1,0:T(8,128)(2,1)}, u32[]{:S(2)}) copy-start(bf16[1024,704]{1,0:T(8,128)(2,1)} %get-tuple-element.171) | copy-start | bytes 4325380
  919.4 72.7 %copy-start.42 = (bf16[1024,704]{1,0:T(8,128)(2,1)S(1)}, bf16[1024,704]{1,0:T(8,128)(2,1)}, u32[]{:S(2)}) copy-start(bf16[1024,704]{1,0:T(8,128)(2,1)} %get-tuple-element.172) | copy-start | bytes 4325380
  1087.0 70.4 %all-to-all-start.2 = ((bf16[8,256,1408]{1,2,0:T(8,128)(2,1)}), bf16[8,256,1408]{1,2,0:T(8,128)(2,1)}, u32[]{:S(2)}, u32[]{:S(2)}) async-start(bf16[8,256,1408]{1,2,0:T(8,128)(2,1)} %pad_maximum_fusion.5), calls=%async_computation.3 | async-start | bytes 11534336 | tf_op jit(solution)/shard_map/all_to_all | solution.py:593
  (53 other events, 337.3 us)
Sparse Core Ops, SparseCore 0:
  250.9 43.1 all-gather.6
  329.7 112.2 reduce-scatter.1
Sparse Core Ops, SparseCore 1:
  351.6 204.3 all-reduce.7
  558.3 86.0 all-reduce.5
  647.2 113.8 all-gather.10
  762.6 113.3 all-gather.12
  879.1 113.0 all-gather.8

commit v2 on v1

v2 whole, which is shorter than its diff:
```python
import functools

import jax
import jax.numpy as jnp
from jax import lax
from jax.experimental import pallas as pl
from jax.experimental.pallas import tpu as pltpu
from jax.sharding import PartitionSpec as P

D = 2048
HEADS = 16
DK = 128
DV = 256
FF = 5632
KERNEL = 4
KD = 2048
VD = 4096
CONVW = 8192
PROJW = 12288
EPS = 1e-06
HIGHEST = lax.Precision.HIGHEST
LOWEST_DECAY = -104.0
F32 = jnp.float32
BF16 = jnp.bfloat16
EVERY = ("shard", "seq", "replica")
GROUP = ("shard", "seq")


def mm(left, right, dims=((1,), (0,))):
    return lax.dot_general(
        left.astype(BF16), right.astype(BF16), (dims, ((), ())), preferred_element_type=F32
    )


def split(value):
    high = value.astype(BF16)
    return high, (value - high.astype(F32)).astype(BF16)


def mm3s(left, right, dims=((1,), (0,))):
    return (
        mm(left[0], right[0], dims) + mm(left[0], right[1], dims) + mm(left[1], right[0], dims)
    )


def mm3(left, right, dims=((1,), (0,))):
    return mm3s(split(left), split(right), dims)


ROWS_ROWS = ((1,), (1,))
COLS_COLS = ((0,), (0,))


def delayed(value, steps, rows):
    if steps == 0:
        return value
    return jnp.where(rows >= steps, pltpu.roll(value, steps, 0), 0.0)


def advanced(value, steps, rows):
    if steps == 0:
        return value
    length = value.shape[0]
    return jnp.where(rows < length - steps, pltpu.roll(value, length - steps, 0), 0.0)


def convolved(source, taps, rows):
    mixed = taps[KERNEL - 1 : KERNEL] * source
    for offset in range(KERNEL - 1):
        mixed = mixed + taps[offset : offset + 1] * delayed(source, KERNEL - 1 - offset, rows)
    return mixed


def unit(value):
    scale = lax.rsqrt(jnp.sum(value * value, -1, keepdims=True) + EPS)
    return value * scale, scale


def decay_matrices(rates):
    length = rates.shape[1]
    row_ids = lax.broadcasted_iota(jnp.int32, (length, length), 0)
    col_ids = lax.broadcasted_iota(jnp.int32, (length, length), 1)
    decay_row = rates[0:1]
    rate_row = rates[1:2]
    diagonal = row_ids == col_ids
    running = jnp.sum(jnp.where(row_ids >= col_ids, decay_row, 0.0), 1, keepdims=True)
    running_row = jnp.sum(jnp.where(diagonal, running, 0.0), 0, keepdims=True)
    rate = jnp.sum(jnp.where(diagonal, rate_row, 0.0), 1, keepdims=True)
    spread = jnp.minimum(running - running_row, 0.0)
    weight = jnp.where(row_ids >= col_ids, jnp.exp(spread), 0.0)
    return row_ids, col_ids, rate, weight


def lower_inverses(systems, row_ids, col_ids):
    length = row_ids.shape[0]
    eye = (row_ids == col_ids).astype(F32)
    same = jnp.bitwise_xor(row_ids, col_ids)
    inverses = [eye - jnp.where(same < 2, system, 0.0) for system in systems]
    size = 2
    while size < length:
        level = (same >= size) & (same < 2 * size)
        halves = [split(inverse) for inverse in inverses]
        inner = [
            mm3s(split(jnp.where(level, system, 0.0)), half)
            for system, half in zip(systems, halves)
        ]
        inverses = [
            inverse - mm3s(half, split(item))
            for inverse, half, item in zip(inverses, halves, inner)
        ]
        size *= 2
    return inverses


def head_inputs(source, taps):
    rows = lax.broadcasted_iota(jnp.int32, (source.shape[0], 1), 0)
    cuts = (0, DK, 2 * DK, 2 * DK + DV)
    raw = [source[:, low:high].astype(BF16).astype(F32) for low, high in zip(cuts, cuts[1:])]
    mixed = [convolved(item, kernel, rows) for item, kernel in zip(raw, taps)]
    slopes = [jax.nn.sigmoid(item) for item in mixed]
    query_unit, query_scale = unit(mixed[0] * slopes[0])
    key_rows, key_scale = unit(mixed[1] * slopes[1])
    values = mixed[2] * slopes[2]
    queries = query_unit * DK ** (-0.5)
    return raw, rows, mixed, slopes, queries, key_rows, values, query_unit, query_scale, key_scale


def slot_rows(ref, place, slot, low, high):
    pieces = ref.shape[0]
    return jnp.concatenate(
        [ref[jnp.bitwise_xor(place, j), slot, :, low:high] for j in range(pieces)], 0
    )


def taps_of(refs, head):
    return [
        ref[:, head * width : (head + 1) * width].astype(F32)
        for ref, width in zip(refs, (DK, DK, DV))
    ]


def forward_kernel(
    place_ref, proj_ref, taps_q, taps_k, taps_v, rates_ref, gain_ref, *outs
):
    *gated_refs, inverse_ref, update_ref, kept = outs
    place = place_ref[0]
    micro, together = rates_ref.shape[0], rates_ref.shape[1]
    pairs = [(slot, head) for slot in range(micro) for head in range(together)]
    work = []
    for slot, head in pairs:
        source = slot_rows(proj_ref, place, slot, head * HEAD_WIDTH, (head + 1) * HEAD_WIDTH)
        items = head_inputs(source, taps_of((taps_q, taps_k, taps_v), head))
        queries, key_rows, values = items[4:7]
        row_ids, col_ids, rate, weight = decay_matrices(rates_ref[slot, head])
        system = jnp.where(
            row_ids > col_ids, rate * mm3(key_rows, key_rows, ROWS_ROWS) * weight, 0.0
        )
        scores = (mm(queries, key_rows, ROWS_ROWS) * weight).astype(BF16)
        gate = source[:, 2 * DK + DV :]
        work.append((system, scores, rate * values, gate * jax.nn.sigmoid(gate)))
    inverses = lower_inverses([item[0] for item in work], row_ids, col_ids)
    row = proj_ref.shape[2]
    for (slot, head), item, inverse in zip(pairs, work, inverses):
        update = mm3(inverse, item[2])
        outputs = mm(item[1], update)
        scaled = (
            outputs
            * lax.rsqrt(jnp.mean(outputs * outputs, -1, keepdims=True) + EPS)
            * gain_ref[...]
        )
        inverse_ref[slot, head] = inverse
        update_ref[slot, head] = update
        kept[...] = (scaled * item[3]).reshape(kept.shape)
        for step, ref in enumerate(gated_refs):
            ref[slot, :, head * DV : (head + 1) * DV] = kept[jnp.bitwise_xor(place, step)].astype(
                ref.dtype
            )


def unit_back(grad, direction, scale):
    return scale * (grad - direction * jnp.sum(grad * direction, -1, keepdims=True))


def backward_kernel(
    place_ref, proj_ref, taps_q, taps_k, taps_v, rates_ref, gain_ref, inverse_ref, update_ref,
    *refs,
):
    *grad_refs, dproj_ref, small_ref, taken, kept = refs
    place = place_ref[0]
    micro, together = rates_ref.shape[0], rates_ref.shape[1]
    small_ref[...] = jnp.zeros_like(small_ref)
    for slot in range(micro):
        for head in range(together):
            backward_head(
                place, slot, head, proj_ref, (taps_q, taps_k, taps_v), rates_ref, gain_ref,
                inverse_ref, update_ref, grad_refs, dproj_ref, small_ref,
                taken.at[slot, head], kept.at[slot, head],
            )


def backward_head(
    place, slot, head, proj_ref, taps_refs, rates_ref, gain_ref, inverse_ref, update_ref,
    grad_refs, dproj_ref, small_ref, taken, kept,
):
    source = slot_rows(proj_ref, place, slot, head * HEAD_WIDTH, (head + 1) * HEAD_WIDTH)
    taps = taps_of(taps_refs, head)
    raw, rows, mixed, slopes, queries, key_rows, values, query_unit, query_scale, key_scale = (
        head_inputs(source, taps)
    )
    for step, ref in enumerate(grad_refs):
        taken[jnp.bitwise_xor(place, step)] = ref[slot, :, head * DV : (head + 1) * DV]
    upstream = jnp.concatenate([taken[j] for j in range(len(grad_refs))], 0).astype(F32)
    row_ids, col_ids, rate, weight = decay_matrices(rates_ref[slot, head])
    inner = mm3(key_rows, key_rows, ROWS_ROWS)
    strict = row_ids > col_ids
    keyed = jnp.where(strict, inner * weight, 0.0)
    scores = mm(queries, key_rows, ROWS_ROWS) * weight
    inverse = inverse_ref[slot, head]
    update = update_ref[slot, head]
    outputs = mm(scores, update)
    gate = source[:, 2 * DK + DV :]
    gate_slope = jax.nn.sigmoid(gate)
    out_scale = lax.rsqrt(jnp.mean(outputs * outputs, -1, keepdims=True) + EPS)
    out_unit = outputs * out_scale
    gain = gain_ref[...]
    scaled_grad = upstream * (gate * gate_slope)
    gate_grad = upstream * out_unit * gain * (gate_slope * (1.0 + gate * (1.0 - gate_slope)))
    gain_grad = jnp.sum(scaled_grad * out_unit, 0, keepdims=True)
    unit_grad = scaled_grad * gain
    out_grad = out_scale * (
        unit_grad - out_unit * jnp.mean(unit_grad * out_unit, -1, keepdims=True)
    )
    scores_grad = jnp.where(row_ids >= col_ids, mm(out_grad, update, ROWS_ROWS), 0.0)
    update_grad = mm(scores, out_grad, COLS_COLS)
    target_grad = mm3(inverse, update_grad, COLS_COLS)
    system_grad = jnp.where(strict, -mm(target_grad, update, ROWS_ROWS), 0.0)
    value_grad = rate * target_grad
    keyed_grad = system_grad * keyed
    rate_grad = jnp.sum(target_grad * values, 1, keepdims=True) + jnp.sum(
        keyed_grad, 1, keepdims=True
    )
    spread_grad = keyed_grad * rate + scores_grad * scores
    inner_grad = system_grad * weight * rate
    raw_scores_grad = scores_grad * weight
    query_grad = mm(raw_scores_grad, key_rows) * DK ** (-0.5)
    key_grad = (
        mm(raw_scores_grad, queries, COLS_COLS)
        + mm(inner_grad, key_rows)
        + mm(inner_grad, key_rows, COLS_COLS)
    )
    diagonal = row_ids == col_ids
    column_sum = jnp.sum(spread_grad, 0, keepdims=True)
    running_grad = jnp.sum(spread_grad, 1, keepdims=True) - jnp.sum(
        jnp.where(diagonal, column_sum, 0.0), 1, keepdims=True
    )
    decay_grad = jnp.sum(jnp.where(row_ids >= col_ids, running_grad, 0.0), 0, keepdims=True)
    rate_grad_row = jnp.sum(jnp.where(diagonal, rate_grad, 0.0), 0, keepdims=True)
    active_grads = (
        unit_back(query_grad, query_unit, query_scale),
        unit_back(key_grad, key_rows, key_scale),
        value_grad,
    )
    cuts = (0, DK, 2 * DK, 2 * DK + DV, HEAD_WIDTH)
    for low, high, grad_out, plain, before, slope, kernel in zip(
        cuts, cuts[1:], active_grads, raw, mixed, slopes, taps
    ):
        mixed_grad = grad_out * (slope * (1.0 + before * (1.0 - slope)))
        total = kernel[KERNEL - 1 : KERNEL] * mixed_grad
        for offset in range(KERNEL):
            steps = KERNEL - 1 - offset
            if steps:
                total = total + kernel[offset : offset + 1] * advanced(mixed_grad, steps, rows)
            small_ref[slot, head, offset : offset + 1, low:high] = jnp.sum(
                mixed_grad * delayed(plain, steps, rows), 0, keepdims=True
            )
        kept[:, :, low:high] = total.reshape(kept.shape[:2] + (high - low,))
    kept[:, :, cuts[3] : cuts[4]] = gate_grad.reshape(kept.shape[:2] + (DV,))
    for step in range(kept.shape[0]):
        dproj_ref[step, slot, :, head * HEAD_WIDTH : (head + 1) * HEAD_WIDTH] = kept[
            jnp.bitwise_xor(place, step)
        ].astype(dproj_ref.dtype)
    small_ref[slot, head, 4:5, 0:DV] = gain_grad
    length = decay_grad.shape[1]
    small_ref[slot, head, 5:6, 0:length] = decay_grad
    small_ref[slot, head, 6:7, 0:length] = rate_grad_row


VMEM_LIMIT = 56 * 1024 * 1024
HEAD_WIDTH = 2 * DK + 2 * DV
SMALL_ROWS = 8


def mixer_specs(pieces, micro, row, heads, length, together):
    def slots(width):
        return pl.BlockSpec((micro, row, together * width), lambda h, place: (0, 0, h))

    def taps(width, first):
        at = first // (together * width)
        return pl.BlockSpec(
            (KERNEL, together * width),
            lambda h, place: (0, at + place[0] * (heads // together) + h),
        )

    proj = pl.BlockSpec(
        (pieces, micro, row, together * HEAD_WIDTH), lambda h, place: (0, 0, 0, h)
    )
    kernel = [taps(DK, 0), taps(DK, KD), taps(DV, 2 * KD)]
    rates = pl.BlockSpec((micro, together, SMALL_ROWS, length), lambda h, place: (0, h, 0, 0))
    gain = pl.BlockSpec((1, DV), lambda h, place: (0, 0))

    def square(width):
        return pl.BlockSpec((micro, together, length, width), lambda h, place: (0, h, 0, 0))

    return slots, proj, kernel, rates, gain, square


def mixer_forward(place, projected, taps, rates, gain, together):
    pieces, micro, row, _ = projected.shape
    heads, length = rates.shape[1], rates.shape[3]
    slots, proj, kernel, rate_spec, gain_spec, square = mixer_specs(
        pieces, micro, row, heads, length, together
    )
    return pl.pallas_call(
        forward_kernel,
        grid_spec=pltpu.PrefetchScalarGridSpec(
            num_scalar_prefetch=1,
            grid=(heads // together,),
            in_specs=[proj] + kernel + [rate_spec, gain_spec],
            out_specs=[slots(DV)] * pieces + [square(length), square(DV)],
            scratch_shapes=[pltpu.VMEM((pieces, row, DV), F32)],
        ),
        out_shape=[jax.ShapeDtypeStruct((micro, row, heads * DV), BF16)] * pieces
        + [
            jax.ShapeDtypeStruct((micro, heads, length, length), F32),
            jax.ShapeDtypeStruct((micro, heads, length, DV), F32),
        ],
        compiler_params=pltpu.CompilerParams(vmem_limit_bytes=VMEM_LIMIT),
        name="mixer_forward",
    )(place, projected, taps, taps, taps, rates, gain)


def mixer_backward(place, projected, taps, rates, gain, inverse, update, grads, together):
    pieces, micro, row, _ = projected.shape
    heads, length = rates.shape[1], rates.shape[3]
    slots, proj, kernel, rate_spec, gain_spec, square = mixer_specs(
        pieces, micro, row, heads, length, together
    )
    small_width = 2 * DK + DV
    return pl.pallas_call(
        backward_kernel,
        grid_spec=pltpu.PrefetchScalarGridSpec(
            num_scalar_prefetch=1,
            grid=(heads // together,),
            in_specs=[proj]
            + kernel
            + [rate_spec, gain_spec, square(length), square(DV)]
            + [slots(DV)] * pieces,
            out_specs=[
                proj,
                pl.BlockSpec(
                    (micro, together, SMALL_ROWS, small_width), lambda h, place: (0, h, 0, 0)
                ),
            ],
            scratch_shapes=[
                pltpu.VMEM((micro, together, pieces, row, DV), BF16),
                pltpu.VMEM((micro, together, pieces, row, HEAD_WIDTH), F32),
            ],
        ),
        out_shape=[
            jax.ShapeDtypeStruct((pieces, micro, row, heads * HEAD_WIDTH), BF16),
            jax.ShapeDtypeStruct((micro, heads, SMALL_ROWS, small_width), F32),
        ],
        compiler_params=pltpu.CompilerParams(vmem_limit_bytes=VMEM_LIMIT),
        name="mixer_backward",
    )(place, projected, taps, taps, taps, rates, gain, inverse, update, *grads)


def pick_kernel(place_ref, q_ref, k_ref, v_ref, g_ref, out_ref):
    at = 0
    for ref in (q_ref, k_ref, v_ref, g_ref):
        out_ref[:, at : at + ref.shape[1]] = ref[...]
        at += ref.shape[1]


def pick_heads(place, w_in, heads):
    depth = w_in.shape[0]

    def one(width, first):
        at = first // width
        return pl.BlockSpec((depth, width), lambda h, place: (0, at + place[0] * heads + h))

    return pl.pallas_call(
        pick_kernel,
        grid_spec=pltpu.PrefetchScalarGridSpec(
            num_scalar_prefetch=1,
            grid=(heads,),
            in_specs=[one(DK, 0), one(DK, KD), one(DV, 2 * KD), one(DV, CONVW)],
            out_specs=pl.BlockSpec((depth, HEAD_WIDTH), lambda h, place: (0, h)),
        ),
        out_shape=jax.ShapeDtypeStruct((depth, heads * HEAD_WIDTH), w_in.dtype),
        compiler_params=pltpu.CompilerParams(vmem_limit_bytes=VMEM_LIMIT),
        name="pick_heads",
    )(place, w_in, w_in, w_in, w_in)


def project_kernel(parts, pieces, place_ref, gain_ref, *refs):
    piece_refs, weight_refs = refs[:pieces], refs[pieces : pieces + parts]
    normed_ref, out_ref = refs[pieces + parts :]
    rows = piece_refs[0].shape[0]

    @pl.when(pl.program_id(0) == 0)
    def _():
        for at, ref in enumerate(piece_refs):
            values = ref[...].astype(F32)
            scale = lax.rsqrt(jnp.mean(values * values, -1, keepdims=True) + EPS)
            normed_ref[at * rows : (at + 1) * rows] = (values * scale * gain_ref[...]).astype(BF16)

    total = None
    for step, ref in enumerate(weight_refs):
        depth = ref.shape[0]
        at = pl.multiple_of(jnp.bitwise_xor(place_ref[0], step) * depth, 128)
        term = jnp.dot(normed_ref[:, pl.ds(at, depth)], ref[...], preferred_element_type=F32)
        total = term if total is None else total + term
    out_ref[...] = total


def project(shard_place, gain, piece_list, weights):
    rows, width = piece_list[0].shape
    columns = weights[0].shape[1]
    tile = HEAD_WIDTH
    pieces, parts = len(piece_list), len(weights)
    whole = pl.BlockSpec((rows, width), lambda j, place: (0, 0))
    return pl.pallas_call(
        functools.partial(project_kernel, parts, pieces),
        grid_spec=pltpu.PrefetchScalarGridSpec(
            num_scalar_prefetch=1,
            grid=(columns // tile,),
            in_specs=[pl.BlockSpec((1, width), lambda j, place: (0, 0))]
            + [whole] * pieces
            + [pl.BlockSpec((weights[0].shape[0], tile), lambda j, place: (0, j))] * parts,
            out_specs=[
                pl.BlockSpec((pieces * rows, width), lambda j, place: (0, 0)),
                pl.BlockSpec((pieces * rows, tile), lambda j, place: (0, j)),
            ],
        ),
        out_shape=[
            jax.ShapeDtypeStruct((pieces * rows, width), BF16),
            jax.ShapeDtypeStruct((pieces * rows, columns), F32),
        ],
        compiler_params=pltpu.CompilerParams(vmem_limit_bytes=VMEM_LIMIT),
        name="project",
    )(shard_place, gain, *piece_list, *weights)


def head_rows(places_ref, step, rows, group):
    width = min(rows, group)
    found = []
    for at in range(rows // width):
        first = jnp.bitwise_xor(places_ref[1], step) * rows + at * width
        whose = jnp.bitwise_xor(first // group, places_ref[0])
        found.append((whose, pl.multiple_of(first % group, 128) if width < group else 0, width))
    return found


def merge_kernel(parts, pieces, places_ref, gain_ref, tokens_ref, *refs):
    mixed_refs, weight_refs = refs[:pieces], refs[pieces : pieces + parts]
    middle_ref, normed_ref, *left_refs, gathered = refs[pieces + parts :]
    step_id = pl.program_id(0)
    group = mixed_refs[0].shape[1]

    @pl.when(step_id == 0)
    def _():
        for at, ref in enumerate(mixed_refs):
            gathered[at] = ref[...]
        height = left_refs[0].shape[1] // parts
        for at, ref in enumerate(left_refs):
            for part in range(parts):
                first = (part * pieces + jnp.bitwise_xor(places_ref[0], at)) * height
                whose = jnp.bitwise_xor(first // group, places_ref[0])
                ref[:, part * height : (part + 1) * height] = gathered[
                    whose, :, pl.ds(pl.multiple_of(first % group, 128), height)
                ]

    tile = weight_refs[0].shape[1]
    total = tokens_ref[...].astype(F32)
    for step, ref in enumerate(weight_refs):
        rows = ref.shape[0]
        for at, (whose, first, width) in enumerate(head_rows(places_ref, step, rows, group)):
            total = total + jnp.dot(
                gathered[whose, :, pl.ds(first, width)],
                ref[at * width : (at + 1) * width],
                preferred_element_type=F32,
            )
    middle_ref[:, pl.ds(pl.multiple_of(step_id * tile, 128), tile)] = total

    @pl.when(step_id == pl.num_programs(0) - 1)
    def _():
        values = middle_ref[...]
        scale = lax.rsqrt(jnp.mean(values * values, -1, keepdims=True) + EPS)
        normed_ref[...] = (values * scale * gain_ref[...]).astype(BF16)


def merge(places, gain, tokens, mixed, weights):
    rows, width = tokens.shape
    tile = 512
    pieces, parts = len(mixed), len(weights)
    group = mixed[0].shape[1]
    whole = pl.BlockSpec((rows, width), lambda j, place: (0, 0))
    return pl.pallas_call(
        functools.partial(merge_kernel, parts, pieces),
        grid_spec=pltpu.PrefetchScalarGridSpec(
            num_scalar_prefetch=1,
            grid=(width // tile,),
            in_specs=[
                pl.BlockSpec((1, width), lambda j, place: (0, 0)),
                pl.BlockSpec((rows, tile), lambda j, place: (0, j)),
            ]
            + [pl.BlockSpec((rows, group), lambda j, place: (0, 0))] * pieces
            + [pl.BlockSpec((weights[0].shape[0], tile), lambda j, place: (0, j))] * parts,
            out_specs=[whole, whole]
            + [pl.BlockSpec((rows, group), lambda j, place: (0, 0))] * pieces,
            scratch_shapes=[pltpu.VMEM((pieces, rows, group), BF16)],
        ),
        out_shape=[
            jax.ShapeDtypeStruct((rows, width), F32),
            jax.ShapeDtypeStruct((rows, width), BF16),
        ]
        + [jax.ShapeDtypeStruct((rows, group), BF16)] * pieces,
        compiler_params=pltpu.CompilerParams(vmem_limit_bytes=VMEM_LIMIT),
        name="merge_heads",
    )(places, gain, tokens, *mixed, *weights)


def feed_kernel(parts, places_ref, *refs):
    normed_refs, grad_ref = refs[:parts], refs[parts]
    gate_refs, wide_refs = refs[parts + 1 : 2 * parts + 1], refs[2 * parts + 1 : 3 * parts + 1]
    outs, hidden_ref = refs[3 * parts + 1 : 4 * parts + 1], refs[4 * parts + 1]
    normed_all, grad_all = refs[4 * parts + 2 :]
    step_id = pl.program_id(0)
    rows, depth = normed_refs[0].shape[0], gate_refs[0].shape[0]

    @pl.when(step_id == 0)
    def _():
        for at in range(parts):
            where = slice(at * rows, (at + 1) * rows)
            for step in range(parts):
                first = pl.multiple_of(jnp.bitwise_xor(places_ref[1], step) * depth, 128)
                normed_all[step, where] = normed_refs[at][:, pl.ds(first, depth)]
        grad_all[...] = jnp.zeros_like(grad_all)

    gate, wide = None, None
    for step in range(parts):
        left = normed_all[step]
        one = jnp.dot(left, gate_refs[step][...], preferred_element_type=F32)
        two = jnp.dot(left, wide_refs[step][...], preferred_element_type=F32)
        gate, wide = (one, two) if gate is None else (gate + one, wide + two)
    hidden_grad = grad_ref[...]
    slope = jax.nn.sigmoid(gate)
    hidden_ref[...] = (gate * slope * wide).astype(BF16)
    gate_grad = (hidden_grad * wide * (slope * (1.0 + gate * (1.0 - slope)))).astype(BF16)
    wide_grad = (hidden_grad * gate * slope).astype(BF16)
    for step in range(parts):
        grad_all[step] += mm(gate_grad, gate_refs[step][...], ROWS_ROWS) + mm(
            wide_grad, wide_refs[step][...], ROWS_ROWS
        )

    @pl.when(step_id == pl.num_programs(0) - 1)
    def _():
        for at in range(parts):
            where = slice(at * rows, (at + 1) * rows)
            for step in range(parts):
                outs[at][step ^ at] = grad_all[step, where]


def feed(places, normed, hidden_grad, weights):
    rows, width = normed[0].shape
    parts = len(weights)
    depth = weights[0].shape[0]
    shard_columns = hidden_grad.shape[1]
    tile = 256 if shard_columns % 256 == 0 else shard_columns
    if tile == 256:
        sources = [(part, part) for part in weights]
        columns = weights[0].shape[1] // 2
        gate_at = lambda j, place: (0, place[1] * (shard_columns // tile) + j)
        wide_at = lambda j, place: (
            0,
            columns // tile + place[1] * (shard_columns // tile) + j,
        )
    else:
        shard = lax.axis_index("shard")
        sources = [
            (
                part_of(part[:, : part.shape[1] // 2], shard, parts, 1),
                part_of(part[:, part.shape[1] // 2 :], shard, parts, 1),
            )
            for part in weights
        ]
        gate_at = wide_at = lambda j, place: (0, j)
    whole = pl.BlockSpec((rows, width), lambda j, place: (0, 0))
    narrow = pl.BlockSpec((parts * rows, tile), lambda j, place: (0, j))
    return pl.pallas_call(
        functools.partial(feed_kernel, parts),
        grid_spec=pltpu.PrefetchScalarGridSpec(
            num_scalar_prefetch=1,
            grid=(shard_columns // tile,),
            in_specs=[whole] * parts
            + [narrow]
            + [pl.BlockSpec((depth, tile), gate_at)] * parts
            + [pl.BlockSpec((depth, tile), wide_at)] * parts,
            out_specs=[pl.BlockSpec((parts, rows, depth), lambda j, place: (0, 0, 0))] * parts
            + [narrow],
            scratch_shapes=[
                pltpu.VMEM((parts, parts * rows, depth), BF16),
                pltpu.VMEM((parts, parts * rows, depth), F32),
            ],
        ),
        out_shape=[jax.ShapeDtypeStruct((parts, rows, depth), F32)] * parts
        + [jax.ShapeDtypeStruct((parts * rows, shard_columns), BF16)],
        compiler_params=pltpu.CompilerParams(vmem_limit_bytes=VMEM_LIMIT),
        name="feed_forward",
    )(
        places,
        *normed,
        hidden_grad,
        *[source[0] for source in sources],
        *[source[1] for source in sources],
    )


def unmerge_kernel(parts, pieces, places_ref, gain_ref, middle_ref, up_ref, *refs):
    grad_refs, weight_refs = refs[:parts], refs[parts : 2 * parts]
    grad_out, sent_out, gain_out = refs[2 * parts : 2 * parts + 3]
    piece_outs = refs[2 * parts + 3 : 2 * parts + 3 + pieces]
    gathered = refs[-1]
    step_id = pl.program_id(0)
    depth = grad_refs[0].shape[2]

    @pl.when(step_id == 0)
    def _():
        for step in range(parts):
            first = pl.multiple_of(jnp.bitwise_xor(places_ref[1], step) * depth, 128)
            total = grad_refs[0][step]
            for ref in grad_refs[1:]:
                total = total + ref[step]
            grad_out[:, pl.ds(first, depth)] = total
        values, grad, gain = middle_ref[...], grad_out[...], gain_ref[...]
        scale = lax.rsqrt(jnp.mean(values * values, -1, keepdims=True) + EPS)
        unit_rows = values * scale
        weighted = grad * gain
        inner = jnp.mean(weighted * unit_rows, -1, keepdims=True)
        gain_out[...] = jnp.sum(grad * unit_rows, 0, keepdims=True)
        total = scale * (weighted - unit_rows * inner) + up_ref[...].astype(F32)
        grad_out[...] = total
        sent_out[...] = total.astype(BF16)

    count = pl.num_programs(0)
    group = gathered.shape[2]
    for step, ref in enumerate(weight_refs):
        width = ref.shape[0]
        first = jnp.bitwise_xor(places_ref[1], step) * (width * count) + step_id * width
        whose = jnp.bitwise_xor(first // group, places_ref[0])
        at = pl.multiple_of(first % group, 128) if width < group else 0
        gathered[whose, :, pl.ds(at, width)] = mm(sent_out[...], ref[...], ROWS_ROWS).astype(BF16)

    @pl.when(step_id == count - 1)
    def _():
        for at, ref in enumerate(piece_outs):
            ref[...] = gathered[at]


def unmerge(places, gain, middle, upstream, grads, weights, pieces):
    rows, width = middle.shape
    parts = len(weights)
    depth = grads[0].shape[2]
    group = VD // pieces
    tile = min(weights[0].shape[0], group)
    whole = pl.BlockSpec((rows, width), lambda j, place: (0, 0))
    one_row = pl.BlockSpec((1, width), lambda j, place: (0, 0))
    return pl.pallas_call(
        functools.partial(unmerge_kernel, parts, pieces),
        grid_spec=pltpu.PrefetchScalarGridSpec(
            num_scalar_prefetch=1,
            grid=(weights[0].shape[0] // tile,),
            in_specs=[one_row, whole, whole]
            + [pl.BlockSpec((parts, rows, depth), lambda j, place: (0, 0, 0))] * parts
            + [pl.BlockSpec((tile, width), lambda j, place: (j, 0))] * parts,
            out_specs=[whole, whole, one_row]
            + [pl.BlockSpec((rows, group), lambda j, place: (0, 0))] * pieces,
            scratch_shapes=[pltpu.VMEM((pieces, rows, group), BF16)],
        ),
        out_shape=[
            jax.ShapeDtypeStruct((rows, width), F32),
            jax.ShapeDtypeStruct((rows, width), BF16),
            jax.ShapeDtypeStruct((1, width), F32),
        ]
        + [jax.ShapeDtypeStruct((rows, group), BF16)] * pieces,
        compiler_params=pltpu.CompilerParams(vmem_limit_bytes=VMEM_LIMIT),
        name="split_heads",
    )(places, gain, middle, upstream, *grads, *weights)


def outer_kernel(parts, places_ref, *refs):
    left_refs, right_refs, out_refs = refs[:parts], refs[parts : 2 * parts], refs[2 * parts :]
    total = None
    for left, right in zip(left_refs, right_refs):
        term = mm(left[...], right[...], COLS_COLS)
        total = term if total is None else total + term
    (out_ref,) = out_refs
    chunks, several, height, _ = out_ref.shape
    for one in range(several):
        for at in range(chunks):
            first = (one * chunks + at) * height
            out_ref[at, one] = total[first : first + height].astype(out_ref.dtype)


def outer_products(places, lefts, own_right, rights, owners, chunks):
    rows, width = lefts[0].shape
    parts = len(lefts)
    columns = own_right.shape[1] // parts
    own = width // owners
    tile = max(own, 256)
    fixed = pl.BlockSpec((rows, columns), lambda j, place: (0, 0))
    return pl.pallas_call(
        functools.partial(outer_kernel, parts),
        grid_spec=pltpu.PrefetchScalarGridSpec(
            num_scalar_prefetch=1,
            grid=(width // tile,),
            in_specs=[pl.BlockSpec((rows, tile), lambda j, place: (0, j))] * parts
            + [pl.BlockSpec((rows, columns), lambda j, place: (0, place[1]))]
            + [fixed] * (parts - 1),
            out_specs=pl.BlockSpec(
                (chunks, tile // own, own // chunks, columns), lambda j, place: (0, j, 0, 0)
            ),
        ),
        out_shape=jax.ShapeDtypeStruct((chunks, owners, own // chunks, columns), BF16),
        compiler_params=pltpu.CompilerParams(vmem_limit_bytes=VMEM_LIMIT),
        name="outer_products",
    )(places, *lefts, own_right, *rights)


def rows_kernel(pieces, places_ref, *refs):
    left_refs, right_refs, out_ref, left, right = (
        refs[:pieces], refs[pieces : 2 * pieces], refs[2 * pieces], refs[-2], refs[-1],
    )
    rows = left_refs[0].shape[0]

    @pl.when(pl.program_id(0) == 0)
    def _():
        for at, ref in enumerate(left_refs):
            left[at * rows : (at + 1) * rows] = ref[...]

    for at, ref in enumerate(right_refs):
        right[at * rows : (at + 1) * rows] = ref[...]
    parts, height, _ = out_ref.shape
    for step in range(parts):
        first = pl.multiple_of(jnp.bitwise_xor(places_ref[1], step) * height, 128)
        out_ref[step] = mm(left[:, pl.ds(first, height)], right[...], COLS_COLS).astype(
            out_ref.dtype
        )


def own_rows(places, lefts, rights, parts):
    pieces = len(lefts)
    rows, columns = lefts[0].shape
    height = columns // parts
    width = rights[0].shape[1]
    tile = 512
    return pl.pallas_call(
        functools.partial(rows_kernel, pieces),
        grid_spec=pltpu.PrefetchScalarGridSpec(
            num_scalar_prefetch=1,
            grid=(width // tile,),
            in_specs=[pl.BlockSpec((rows, columns), lambda j, place: (0, 0))] * pieces
            + [pl.BlockSpec((rows, tile), lambda j, place: (0, j))] * pieces,
            out_specs=pl.BlockSpec((parts, height, tile), lambda j, place: (0, 0, j)),
            scratch_shapes=[
                pltpu.VMEM((pieces * rows, columns), BF16),
                pltpu.VMEM((pieces * rows, tile), BF16),
            ],
        ),
        out_shape=jax.ShapeDtypeStruct((parts, height, width), BF16),
        compiler_params=pltpu.CompilerParams(vmem_limit_bytes=VMEM_LIMIT),
        name="own_rows",
    )(places, *lefts, *rights)


def again_kernel(parts, places_ref, normed_ref, up_ref, *refs):
    gate_refs, wide_refs, down_ref = refs[:parts], refs[parts : 2 * parts], refs[2 * parts]
    hidden_ref, gate_out, wide_out = refs[-3:]
    depth = gate_refs[0].shape[0]
    gate, wide = None, None
    for step in range(parts):
        first = pl.multiple_of(jnp.bitwise_xor(places_ref[1], step) * depth, 128)
        left = normed_ref[:, pl.ds(first, depth)]
        one, two = mm(left, gate_refs[step][...]), mm(left, wide_refs[step][...])
        gate, wide = (one, two) if gate is None else (gate + one, wide + two)
    hidden_grad = mm(up_ref[...], down_ref[...], ROWS_ROWS)
    slope = jax.nn.sigmoid(gate)
    hidden_ref[...] = (gate * slope * wide).astype(BF16)
    gate_out[...] = (hidden_grad * wide * (slope * (1.0 + gate * (1.0 - slope)))).astype(BF16)
    wide_out[...] = (hidden_grad * gate * slope).astype(BF16)


def feed_again(places, normed, upstream, gates, wides, down, part, cut, before=()):
    width = normed.shape[1]
    count = normed.shape[0] // cut
    parts = len(gates)
    depth, columns = gates[0].shape
    tile = 256
    rows = pl.BlockSpec((tile, width), lambda j, place: (part * (count // tile) + j, 0))
    narrow = pl.BlockSpec((tile, columns), lambda j, place: (part * (count // tile) + j, 0))
    carried = 1 + 2 + 2 * parts + 1
    fixed = pl.BlockSpec((depth, columns), lambda j, place: (0, 0))
    return pl.pallas_call(
        functools.partial(again_kernel, parts),
        grid_spec=pltpu.PrefetchScalarGridSpec(
            num_scalar_prefetch=1,
            grid=(count // tile,),
            in_specs=[rows, rows]
            + [fixed] * (2 * parts)
            + [pl.BlockSpec((columns, width), lambda j, place: (0, 0))]
            + [pl.BlockSpec(memory_space=pl.ANY)] * len(before),
            out_specs=[narrow] * 3,
        ),
        out_shape=[jax.ShapeDtypeStruct((normed.shape[0], columns), BF16)] * 3,
        input_output_aliases={carried + at: at for at in range(len(before))},
        compiler_params=pltpu.CompilerParams(vmem_limit_bytes=VMEM_LIMIT),
        name="feed_again",
    )(places, normed, upstream, *gates, *wides, down, *before)


def place_in_kernel(columns_of, head_of, in_ref, out_ref, held, sems):
    step_id = pl.program_id(0)
    slot = lax.rem(step_id, 2)

    def copies(which, where):
        found = []
        for number, (low, width, first) in enumerate(columns_of):
            at = pl.multiple_of(first + head_of(which) * width, 128)
            found.append(
                pltpu.make_async_copy(
                    held.at[where, :, pl.ds(low, width)],
                    out_ref.at[:, pl.ds(at, width)],
                    sems.at[where, number],
                )
            )
        return found

    @pl.when(step_id >= 2)
    def _():
        for copy in copies(step_id - 2, slot):
            copy.wait()

    held[slot] = in_ref[:, 0].astype(F32).reshape(held.shape[1:])
    for copy in copies(step_id, slot):
        copy.start()

    @pl.when(step_id == pl.num_programs(0) - 1)
    def _():
        for copy in copies(step_id - 1, 1 - slot) + copies(step_id, slot):
            copy.wait()


def place_in(value, seqs):
    blocks, sources, rows, columns = value.shape
    heads = HEADS // seqs
    per_source = columns // HEAD_WIDTH
    columns_of = [(0, DK, 0), (DK, DK, KD), (2 * DK, DV, 2 * KD), (2 * DK + DV, DV, CONVW)]

    def head_of(step):
        source = step // per_source
        return source % seqs * heads + source // seqs * per_source + step % per_source

    return pl.pallas_call(
        functools.partial(place_in_kernel, columns_of, head_of),
        grid=(sources * per_source,),
        in_specs=[
            pl.BlockSpec(
                (blocks, 1, rows, HEAD_WIDTH), lambda h: (0, h // per_source, 0, h % per_source)
            )
        ],
        out_specs=pl.BlockSpec(memory_space=pl.ANY),
        out_shape=jax.ShapeDtypeStruct((blocks * rows, PROJW), F32),
        scratch_shapes=[
            pltpu.VMEM((2, blocks * rows, HEAD_WIDTH), F32),
            pltpu.SemaphoreType.DMA((2, len(columns_of))),
        ],
        compiler_params=pltpu.CompilerParams(vmem_limit_bytes=VMEM_LIMIT),
        name="place_w_in",
    )(value)


def place_gu_kernel(half, gate_ref, wide_ref, out_ref):
    def put(ref):
        width = ref.shape[2]
        for at in range(ref.shape[0]):
            out_ref[:, at * width : (at + 1) * width] = ref[at].astype(F32)

    @pl.when(pl.program_id(0) < half)
    def _():
        put(gate_ref)

    @pl.when(pl.program_id(0) >= half)
    def _():
        put(wide_ref)


def place_gu(gate, wide):
    sources, rows, width = gate.shape
    together = 1
    while together * width % 128:
        together *= 2
    half = sources // together
    return pl.pallas_call(
        functools.partial(place_gu_kernel, half),
        grid=(2 * half,),
        in_specs=[
            pl.BlockSpec((together, rows, width), lambda j: (jnp.minimum(j, half - 1), 0, 0)),
            pl.BlockSpec((together, rows, width), lambda j: (jnp.maximum(j - half, 0), 0, 0)),
        ],
        out_specs=pl.BlockSpec((rows, together * width), lambda j: (0, j)),
        out_shape=jax.ShapeDtypeStruct((rows, 2 * sources * width), F32),
        compiler_params=pltpu.CompilerParams(vmem_limit_bytes=VMEM_LIMIT),
        name="place_w_gu",
    )(gate, wide)


def line_first(value):
    return lax.ppermute(value, "replica", [(0, 1), (3, 2)])


def line_second(value):
    return lax.ppermute(value, "replica", [(1, 2), (2, 1)])


def line_third(value):
    return lax.ppermute(value, "replica", [(1, 0), (2, 3)])


def added(left, right):
    return (left.astype(F32) + right.astype(F32)).astype(BF16)


def pinned(*values):
    return lax.optimization_barrier(values)


def line_sum(value):
    value = added(value, line_first(value))
    value = added(value, line_second(value))
    return settled_pair((value, line_third(value)))


def settled_pair(pair):
    place = lax.axis_index("replica")
    return jnp.where((place == 1) | (place == 2), pair[0], pair[1]).astype(F32)


def swapped(value, axis, step):
    count = lax.axis_size(axis)
    return lax.ppermute(value, axis, [(source, source ^ step) for source in range(count)])


def around(value, axis):
    return [value] + [swapped(value, axis, step) for step in range(1, lax.axis_size(axis))]


def settled(parts, index):
    stacked = jnp.stack(parts)
    return [
        lax.dynamic_index_in_dim(stacked, jnp.bitwise_xor(index, at), 0, keepdims=False)
        for at in range(len(parts))
    ]


def part_of(value, index, count, axis):
    width = value.shape[axis] // count
    return lax.dynamic_slice_in_dim(value, index * width, width, axis)


def dot(left, right):
    return jnp.dot(left, right, preferred_element_type=F32)


def dot_rows(left, right):
    return lax.dot_general(left, right, (((1,), (1,)), ((), ())), preferred_element_type=F32)


def dot_cols(left, right):
    return lax.dot_general(left, right, (((0,), (0,)), ((), ())), preferred_element_type=F32)


def rms_parts(values):
    return lax.rsqrt(jnp.mean(values * values, -1, keepdims=True) + EPS)


def rms_back(values, scale, gain, grad):
    weighted = grad * gain
    unit_rows = values * scale
    inner = jnp.mean(weighted * unit_rows, -1, keepdims=True)
    return scale * (weighted - unit_rows * inner), jnp.sum(grad * unit_rows, 0)


def body(
    tokens,
    cotangent,
    lengths,
    norm_gains,
    w_in,
    w_ab,
    conv_weight,
    gate_params,
    onorm_gain,
    w_o,
    w_gu,
    w_down,
):
    shards, seqs, replicas = (lax.axis_size(name) for name in EVERY)
    shard, seq = lax.axis_index("shard"), lax.axis_index("seq")
    owners = shards * seqs
    owner = shard * seqs + seq
    micro, row = tokens.shape[0], tokens.shape[1]
    flat = micro * row
    length = row * seqs
    heads = HEADS // seqs
    depth = D // shards
    seq_place = jnp.reshape(seq, (1,)).astype(jnp.int32)
    shard_place = jnp.reshape(shard, (1,)).astype(jnp.int32)
    places = jnp.stack([seq, shard]).astype(jnp.int32)

    def blocks(value, count, axis=1):
        return [part_of(value, jnp.bitwise_xor(shard, step), count, axis) for step in range(count)]

    flat_tokens = tokens.reshape(flat, D)
    in_own = pick_heads(seq_place, w_in, heads)
    sent_tokens, in_own = pinned(flat_tokens, in_own)
    pieces = around(sent_tokens, "seq")
    gain_parts = around(norm_gains, "shard")
    in_parts = around(in_own, "shard")
    taps_parts = around(conv_weight, "shard")
    ab_parts = around(w_ab, "shard")
    gains = jnp.concatenate(settled(gain_parts, shard), 1).astype(F32)
    gain_first, gain_second = gains[:1], gains[1:]
    taps = jnp.concatenate(settled(taps_parts, shard), 1)
    upstream = cotangent.reshape(flat, D)
    up_parts = around(upstream, "shard")
    hidden_grad = dot_rows(jnp.concatenate(up_parts, 0), w_down)
    own_out, own_gu, late_up, hidden_grad, *arrived = pinned(
        w_o, w_gu, upstream, hidden_grad, *pieces, *in_parts
    )
    pieces, in_parts = arrived[:seqs], arrived[seqs:]
    all_up = lax.all_gather(late_up, EVERY, axis=0, tiled=True)
    out_parts = around(own_out, "shard")
    gu_parts = around(own_gu, "shard")

    normed, projected = project(shard_place, gain_first, pieces, in_parts)
    rate_in = sum(dot(left, right) for left, right in zip(blocks(normed, shards), ab_parts))
    rate_in = part_of(rate_in.reshape(seqs, micro, row, 2, HEADS), seq, seqs, 4)
    rate_in = jnp.stack(settled(list(rate_in), seq))
    rate_in = jnp.transpose(rate_in, (3, 1, 4, 0, 2)).reshape(2, micro, heads, length)
    position = jnp.arange(length, dtype=jnp.int32)
    valid = (position[None, :] < lengths[:, None]).astype(F32)[:, None, :]
    own_params = part_of(gate_params, seq, seqs, 1)[:, None, :, None]
    rate_shifted = rate_in[0] + own_params[1]
    decays = -jnp.exp(own_params[0]) * jax.nn.softplus(rate_shifted) * valid
    written = jax.nn.sigmoid(rate_in[1])
    rates = jnp.stack([jnp.maximum(decays, LOWEST_DECAY), written * valid], 2)
    rates = jnp.pad(rates, ((0, 0), (0, 0), (0, SMALL_ROWS - 2), (0, 0)))
    gain_row = onorm_gain.reshape(1, DV)
    projected = projected.reshape(seqs, micro, row, -1)
    *gated, inverse, update = mixer_forward(seq_place, projected, taps, rates, gain_row, 2)
    gated = [item.reshape(flat, heads * DV) for item in gated]

    mixed_parts = [gated[0]] + [swapped(gated[step], "seq", step) for step in range(1, seqs)]
    arrived = pinned(*mixed_parts, *gu_parts)
    mixed_parts, gu_parts = list(arrived[:seqs]), list(arrived[seqs:])
    middle, renormed, *mixed_left = merge(
        places, gain_second, flat_tokens, mixed_parts, out_parts
    )
    all_renormed = lax.all_gather(renormed, EVERY, axis=0, tiled=True)

    mixed_left = [
        swapped(item, "seq", step) if step else item for step, item in enumerate(mixed_left)
    ]
    fed = feed(places, around(renormed, "shard"), hidden_grad, gu_parts)
    pair = len(fed)
    fed = list(pinned(*fed, *mixed_left))
    fed, mixed_left = fed[:pair], fed[pair:]
    grads_back = [fed[0]] + [swapped(fed[step], "shard", step) for step in range(1, shards)]
    middle_grad, mixed_grad, gain2_grad, *gated_grad = unmerge(
        places, gain_second, middle, upstream, grads_back, out_parts, seqs
    )
    hidden = fed[shards]

    ff_own = FF // owners
    own_down = part_of(w_down, seq, seqs, 0)
    own_gate = [part_of(part, owner, 2 * owners, 1) for part in gu_parts]
    own_wide = [part_of(part, owners + owner, 2 * owners, 1) for part in gu_parts]

    gated_grad = [
        swapped(item, "seq", step) if step else item for step, item in enumerate(gated_grad)
    ]
    mixed_grad, own_down, *others = pinned(
        mixed_grad, own_down, *own_gate, *own_wide, *mixed_left, *gated_grad
    )
    own_gate, own_wide = others[:shards], others[shards : 2 * shards]
    mixed_left, gated_grad = others[2 * shards : 2 * shards + seqs], others[2 * shards + seqs :]
    gated_grad = [item.reshape(micro, row, heads * DV) for item in gated_grad]
    mid_pieces = around(mixed_grad, "seq")
    proj_grad, small_grad = mixer_backward(
        seq_place, projected, taps, rates, gain_row, inverse, update, gated_grad, 1
    )
    proj_grad, *mid_pieces = pinned(proj_grad, *mid_pieces)
    rows_all = seqs * flat
    proj_grad = proj_grad.reshape(rows_all, -1)
    pair_proj = [
        swapped(part_of(proj_grad, jnp.bitwise_xor(shard, step), shards, 1), "shard", step)
        for step in range(1, shards)
    ]

    def to_group(value):
        return lax.all_to_all(value, GROUP, split_axis=0, concat_axis=0, tiled=False)

    pair_normed = around(normed, "shard")
    grad_in = outer_products(places, pair_normed, proj_grad, pair_proj, owners, replicas)
    width = grad_in.shape[3]
    proj_grad, small_grad, grad_in, *mid_pieces = pinned(
        proj_grad, small_grad, grad_in, *mid_pieces
    )

    grad_out = own_rows(places, mixed_left, mid_pieces, shards)
    grad_out = functools.reduce(
        added, [grad_out[0]] + [swapped(grad_out[step], "shard", step) for step in range(1, shards)]
    )

    def input_gradient_parts(proj_grad, small_grad):
        decay_grad = small_grad[:, :, 5, :length]
        write_grad = small_grad[:, :, 6, :length]
        shifted_grad = decay_grad * -jnp.exp(own_params[0]) * jax.nn.sigmoid(rate_shifted) * valid
        params_grad = jnp.stack(
            [jnp.sum(decay_grad * decays, (0, 2)), jnp.sum(shifted_grad, (0, 2))]
        )
        rate_grad = jnp.stack([shifted_grad, write_grad * written * (1.0 - written) * valid])
        rate_grad = jnp.transpose(rate_grad.reshape(2, micro, heads, seqs, row), (3, 1, 4, 0, 2))
        rate_grad = jnp.stack(settled(list(rate_grad), seq))
        rate_grad = rate_grad.reshape(rows_all, 2 * heads)
        grad_ab = lax.dot_general(
            rate_grad, normed.astype(F32), (((0,), (0,)), ((), ())), precision=HIGHEST
        )
        own_ab = [
            part_of(part.reshape(depth, 2, HEADS), seq, seqs, 2).reshape(depth, 2 * heads)
            for part in ab_parts
        ]
        normed_grad = [
            dot_rows(proj_grad, part)
            + lax.dot_general(
                rate_grad, ab.astype(F32), (((1,), (1,)), ((), ())), precision=HIGHEST
            )
            for part, ab in zip(in_parts, own_ab)
        ]
        return (*normed_grad, grad_ab, params_grad)

    def input_gradient(*normed_grad):
        *normed_grad, grad_ab, params_grad = normed_grad
        normed_grad = jnp.concatenate(settled(normed_grad, shard), 1).reshape(seqs, flat, D)
        normed_grad = normed_grad[0] + sum(
            swapped(normed_grad[step].astype(BF16), "seq", step).astype(F32)
            for step in range(1, seqs)
        )
        flat_in = flat_tokens.astype(F32)
        inputs_grad, gain1_grad = rms_back(flat_in, rms_parts(flat_in), gains[0], normed_grad)
        input_grads = (inputs_grad + middle_grad).astype(BF16).reshape(micro, row, D)
        return input_grads, gain1_grad, grad_ab, params_grad

    def to_group(value):
        return lax.all_to_all(value, GROUP, split_axis=0, concat_axis=0, tiled=False)

    def to_owners(value):
        return to_group(value.astype(BF16).reshape(owners, D // owners, ff_own))

    grad_out, proj_grad, small_grad = pinned(grad_out, proj_grad, small_grad)
    grad_out = lax.all_to_all(
        grad_out.reshape(replicas, -1, D), "replica", split_axis=0, concat_axis=0
    )
    normed_parts = input_gradient_parts(proj_grad, small_grad)
    grad_out, grad_in, all_renormed, all_up, *normed_parts = pinned(
        grad_out, grad_in, all_renormed, all_up, *normed_parts
    )
    grad_in = lax.psum_scatter(grad_in, "replica", scatter_dimension=0, tiled=False)
    input_grads, gain1_grad, grad_ab, params_grad = input_gradient(*normed_parts)
    gain2_grad = gain2_grad[0]
    taps_grad = jnp.sum(small_grad[:, :, :KERNEL], 0)
    conv_grad = jnp.concatenate(
        [
            jnp.swapaxes(taps_grad[..., low:high], 0, 1).reshape(KERNEL, -1)
            for low, high in ((0, DK), (DK, 2 * DK), (2 * DK, 2 * DK + DV))
        ],
        1,
    )
    onorm_grad = jnp.sum(small_grad[:, :, 4, :DV], (0, 1))
    loose = jnp.concatenate([onorm_grad, params_grad.reshape(-1)])
    loose = jnp.pad(loose, (0, D - loose.size))
    rows_ab = 2 * heads
    smalls = jnp.concatenate(
        [grad_ab, conv_grad, loose[None], gain1_grad[None], gain2_grad[None]], 0
    )
    step = 1
    while step < shards:
        smalls = smalls + swapped(smalls, "shard", step)
        step *= 2
    all_renormed, all_up, smalls, input_grads = pinned(
        all_renormed, all_up, smalls, input_grads
    )
    grad_out = jnp.sum(grad_out.astype(F32), 0).astype(BF16)
    own_hidden, gate_grad, wide_grad = feed_again(
        places, all_renormed, all_up, own_gate, own_wide, own_down, 0, 1
    )
    grad_gate = dot_cols(all_renormed, gate_grad).astype(BF16)
    grad_out, grad_in, grad_gate, wide_grad, own_hidden = pinned(
        grad_out, grad_in, grad_gate, wide_grad, own_hidden
    )
    grad_out = lax.all_gather(grad_out, "replica", axis=0, tiled=True)
    grad_in = to_group(grad_in)
    grad_wide = dot_cols(all_renormed, wide_grad).astype(BF16)
    grad_out, grad_in, grad_gate, grad_wide, own_hidden, hidden, smalls = pinned(
        grad_out, grad_in, grad_gate, grad_wide, own_hidden, hidden, smalls
    )
    grad_in = lax.all_gather(grad_in, "replica", axis=0)
    grad_gate = to_owners(grad_gate)
    grad_down = dot_cols(own_hidden, all_up)
    grad_wide, grad_gate = pinned(grad_wide, grad_gate)
    grad_wide = to_owners(grad_wide)
    step = 1
    while step < replicas:
        smalls = smalls + swapped(smalls, "replica", step)
        step *= 2
    rows_down = dot(hidden, w_down).reshape(shards, flat, D)
    result = (
        middle
        + rows_down[0]
        + sum(swapped(rows_down[step], "shard", step) for step in range(1, shards))
    )
    results = result.astype(BF16).reshape(micro, row, D)
    grad_out = grad_out.astype(F32)
    every = jnp.stack(settled(around(smalls, "seq"), seq))
    grad_gu = place_gu(grad_gate, grad_wide)
    if width % HEAD_WIDTH == 0:
        grad_in = place_in(grad_in, seqs)
    else:
        grad_in = grad_in.reshape(replicas, shards, seqs, -1, width)
        grad_in = jnp.transpose(grad_in, (0, 3, 2, 1, 4)).reshape(D // owners, HEADS, HEAD_WIDTH)
        cuts = (0, DK, 2 * DK, 2 * DK + DV, HEAD_WIDTH)
        grad_in = jnp.concatenate(
            [
                grad_in[..., low:high].reshape(D // owners, -1)
                for low, high in zip(cuts[:-1], cuts[1:])
            ],
            1,
        ).astype(F32)

    ab_total = jnp.transpose(every[:, :rows_ab].reshape(seqs, 2, heads, D), (3, 1, 0, 2))
    ab_total = ab_total.reshape(D, 2 * HEADS)
    conv_all = every[:, rows_ab : rows_ab + KERNEL]
    conv_total = jnp.concatenate(
        [
            jnp.swapaxes(conv_all[..., low:high], 0, 1).reshape(KERNEL, -1)
            for low, high in (
                (0, heads * DK),
                (heads * DK, 2 * heads * DK),
                (2 * heads * DK, heads * (2 * DK + DV)),
            )
        ],
        1,
    )
    loose_all = every[:, rows_ab + KERNEL]
    onorm_total = jnp.sum(loose_all[:, :DV], 0)
    params_total = loose_all[:, DV : DV + 2 * heads].reshape(seqs, 2, heads)
    params_total = jnp.swapaxes(params_total, 0, 1).reshape(2, HEADS)
    gains_total = jnp.sum(every[:, rows_ab + KERNEL + 1 : rows_ab + KERNEL + 3], 0)
    gains_own = part_of(gains_total, owner, owners, 1)
    ab_own = part_of(ab_total, owner, owners, 0)
    conv_own = part_of(conv_total, owner, owners, 1)
    return (
        results,
        input_grads,
        gains_own,
        grad_in,
        ab_own,
        conv_own,
        params_total,
        onorm_total,
        grad_out,
        grad_gu,
        grad_down,
    )


def solution(mesh):
    in_specs = (
        P(("shard", "replica"), "seq", None),
        P(("shard", "replica"), "seq", None),
        P(("shard", "replica")),
        P(None, "shard"),
        P("shard", None),
        P("shard", None),
        P(None, "shard"),
        P(),
        P(),
        P("shard", None),
        P("shard", None),
        P("shard", None),
    )
    out_specs = (
        P(("shard", "replica"), "seq", None),
        P(("shard", "replica"), "seq", None),
        P(None, ("shard", "seq")),
        P(("shard", "seq"), None),
        P(("shard", "seq"), None),
        P(None, ("shard", "seq")),
        P(),
        P(),
        P(("shard", "seq"), None),
        P(("shard", "seq"), None),
        P(("shard", "seq"), None),
    )
    return jax.shard_map(body, mesh=mesh, in_specs=in_specs, out_specs=out_specs, check_vma=False)
```

time: 1200 us -> 636 us (0.53)
  waiting for transfers between devices: 527 us -> 195 us
  matrix products: 249 us -> 91.7 us
  Pallas kernels: 67.1 us -> 200 us
  local copies, waits for them, and re-layouts: 155 us -> 53.1 us
  blocking collectives: 77.3 us -> 0 us
  other arithmetic: 74.6 us -> 25.8 us
  starting transfers between devices: 26.9 us -> 48.1 us
    pallas_call x0 -> x10, Pallas kernels: none -> 157 us  [the longest x1 50 us: feed_again(): pl.pallas_call(functools.partial(again_kernel, parts), grid_spec=pltpu.Pr...]
    all_gather x2, waiting for transfers between devices: 113 us -> 23.6 us  [the longest x1 23.6 us: body(): grad_out = lax.all_gather(grad_out, 'replica', axis=0, tiled=True)]
    psum x2 -> x0, waiting for transfers between devices: 81.1 us -> none  [the longest x1 44 us: body(): lax.psum((wide_params, onorm_grad, jnp.stack([gain1_grad, gain2_grad]), c...]
    dot_general x10 -> x3, matrix products: 90.1 us -> 9.75 us  [dot(): return jnp.dot(left, right, preferred_element_type=F32)]
    all_gather x1, waiting for transfers between devices: 95.9 us -> 20.3 us  [body(): grad_in = lax.all_gather(grad_in, 'replica', axis=0)]
    reduce_scatter x1, waiting for transfers between devices: 74.5 us -> 2.71 us  [body(): lax.psum_scatter(grad_in, 'replica', scatter_dimension=0, tiled=False)]
    all_gather x1, waiting for transfers between devices: 59.9 us -> 0.01 us  [body(): all_renormed = lax.all_gather(renormed, EVERY, axis=0, tiled=True)]
    slice x21 -> x6, local copies, waits for them, and re-layouts: 54 us -> 3.61 us  [the longest x1 1.15 us: body(): rows_down[step]]
  transfers between devices with their start and end apart: 30 -> 46, of which waited for: 17 -> 19; matrix products, arithmetic and copies ran while one was open for 27% -> 26% of each run, Pallas kernels for 6% -> 29%
where the time goes in v2:
time: 636 us; the launch traced here: 628 us
  Pallas kernels  200 us (31%)
  waiting for transfers between devices  195 us (31%)
  matrix products  91.7 us (14%)
  local copies, waits for them, and re-layouts  53.1 us (8%)
  starting transfers between devices  48.1 us (8%)
  other arithmetic  25.8 us (4%)
  between operations  14.7 us (2%)
    ppermute x37, waiting for transfers between devices, swapped(): lax.ppermute(value, axis, [(source, source ^ step) for source in range(co...  70.8 us
    all_to_all x1, waiting for transfers between devices, body(): lax.all_to_all(grad_out.reshape(replicas, -1, D), 'replica', split_axis=0...  58.9 us
    dot_general x3, matrix products, dot_cols(): lax.dot_general(left, right, (((0,), (0,)), ((), ())), preferred_element_...  57.3 us
    pallas_call x1, Pallas kernels, feed_again(): pl.pallas_call(functools.partial(again_kernel, parts), grid_spec=pltpu.Pr...  50 us
    ppermute x37, starting transfers between devices, swapped(): lax.ppermute(value, axis, [(source, source ^ step) for source in range(co...  30.6 us
    all_gather x1, waiting for transfers between devices, body(): grad_out = lax.all_gather(grad_out, 'replica', axis=0, tiled=True)  23.6 us
    pallas_call x1, Pallas kernels, mixer_forward(): pl.pallas_call(forward_kernel, grid_spec=pltpu.PrefetchScalarGridSpec(num...  22.4 us
    pallas_call x1, Pallas kernels, feed(): pl.pallas_call(functools.partial(feed_kernel, parts), grid_spec=pltpu.Pre...  21.8 us
  transfers between devices with their start and end apart: 46, of which 19 were waited for; matrix products, arithmetic and copies ran while one was open for 26% of the time, Pallas kernels for 29%

profile of v2, /device:TPU:0, one launch (start us, length us, event | category | flops | bytes accessed | tf_op | source)
XLA Modules:
  0.0 627.5 jit_solution(9684635805365553776)
XLA Ops:
  7.3 6.1 pick_heads.1.refs_4_
  13.9 2.9 collective-permute-start.2
  18.4 3.0 collective-permute-done.1
  21.4 9.0 %fusion.10.refs_2_ = f32[256,2816]{1,0:T(8,128)} fusion(bf16[2816,2048]{1,0:T(8,128)(2,1)} %param.23, bf16[128,2048]{1,0:T(8,128)(2,1)S(1)} %collective-permute-done.1, bf16[128,2048]{1,0:T(8,128)(2,1)S(1)} %bitcast.169), kind=kOutput, calls=%fused_computation.28 | convolution fusion | flops 2954887168 | bytes 15466496 | tf_op jit(solution)/shard_map/dot_general | solution.py:986
  30.5 11.3 %collective-permute-done.3.refs_2_ = bf16[128,2048]{1,0:T(8,128)(2,1)S(1)} collective-permute-done((bf16[128,2048]{1,0:T(8,128)(2,1)S(1)}, bf16[128,2048]{1,0:T(8,128)(2,1)S(1)}, u32[]{:S(2)}, u32[]{:S(2)}) %collective-permute-start.3) | collective-permute-done | bytes 524320 | tf_op jit(solution)/shard_map/ppermute | solution.py:961
  43.2 5.4 collective-permute-done
  50.0 12.9 %project.1 = (bf16[512,2048]{1,0:T(8,128)(2,1)}, f32[512,3072]{1,0:T(8,128)}) custom-call(s32[1]{0:T(128)} %bitcast.1.place_ref, f32[1,2048]{1,0:T(1,128)} %get-tuple-element.267.gain_ref, bf16[128,2048]{1,0:T(8,128)(2,1)} %bitcast.150, bf16[128,2048]{1,0:T(8,128)(2,1)} %copy-done.15, bf16[128,2048]{1,0:T(8,128)(2,1)} %copy-done.16, ...), custom_call_target="tpu_custom_call" | custom-call | tf_op jit(solution)/shard_map/project/pallas_call | solution.py:433
  67.5 22.4 %mixer_forward.1 = (bf16[2,64,1024]{2,1,0:T(8,128)(2,1)}, bf16[2,64,1024]{2,1,0:T(8,128)(2,1)}, bf16[2,64,1024]{2,1,0:T(8,128)(2,1)}, bf16[2,64,1024]{2,1,0:T(8,...) custom-call(s32[1]{0:T(128)} %bitcast.place_ref, f32[4,2,64,3072]{3,2,1,0:T(8,128)} %bitcast.148, ...), custom_call_target="tpu_custom_call" | custom-call | tf_op jit(solution)/shard_map/mixer_forward/pallas_call | solution.py:323
  94.1 6.2 collective-permute-done.10.refs_3_
  100.3 5.1 collective-permute-done.8.refs_1_
  106.2 11.1 %merge_heads.1 = (f32[128,2048]{1,0:T(8,128)}, bf16[128,2048]{1,0:T(8,128)(2,1)}, bf16[128,1024]{1,0:T(8,128)(2,1)}, bf16[128,1024]{1,0:T(8,128)(2,1)}, bf16[128...) custom-call(s32[2]{0:T(128)} %pad_add_fusion.places_ref, f32[1,2048]{1,0:T(1,128)} %get-tuple-element.268.gain_ref, ...), custom_call_target="tpu_custom_call" | custom-call | tf_op jit(solution)/shard_map/merge_heads/pallas_call | solution.py:509
  121.7 21.8 %feed_forward.1 = (f32[2,128,1024]{2,1,0:T(8,128)}, f32[2,128,1024]{2,1,0:T(8,128)}, bf16[256,2816]{1,0:T(8,128)(2,1)}) custom-call(s32[2]{0:T(128)} %pad_add_fusion.places_ref, bf16[128,2048]{1,0:T(8,128)(2,1)} %get-tuple-element.141.refs_0_, bf16[128,2048]{1,0:T(8,128)(2,1)} %copy-done.14, f32[256,2816]{1,0:T(8,128)} %fusion.10.refs_2_, ...), custom_call_target="tpu_custom_call" | custom-call | tf_op jit(solution)/shard_map/feed_forward/pallas_call | solution.py:601
  145.6 3.8 constant_dynamic-slice_fusion.15.refs_4_
  150.3 13.4 %split_heads.1 = (f32[128,2048]{1,0:T(8,128)}, bf16[128,2048]{1,0:T(8,128)(2,1)}, f32[1,2048]{1,0:T(1,128)}, bf16[128,1024]{1,0:T(8,128)(2,1)}, bf16[128,1024]{1...) custom-call(s32[2]{0:T(128)} %pad_add_fusion.places_ref, f32[1,2048]{1,0:T(1,128)} %get-tuple-element.268.gain_ref, ...), custom_call_target="tpu_custom_call" | custom-call | tf_op jit(solution)/shard_map/split_heads/pallas_call | solution.py:679
  167.2 9.4 %constant_dynamic-slice_fusion.11 = (bf16[1024,704]{1,0:T(8,128)(2,1)}, bf16[1024,704]{1,0:T(8,128)(2,1)}, bf16[1024,704]{1,0:T(8,128)(2,1)}, bf16[1024,704]{1,0:T(8,128)(2,1)}) fusion(bf16[1024,11264]{1,0:T(8,128)(2,1)} %collective-permute-done.11.refs_4_.refs_6_, s32[]{:T(128)S(6)} %select_n.108, s32[]{:T(128)S(6)} %select_n.107, bf16[1024,11264]{1,0:T(8,128)(2,1)} %refs_5_), kind=kLoop, calls=%fused_computation.96 | loop fusion | bytes 11534344 | tf_op jit(solution)/shard_map/dynamic_slice | solution.py:978
  183.0 20.2 %mixer_backward.1 = (bf16[4,2,64,3072]{3,2,1,0:T(8,128)(2,1)}, f32[2,4,8,512]{3,2,1,0:T(8,128)}) custom-call(s32[1]{0:T(128)} %bitcast.place_ref, f32[4,2,64,3072]{3,2,1,0:T(8,128)} %bitcast.149, bf16[4,8192]{1,0:T(4,128)(2,1)} %pad_maximum_fusion.4.taps_q.taps_k.taps_v, bf16[4,8192]{1,0:T(4,128)(2,1)} %pad_maximum_fusion.4.taps_q.taps_k.taps_v, ...), custom_call_target="tpu_custom_call" | custom-call | tf_op jit(solution)/shard_map/mixer_backward/pallas_call | solution.py:349
  203.2 9.4 %collective-permute-done.23.refs_7_ = bf16[128,2048]{1,0:T(8,128)(2,1)} collective-permute-done((bf16[128,2048]{1,0:T(8,128)(2,1)S(1)}, bf16[128,2048]{1,0:T(8,128)(2,1)}, u32[]{:S(2)}, u32[]{:S(2)}) %collective-permute-start.23) | collective-permute-done | bytes 524320 | tf_op jit(solution)/shard_map/ppermute | solution.py:961
  214.3 3.4 collective-permute-done.25.refs_3_
  218.8 12.8 %outer_products.1 = bf16[4,8,64,1536]{3,2,1,0:T(8,128)(2,1)} custom-call(s32[2]{0:T(128)} %pad_add_fusion.places_ref, bf16[512,2048]{1,0:T(8,128)(2,1)} %get-tuple-element.129.refs_0_, bf16[512,2048]{1,0:T(8,128)(2,1)} %collective-permute-done.24.refs_1_, bf16[512,3072]{1,0:T(8,128)(2,1)} %bitcast.158, bf16[512,1536]{1,0:T(8,128)(2,1)} %copy-done.12), custom_call_target="tpu_custom_call" | custom-call | tf_op jit(solution)/shard_map/outer_products/pallas_call | solution.py:723
  231.6 7.1 %own_rows.1 = bf16[2,512,2048]{2,1,0:T(8,128)(2,1)} custom-call(s32[2]{0:T(128)} %pad_add_fusion.places_ref, bf16[128,1024]{1,0:T(8,128)(2,1)} %get-tuple-element.163.refs_0_, bf16[128,1024]{1,0:T(8,128)(2,1)} %copy-done.26, bf16[128,1024]{1,0:T(8,128)(2,1)} %copy-done.27, bf16[128,1024]{1,0:T(8,128)(2,1)} %copy-done.28, ...), custom_call_target="tpu_custom_call" | custom-call | tf_op jit(solution)/shard_map/own_rows/pallas_call | solution.py:768
  238.7 3.8 slice_bitcast_fusion
  243.6 3.5 collective-permute-done.26
  247.1 3.7 fusion.1
  251.1 4.6 all-to-all-start
  259.8 7.9 %convolution_add_fusion = f32[512,1024]{1,0:T(8,128)} fusion(f32[512,1024]{1,0:T(8,128)S(1)} %fusion.52, bf16[512,3072]{1,0:T(8,128)(2,1)S(1)} %bitcast.159, bf16[1024,3072]{1,0:T(8,128)(2,1)} %collective-permute-done.5.refs_5_), kind=kOutput, calls=%fused_computation.20 | convolution fusion | flops 3221749760 | bytes 13631488 | tf_op jit(solution)/shard_map/dot_general | solution.py:986
  267.7 4.8 convolution_add_fusion.1
  272.5 58.9 %all-to-all-done = bf16[4,128,2048]{2,1,0:T(8,128)(2,1)} async-done(((bf16[4,128,2048]{2,1,0:T(8,128)(2,1)}), bf16[4,128,2048]{2,1,0:T(8,128)(2,1)}, u32[]{:S(2)}, u32[]{:S(2)}) %all-to-all-start) | async-done | bytes 2097184 | tf_op jit(solution)/shard_map/all_to_all | solution.py:1182
  331.9 3.2 fusion.5
  341.2 2.9 reduce_sum.95
  344.1 8.6 %collective-permute-done.27 = bf16[128,2048]{1,0:T(8,128)(2,1)} collective-permute-done((bf16[128,2048]{1,0:T(8,128)(2,1)}, bf16[128,2048]{1,0:T(8,128)(2,1)}, u32[]{:S(2)}, u32[]{:S(2)}) %collective-permute-start.27) | collective-permute-done | bytes 524320 | tf_op jit(solution)/shard_map/ppermute | solution.py:961
  352.7 11.3 %collective-permute-done.28 = bf16[128,2048]{1,0:T(8,128)(2,1)} collective-permute-done((bf16[128,2048]{1,0:T(8,128)(2,1)}, bf16[128,2048]{1,0:T(8,128)(2,1)}, u32[]{:S(2)}, u32[]{:S(2)}) %collective-permute-start.28) | collective-permute-done | bytes 524320 | tf_op jit(solution)/shard_map/ppermute | solution.py:961
  369.8 50.0 %feed_again.1 = (bf16[4096,704]{1,0:T(8,128)(2,1)}, bf16[4096,704]{1,0:T(8,128)(2,1)}, bf16[4096,704]{1,0:T(8,128)(2,1)}) custom-call(s32[2]{0:T(128)} %pad_add_fusion.places_ref, bf16[4096,2048]{1,0:T(8,128)(2,1)} %all-gather.6.cloned.1.call-done.normed_ref, bf16[4096,2048]{1,0:T(8,128)(2,1)} %all-gather.8.cloned.1.call-done.up_ref, ...), custom_call_target="tpu_custom_call" | custom-call | tf_op jit(solution)/shard_map/feed_again/pallas_call | solution.py:814
  419.8 18.7 %convolution_convert_fusion.1 = bf16[2048,704]{0,1:T(8,128)(2,1)} fusion(bf16[4096,2048]{1,0:T(8,128)(2,1)} %all-gather.6.cloned.1.call-done.normed_ref, bf16[4096,704]{1,0:T(8,128)(2,1)} %get-tuple-element.209), kind=kOutput, calls=%fused_computation.11 | convolution fusion | flops 11812601856 | bytes 25427968 | tf_op jit(solution)/shard_map/dot_general | solution.py:990
  441.3 3.8 all-to-all-start.1
  445.2 18.9 %convolution_convert_fusion = bf16[2048,704]{0,1:T(8,128)(2,1)} fusion(bf16[4096,2048]{1,0:T(8,128)(2,1)} %all-gather.6.cloned.1.call-done.normed_ref, bf16[4096,704]{1,0:T(8,128)(2,1)} %get-tuple-element.215), kind=kOutput, calls=%fused_computation.10 | convolution fusion | flops 11812601856 | bytes 25427968 | tf_op jit(solution)/shard_map/dot_general | solution.py:990
  465.5 23.6 %all-gather.10.cloned.1.call-done = bf16[512,2048]{1,0:T(8,128)(2,1)} async-done(((bf16[128,2048]{1,0:T(8,128)(2,1)}), bf16[512,2048]{1,0:T(8,128)(2,1)}) %all-gather.10.cloned.1.call-update) | async-done | bytes 2097168 | tf_op jit(solution)/shard_map/all_gather | solution.py:1222
  489.3 3.6 copy.83
  492.9 3.9 all-to-all-start.2
  498.6 19.6 %fusion.55 = f32[704,2048]{1,0:T(8,128)} fusion(bf16[4096,704]{1,0:T(8,128)(2,1)} %get-tuple-element.228, bf16[4096,2048]{1,0:T(8,128)(2,1)} %all-gather.8.cloned.1.call-done.up_ref), kind=kOutput, calls=%fused_computation.158 | convolution fusion | flops 11811160064 | bytes 28311552 | tf_op jit(solution)/shard_map/dot_general | solution.py:990
  521.8 9.5 %all-to-all-done.2 = bf16[8,256,704]{1,2,0:T(8,128)(2,1)S(1)} async-done(((bf16[8,256,704]{1,2,0:T(8,128)(2,1)}), bf16[8,256,704]{1,2,0:T(8,128)(2,1)S(1)}, u32[]{:S(2)}, u32[]{:S(2)}) %all-to-all-start.2) | async-done | bytes 2883616 | tf_op jit(solution)/shard_map/all_to_all | solution.py:1176
  531.4 3.6 copy.82
  535.0 4.4 all-to-all-start.3
  539.4 6.4 %fusion.54 = f32[256,2048]{1,0:T(8,128)S(1)} fusion(bf16[256,2816]{1,0:T(8,128)(2,1)} %get-tuple-element.219, bf16[2816,2048]{1,0:T(8,128)(2,1)} %param.23), kind=kOutput, calls=%fused_computation.157 | convolution fusion | flops 2952790016 | bytes 15073280 | tf_op jit(solution)/shard_map/dot_general | solution.py:982
  566.9 7.1 %all-to-all-done.3 = bf16[8,256,704]{1,2,0:T(8,128)(2,1)} async-done(((bf16[8,256,704]{1,2,0:T(8,128)(2,1)}), bf16[8,256,704]{1,2,0:T(8,128)(2,1)}, u32[]{:S(2)}, u32[]{:S(2)}) %all-to-all-start.3) | async-done | bytes 2883616 | tf_op jit(solution)/shard_map/all_to_all | solution.py:1176
  573.9 4.6 copy.68.wide_ref
  578.6 9.5 %place_w_gu.1 = f32[256,11264]{1,0:T(8,128)} custom-call(bf16[8,256,704]{2,1,0:T(8,128)(2,1)} %copy.67.gate_ref, bf16[8,256,704]{2,1,0:T(8,128)(2,1)} %copy.68.wide_ref), custom_call_target="tpu_custom_call" | custom-call | tf_op jit(solution)/shard_map/place_w_gu/pallas_call | solution.py:914
  588.1 20.3 %all-gather.12.cloned.1.call-done = bf16[32,64,1536]{2,1,0:T(8,128)(2,1)} async-done(((bf16[8,64,1536]{2,1,0:T(8,128)(2,1)}), bf16[32,64,1536]{2,1,0:T(8,128)(2,1)}) %all-gather.12.cloned.1.call-update) | async-done | bytes 6291472 | tf_op jit(solution)/shard_map/all_gather | solution.py:1228
  608.4 12.2 %place_w_in.1 = f32[256,12288]{1,0:T(8,128)} custom-call(bf16[4,8,64,1536]{3,2,1,0:T(8,128)(2,1)} %bitcast.161), custom_call_target="tpu_custom_call" | custom-call | tf_op jit(solution)/shard_map/place_w_in/pallas_call | solution.py:874
  (242 shorter events, 82.9 us)
Async XLA Ops:
  7.2 35.8 %copy-start = (f32[2,16]{1,0:T(2,128)S(1)}, f32[2,16]{1,0:T(2,128)}, u32[]{:S(2)}) copy-start(f32[2,16]{1,0:T(2,128)} %param.19) | copy-start | bytes 388
  7.2 324.1 %all-gather.8.cloned.1.call-start = ((), (), s32[]{:S(2)}) async-start(), calls=%async_computation.6 | async-start | bytes 17301504 | tf_op jit(solution)/shard_map/all_gather | solution.py:1052
  13.3 28.4 %collective-permute-start.5 = (bf16[1024,3072]{1,0:T(8,128)(2,1)}, bf16[1024,3072]{1,0:T(8,128)(2,1)}, u32[]{:S(2)}, u32[]{:S(2)}) collective-permute-start(bf16[1024,3072]{1,0:T(8,128)(2,1)} %pick_heads.1.refs_4_), channel_id=1, source_target_pairs={{0,16},{16,0},{1,17},{17,1},{2,18},{18,2},{3,19},{19,3},{4,20},{20... | collective-permute-start | bytes 18874376 | tf_op jit(solution)/shard_map/ppermute | solution.py:961
  13.8 7.6 %collective-permute-start.1 = (bf16[128,2048]{1,0:T(8,128)(2,1)S(1)}, bf16[128,2048]{1,0:T(8,128)(2,1)S(1)}, u32[]{:S(2)}, u32[]{:S(2)}) collective-permute-start(bf16[128,2048]{1,0:T(8,128)(2,1)S(1)} %bitcast.168), channel_id=1, source_target_pairs={{0,16},{16,0},{1,17},{17,1},{2,18},{18,2},{3,19},{19,3},{4,20},{20... | collective-permute-start | bytes 1572872 | tf_op jit(solution)/shard_map/ppermute | solution.py:961
  13.9 16.5 %collective-permute-start.2 = (bf16[128,2048]{1,0:T(8,128)(2,1)S(1)}, bf16[128,2048]{1,0:T(8,128)(2,1)S(1)}, u32[]{:S(2)}, u32[]{:S(2)}) collective-permute-start(bf16[128,2048]{1,0:T(8,128)(2,1)S(1)} %bitcast.152), channel_id=1, source_target_pairs={{0,4},{4,0},{8,12},{12,8},{1,5},{5,1},{9,13},{13,9},{2,6},{6,2},{1... | collective-permute-start | bytes 1572872 | tf_op jit(solution)/shard_map/ppermute | solution.py:961
  16.9 24.9 %collective-permute-start.3 = (bf16[128,2048]{1,0:T(8,128)(2,1)S(1)}, bf16[128,2048]{1,0:T(8,128)(2,1)S(1)}, u32[]{:S(2)}, u32[]{:S(2)}) collective-permute-start(bf16[128,2048]{1,0:T(8,128)(2,1)S(1)} %bitcast.153), channel_id=1, source_target_pairs={{0,8},{4,12},{8,0},{12,4},{1,9},{5,13},{9,1},{13,5},{2,10},{6,14},... | collective-permute-start | bytes 1572872 | tf_op jit(solution)/shard_map/ppermute | solution.py:961
  18.4 23.4 %collective-permute-start.4 = (bf16[128,2048]{1,0:T(8,128)(2,1)S(1)}, bf16[128,2048]{1,0:T(8,128)(2,1)S(1)}, u32[]{:S(2)}, u32[]{:S(2)}) collective-permute-start(bf16[128,2048]{1,0:T(8,128)(2,1)S(1)} %bitcast.154), channel_id=1, source_target_pairs={{0,12},{4,8},{8,4},{12,0},{1,13},{5,9},{9,5},{13,1},{2,14},{6,10},... | collective-permute-start | bytes 1572872 | tf_op jit(solution)/shard_map/ppermute | solution.py:961
  41.8 289.5 %all-gather.6.cloned.1.call-start = ((), (), s32[]{:S(2)}) async-start(), calls=%async_computation.5 | async-start | bytes 17301504 | tf_op jit(solution)/shard_map/all_gather | solution.py:1080
  41.8 63.6 %collective-permute-start.11 = (bf16[1024,11264]{1,0:T(8,128)(2,1)}, bf16[1024,11264]{1,0:T(8,128)(2,1)}, u32[]{:S(2)}, u32[]{:S(2)}) collective-permute-start(bf16[1024,11264]{1,0:T(8,128)(2,1)} %refs_5_), channel_id=1, source_target_pairs={{0,16},{16,0},{1,17},{17,1},{2,18},{18,2},{3,19},{19,3},{4,20},{20... | collective-permute-start | bytes 69206024 | tf_op jit(solution)/shard_map/ppermute | solution.py:961
  41.9 63.5 %collective-permute-start.12 = (bf16[2048,2048]{1,0:T(8,128)(2,1)}, bf16[2048,2048]{1,0:T(8,128)(2,1)}, u32[]{:S(2)}, u32[]{:S(2)}) collective-permute-start(bf16[2048,2048]{1,0:T(8,128)(2,1)} %refs_2_), channel_id=1, source_target_pairs={{0,16},{16,0},{1,17},{17,1},{2,18},{18,2},{3,19},{19,3},{4,20},{20... | collective-permute-start | bytes 25165832 | tf_op jit(solution)/shard_map/ppermute | solution.py:961
  42.4 6.2 collective-permute-start
  42.5 22.0 %collective-permute-start.7 = (bf16[1024,32]{0,1:T(8,128)(2,1)S(1)}, bf16[1024,32]{0,1:T(8,128)(2,1)S(1)}, u32[]{:S(2)}, u32[]{:S(2)}) collective-permute-start(bf16[1024,32]{0,1:T(8,128)(2,1)S(1)} %copy-done.30), channel_id=1, source_target_pairs={{0,16},{16,0},{1,17},{17,1},{2,18},{18,2},{3,19},{19,3},{4,20},{20... | collective-permute-start | bytes 196616 | tf_op jit(solution)/shard_map/ppermute | solution.py:961
  42.9 6.3 %collective-permute-start.6 = (bf16[4,4096]{1,0:T(4,128)(2,1)S(1)}, bf16[4,4096]{1,0:T(4,128)(2,1)S(1)}, u32[]{:S(2)}, u32[]{:S(2)}) collective-permute-start(bf16[4,4096]{1,0:T(4,128)(2,1)S(1)} %copy-done.33), channel_id=1, source_target_pairs={{0,16},{16,0},{1,17},{17,1},{2,18},{18,2},{3,19},{19,3},{4,20},{20... | collective-permute-start | bytes 98312 | tf_op jit(solution)/shard_map/ppermute | solution.py:961
  89.9 10.3 %collective-permute-start.10 = (bf16[128,1024]{1,0:T(8,128)(2,1)}, bf16[128,1024]{1,0:T(8,128)(2,1)S(1)}, u32[]{:S(2)}, u32[]{:S(2)}) collective-permute-start(bf16[128,1024]{1,0:T(8,128)(2,1)} %bitcast.206), channel_id=1, source_target_pairs={{0,12},{4,8},{8,4},{12,0},{1,13},{5,9},{9,5},{13,1},{2,14},{6,10},... | collective-permute-start | bytes 786440 | tf_op jit(solution)/shard_map/ppermute | solution.py:961
  91.5 13.9 %collective-permute-start.8 = (bf16[128,1024]{1,0:T(8,128)(2,1)}, bf16[128,1024]{1,0:T(8,128)(2,1)S(1)}, u32[]{:S(2)}, u32[]{:S(2)}) collective-permute-start(bf16[128,1024]{1,0:T(8,128)(2,1)} %bitcast.205), channel_id=1, source_target_pairs={{0,4},{4,0},{8,12},{12,8},{1,5},{5,1},{9,13},{13,9},{2,6},{6,2},{1... | collective-permute-start | bytes 786440 | tf_op jit(solution)/shard_map/ppermute | solution.py:961
  93.0 12.4 %collective-permute-start.9 = (bf16[128,1024]{1,0:T(8,128)(2,1)}, bf16[128,1024]{1,0:T(8,128)(2,1)S(1)}, u32[]{:S(2)}, u32[]{:S(2)}) collective-permute-start(bf16[128,1024]{1,0:T(8,128)(2,1)} %bitcast.204), channel_id=1, source_target_pairs={{0,8},{4,12},{8,0},{12,4},{1,9},{5,13},{9,1},{13,5},{2,10},{6,14},... | collective-permute-start | bytes 786440 | tf_op jit(solution)/shard_map/ppermute | solution.py:961
  117.3 3.6 collective-permute-start.13
  117.4 26.2 %collective-permute-start.14 = (bf16[128,1024]{1,0:T(8,128)(2,1)}, bf16[128,1024]{1,0:T(8,128)(2,1)S(1)}, u32[]{:S(2)}, u32[]{:S(2)}) collective-permute-start(bf16[128,1024]{1,0:T(8,128)(2,1)} %get-tuple-element.149), channel_id=1, source_target_pairs={{0,4},{4,0},{8,12},{12,8},{1,5},{5,1},{9,13},{13,9},{2,6},{6,2},{1... | collective-permute-start | bytes 786440 | tf_op jit(solution)/shard_map/ppermute | solution.py:961
  118.5 25.1 %collective-permute-start.15 = (bf16[128,1024]{1,0:T(8,128)(2,1)}, bf16[128,1024]{1,0:T(8,128)(2,1)S(1)}, u32[]{:S(2)}, u32[]{:S(2)}) collective-permute-start(bf16[128,1024]{1,0:T(8,128)(2,1)} %get-tuple-element.150), channel_id=1, source_target_pairs={{0,8},{4,12},{8,0},{12,4},{1,9},{5,13},{9,1},{13,5},{2,10},{6,14},... | collective-permute-start | bytes 786440 | tf_op jit(solution)/shard_map/ppermute | solution.py:961
  119.5 25.4 %collective-permute-start.16 = (bf16[128,1024]{1,0:T(8,128)(2,1)}, bf16[128,1024]{1,0:T(8,128)(2,1)S(1)}, u32[]{:S(2)}, u32[]{:S(2)}) collective-permute-start(bf16[128,1024]{1,0:T(8,128)(2,1)} %get-tuple-element.151), channel_id=1, source_target_pairs={{0,12},{4,8},{8,4},{12,0},{1,13},{5,9},{9,5},{13,1},{2,14},{6,10},... | collective-permute-start | bytes 786440 | tf_op jit(solution)/shard_map/ppermute | solution.py:961
  145.6 3.8 collective-permute-start.17
  163.7 12.9 %collective-permute-start.18 = (bf16[128,1024]{1,0:T(8,128)(2,1)}, bf16[128,1024]{1,0:T(8,128)(2,1)S(1)}, u32[]{:S(2)}, u32[]{:S(2)}) collective-permute-start(bf16[128,1024]{1,0:T(8,128)(2,1)} %get-tuple-element.160), channel_id=1, source_target_pairs={{0,4},{4,0},{8,12},{12,8},{1,5},{5,1},{9,13},{13,9},{2,6},{6,2},{1... | collective-permute-start | bytes 786440 | tf_op jit(solution)/shard_map/ppermute | solution.py:961
  163.8 12.8 %collective-permute-start.19 = (bf16[128,1024]{1,0:T(8,128)(2,1)}, bf16[128,1024]{1,0:T(8,128)(2,1)S(1)}, u32[]{:S(2)}, u32[]{:S(2)}) collective-permute-start(bf16[128,1024]{1,0:T(8,128)(2,1)} %get-tuple-element.161), channel_id=1, source_target_pairs={{0,8},{4,12},{8,0},{12,4},{1,9},{5,13},{9,1},{13,5},{2,10},{6,14},... | collective-permute-start | bytes 786440 | tf_op jit(solution)/shard_map/ppermute | solution.py:961
  164.8 14.1 %collective-permute-start.20 = (bf16[128,1024]{1,0:T(8,128)(2,1)}, bf16[128,1024]{1,0:T(8,128)(2,1)S(1)}, u32[]{:S(2)}, u32[]{:S(2)}) collective-permute-start(bf16[128,1024]{1,0:T(8,128)(2,1)} %get-tuple-element.162), channel_id=1, source_target_pairs={{0,12},{4,8},{8,4},{12,0},{1,13},{5,9},{9,5},{13,1},{2,14},{6,10},... | collective-permute-start | bytes 786440 | tf_op jit(solution)/shard_map/ppermute | solution.py:961
  179.5 23.7 %collective-permute-start.21 = (bf16[128,2048]{1,0:T(8,128)(2,1)S(1)}, bf16[128,2048]{1,0:T(8,128)(2,1)S(1)}, u32[]{:S(2)}, u32[]{:S(2)}) collective-permute-start(bf16[128,2048]{1,0:T(8,128)(2,1)S(1)} %copy-done.18), channel_id=1, source_target_pairs={{0,4},{4,0},{8,12},{12,8},{1,5},{5,1},{9,13},{13,9},{2,6},{6,2},{1... | collective-permute-start | bytes 1572872 | tf_op jit(solution)/shard_map/ppermute | solution.py:961
  181.1 22.2 %collective-permute-start.22 = (bf16[128,2048]{1,0:T(8,128)(2,1)S(1)}, bf16[128,2048]{1,0:T(8,128)(2,1)}, u32[]{:S(2)}, u32[]{:S(2)}) collective-permute-start(bf16[128,2048]{1,0:T(8,128)(2,1)S(1)} %copy-done.18), channel_id=1, source_target_pairs={{0,8},{4,12},{8,0},{12,4},{1,9},{5,13},{9,1},{13,5},{2,10},{6,14},... | collective-permute-start | bytes 1572872 | tf_op jit(solution)/shard_map/ppermute | solution.py:961
  182.0 30.7 %collective-permute-start.23 = (bf16[128,2048]{1,0:T(8,128)(2,1)S(1)}, bf16[128,2048]{1,0:T(8,128)(2,1)}, u32[]{:S(2)}, u32[]{:S(2)}) collective-permute-start(bf16[128,2048]{1,0:T(8,128)(2,1)S(1)} %copy-done.18), channel_id=1, source_target_pairs={{0,12},{4,8},{8,4},{12,0},{1,13},{5,9},{9,5},{13,1},{2,14},{6,10},... | collective-permute-start | bytes 1572872 | tf_op jit(solution)/shard_map/ppermute | solution.py:961
  183.0 31.2 %collective-permute-start.24 = (bf16[512,2048]{1,0:T(8,128)(2,1)S(1)}, bf16[512,2048]{1,0:T(8,128)(2,1)}, u32[]{:S(2)}, u32[]{:S(2)}) collective-permute-start(bf16[512,2048]{1,0:T(8,128)(2,1)S(1)} %copy-done.3), channel_id=1, source_target_pairs={{0,16},{16,0},{1,17},{17,1},{2,18},{18,2},{3,19},{19,3},{4,20},{20... | collective-permute-start | bytes 6291464 | tf_op jit(solution)/shard_map/ppermute | solution.py:961
  214.2 3.5 collective-permute-start.25
  242.5 4.6 collective-permute-start.26
  251.1 80.2 %all-to-all-start = ((bf16[4,128,2048]{2,1,0:T(8,128)(2,1)}), bf16[4,128,2048]{2,1,0:T(8,128)(2,1)}, u32[]{:S(2)}, u32[]{:S(2)}) async-start(bf16[4,128,2048]{2,1,0:T(8,128)(2,1)} %bitcast.28), calls=%async_computation | async-start | bytes 4194304 | tf_op jit(solution)/shard_map/all_to_all | solution.py:1182
  255.7 185.6 %reduce-scatter.2.cloned.1.call-start = ((), (), s32[]{:S(2)}) async-start(), calls=%async_computation.7 | async-start | bytes 7864320 | tf_op jit(solution)/shard_map/reduce_scatter | solution.py:1189
  272.5 59.1 %copy-start.6 = (bf16[2,64,2048]{2,1,0:T(8,128)(2,1)S(1)}, bf16[2,64,2048]{2,1,0:T(8,128)(2,1)}, u32[]{:S(2)}) copy-start(bf16[2,64,2048]{2,1,0:T(8,128)(2,1)} %param.12) | copy-start | bytes 1572868
  331.4 157.8 %all-gather.10.cloned.1.call-start = ((), (), s32[]{:S(2)}) async-start(), calls=%async_computation.8 | async-start | bytes 2621440 | tf_op jit(solution)/shard_map/all_gather | solution.py:1222
  337.6 15.1 %collective-permute-start.27 = (bf16[128,2048]{1,0:T(8,128)(2,1)}, bf16[128,2048]{1,0:T(8,128)(2,1)}, u32[]{:S(2)}, u32[]{:S(2)}) collective-permute-start(bf16[128,2048]{1,0:T(8,128)(2,1)} %get-tuple-element.243), channel_id=1, source_target_pairs={{0,4},{4,0},{8,12},{12,8},{1,5},{5,1},{9,13},{13,9},{2,6},{6,2},{1... | collective-permute-start | bytes 1572872 | tf_op jit(solution)/shard_map/ppermute | solution.py:961
  339.0 24.9 %collective-permute-start.28 = (bf16[128,2048]{1,0:T(8,128)(2,1)}, bf16[128,2048]{1,0:T(8,128)(2,1)}, u32[]{:S(2)}, u32[]{:S(2)}) collective-permute-start(bf16[128,2048]{1,0:T(8,128)(2,1)} %get-tuple-element.245), channel_id=1, source_target_pairs={{0,8},{4,12},{8,0},{12,4},{1,9},{5,13},{9,1},{13,5},{2,10},{6,14},... | collective-permute-start | bytes 1572872 | tf_op jit(solution)/shard_map/ppermute | solution.py:961
  340.5 23.5 %collective-permute-start.29 = (bf16[128,2048]{1,0:T(8,128)(2,1)S(1)}, bf16[128,2048]{1,0:T(8,128)(2,1)}, u32[]{:S(2)}, u32[]{:S(2)}) collective-permute-start(bf16[128,2048]{1,0:T(8,128)(2,1)S(1)} %get-tuple-element.244), channel_id=1, source_target_pairs={{0,12},{4,8},{8,4},{12,0},{1,13},{5,9},{9,5},{13,1},{2,14},{6,10},... | collective-permute-start | bytes 1572872 | tf_op jit(solution)/shard_map/ppermute | solution.py:961
  367.0 2.8 collective-permute-start.30
  441.3 24.2 %all-to-all-start.1 = ((bf16[8,64,1536]{2,1,0:T(8,128)(2,1)}), bf16[8,64,1536]{2,1,0:T(8,128)(2,1)S(1)}, u32[]{:S(2)}, u32[]{:S(2)}) async-start(bf16[8,64,1536]{2,1,0:T(8,128)(2,1)} %bitcast.170), calls=%async_computation.2 | async-start | bytes 3145728 | tf_op jit(solution)/shard_map/all_to_all | solution.py:1176
  445.1 163.3 %all-gather.12.cloned.1.call-start = ((), (), s32[]{:S(2)}) async-start(), calls=%async_computation.9 | async-start | bytes 7864320 | tf_op jit(solution)/shard_map/all_gather | solution.py:1228
  489.2 7.6 %collective-permute-start.32 = (f32[15,2048]{1,0:T(8,128)S(1)}, f32[15,2048]{1,0:T(8,128)S(1)}, u32[]{:S(2)}, u32[]{:S(2)}) collective-permute-start(f32[15,2048]{1,0:T(8,128)S(1)} %add.249), channel_id=1, source_target_pairs={{0,1},{1,0},{2,3},{3,2},{4,5},{5,4},{6,7},{7,6},{8,9},{9,8},{10,11... | collective-permute-start | bytes 368648 | tf_op jit(solution)/shard_map/ppermute | solution.py:961
  492.9 38.5 %all-to-all-start.2 = ((bf16[8,256,704]{1,2,0:T(8,128)(2,1)}), bf16[8,256,704]{1,2,0:T(8,128)(2,1)S(1)}, u32[]{:S(2)}, u32[]{:S(2)}) async-start(bf16[8,256,704]{1,2,0:T(8,128)(2,1)} %bitcast.156), calls=%async_computation.3 | async-start | bytes 5767168 | tf_op jit(solution)/shard_map/all_to_all | solution.py:1176
  496.8 21.4 %collective-permute-start.33 = (f32[15,2048]{1,0:T(8,128)S(1)}, f32[15,2048]{1,0:T(8,128)S(1)}, u32[]{:S(2)}, u32[]{:S(2)}) collective-permute-start(f32[15,2048]{1,0:T(8,128)S(1)} %add.253), channel_id=1, source_target_pairs={{0,2},{1,3},{2,0},{3,1},{4,6},{5,7},{6,4},{7,5},{8,10},{9,11},{10,... | collective-permute-start | bytes 368648 | tf_op jit(solution)/shard_map/ppermute | solution.py:961
  518.2 32.9 %collective-permute-start.34 = (f32[15,2048]{1,0:T(8,128)S(1)}, f32[15,2048]{1,0:T(8,128)S(1)}, u32[]{:S(2)}, u32[]{:S(2)}) collective-permute-start(f32[15,2048]{1,0:T(8,128)S(1)} %add.254), channel_id=1, source_target_pairs={{0,4},{4,0},{8,12},{12,8},{1,5},{5,1},{9,13},{13,9},{2,6},{6,2},{1... | collective-permute-start | bytes 368648 | tf_op jit(solution)/shard_map/ppermute | solution.py:961
  520.3 30.8 %collective-permute-start.35 = (f32[15,2048]{1,0:T(8,128)S(1)}, f32[15,2048]{1,0:T(8,128)S(1)}, u32[]{:S(2)}, u32[]{:S(2)}) collective-permute-start(f32[15,2048]{1,0:T(8,128)S(1)} %add.254), channel_id=1, source_target_pairs={{0,8},{4,12},{8,0},{12,4},{1,9},{5,13},{9,1},{13,5},{2,10},{6,14},... | collective-permute-start | bytes 368648 | tf_op jit(solution)/shard_map/ppermute | solution.py:961
  521.8 29.4 %collective-permute-start.36 = (f32[15,2048]{1,0:T(8,128)S(1)}, f32[15,2048]{1,0:T(8,128)S(1)}, u32[]{:S(2)}, u32[]{:S(2)}) collective-permute-start(f32[15,2048]{1,0:T(8,128)S(1)} %add.254), channel_id=1, source_target_pairs={{0,12},{4,8},{8,4},{12,0},{1,13},{5,9},{9,5},{13,1},{2,14},{6,10},... | collective-permute-start | bytes 368648 | tf_op jit(solution)/shard_map/ppermute | solution.py:961
  535.0 39.0 %all-to-all-start.3 = ((bf16[8,256,704]{1,2,0:T(8,128)(2,1)}), bf16[8,256,704]{1,2,0:T(8,128)(2,1)}, u32[]{:S(2)}, u32[]{:S(2)}) async-start(bf16[8,256,704]{1,2,0:T(8,128)(2,1)} %bitcast.155), calls=%async_computation.4 | async-start | bytes 5767168 | tf_op jit(solution)/shard_map/all_to_all | solution.py:1176
  547.0 14.3 %collective-permute-start.31 = (f32[128,2048]{1,0:T(8,128)}, f32[128,2048]{1,0:T(8,128)}, u32[]{:S(2)}, u32[]{:S(2)}) collective-permute-start(f32[128,2048]{1,0:T(8,128)} %slice.152), channel_id=1, source_target_pairs={{0,16},{16,0},{1,17},{17,1},{2,18},{18,2},{3,19},{19,3},{4,20},{20... | collective-permute-start | bytes 3145736 | tf_op jit(solution)/shard_map/ppermute | solution.py:961
  (37 other events, 381.0 us)
Sparse Core Ops, SparseCore 0:
  41.9 126.4 all-gather.7
  172.0 153.0 all-gather.5
  331.5 109.7 reduce-scatter.1
  442.7 46.4 all-gather.9
  490.6 117.7 all-gather.11
